TPU v7x, 256 devices: a whole 4x4x8 slice. The times are simulated.
256 devices in a mesh: depth: 16 (over y_lo, x, core), cols: 16 (over z, y_hi).
Axes of the slice: x: 4, y: 4 (y_hi: 2, y_lo: 2; y = y_hi * 2 + y_lo), z: 8, core: 2. Of those that a mesh axis runs over, the one named last changes fastest.
Arguments:
- alignment_activations: bfloat16 [256, 512, 768], P('depth', 'cols'), may hold values from -6 to 6
- occupancy_indicator: int32 [256, 512], P('depth', 'cols'), may hold values from 0 to 1, as said below
- horizontal_probe_proj: bfloat16 [768, 768], replicated
- horizontal_lookup_proj: bfloat16 [768, 768], replicated
- horizontal_content_proj: bfloat16 [768, 768], replicated, may hold values from -0.21875 to 0.21875
- horizontal_result_proj: bfloat16 [768, 768], replicated, may hold values from -0.21875 to 0.21875
- vertical_probe_proj: bfloat16 [768, 768], replicated
- vertical_lookup_proj: bfloat16 [768, 768], replicated
- vertical_content_proj: bfloat16 [768, 768], replicated, may hold values from -0.21875 to 0.21875
- vertical_result_proj: bfloat16 [768, 768], replicated, may hold values from -0.21875 to 0.21875
- pairing_first_factor: bfloat16 [768, 32], replicated, may hold values from -0.21875 to 0.21875
- pairing_second_factor: bfloat16 [768, 32], replicated, may hold values from -0.21875 to 0.21875
- pairing_channel_proj: bfloat16 [1024, 128], replicated, may hold values from -4 to 4
Outputs:
- alignment_output: bfloat16 [256, 512, 768], P('depth', 'cols')
- pair: bfloat16 [512, 512, 128], P('cols', 'depth')
Inputs may be any that keep to these rules, and one draw needn't show every extreme that they name: `occupancy_indicator`: sequence 0 has no padding; every other sequence has residues on the columns from 0 up to some last column, more than 384 columns in all, and padding after it.
All inputs are finite; a program needn't handle non-finite values.
Results may differ from a plain program's by a relative error of at most 0.028.
Values may be sent and summed in bfloat16 or wider, within the bound.
No kernel may reach another device: no remote copies, remote signals or barrier semaphores. Data moves between devices by JAX's collectives and lax.ppermute only.
A program may use at most 128 MiB of HBM per device.

v0:
```python
import math

import jax
import jax.numpy as jnp
from jax import lax
from jax.sharding import PartitionSpec as P

H = 12
HD = 64


def standardize_features(values):
    wide = values.astype(jnp.float32)
    center = wide - jnp.mean(wide, axis=-1, keepdims=True)
    spread = jnp.mean(center * center, axis=-1, keepdims=True)
    return (center * lax.rsqrt(spread + 1e-05)).astype(jnp.bfloat16)


def project_through(values, weight):
    return jnp.dot(values, weight, preferred_element_type=jnp.float32)


def on_device(
    alignment_activations,
    occupancy_indicator,
    horizontal_probe_proj,
    horizontal_lookup_proj,
    horizontal_content_proj,
    horizontal_result_proj,
    vertical_probe_proj,
    vertical_lookup_proj,
    vertical_content_proj,
    vertical_result_proj,
    pairing_first_factor,
    pairing_second_factor,
    pairing_channel_proj,
):
    homolog_tally, site_tally, portion_extent = alignment_activations.shape
    total_seqs = homolog_tally * lax.axis_size("depth")
    scale = 1.0 / math.sqrt(HD * total_seqs)
    live = occupancy_indicator.astype(jnp.bfloat16)
    standardized_features = standardize_features(alignment_activations)
    query = (
        project_through(standardized_features, horizontal_probe_proj) * live[:, :, None]
    ).astype(jnp.bfloat16)
    keys = (
        project_through(standardized_features, horizontal_lookup_proj) * live[:, :, None]
    ).astype(jnp.bfloat16)
    values = project_through(standardized_features, horizontal_content_proj).astype(jnp.bfloat16)
    query_heads = query.reshape(homolog_tally, site_tally, H, HD)
    piece = lax.all_gather(keys, "cols", axis=1, tiled=True)
    piece_heads = piece.reshape(homolog_tally, piece.shape[1], H, HD)
    partial_logits = (
        jnp.einsum("sihe,sjhe->ihj", query_heads, piece_heads, preferred_element_type=jnp.float32)
        * scale
    )
    logits = lax.psum(partial_logits, "depth")
    weights_all = jax.nn.softmax(logits, axis=-1).astype(jnp.bfloat16)
    piece = lax.all_gather(values, "cols", axis=1, tiled=True)
    count = piece.shape[1]
    piece_heads = piece.reshape(homolog_tally, count, H, HD)
    summed = jnp.einsum(
        "ihj,sjhe->sihe", weights_all, piece_heads, preferred_element_type=jnp.float32
    )
    mixed_homologs = summed.astype(jnp.bfloat16).reshape(homolog_tally, site_tally, portion_extent)
    state_after_row_attention = (
        alignment_activations.astype(jnp.float32)
        + project_through(mixed_homologs, horizontal_result_proj)
    ).astype(jnp.bfloat16)
    standardized_features = standardize_features(state_after_row_attention)
    col_input, col_live = (
        lax.all_to_all(standardized_features, "depth", split_axis=1, concat_axis=0, tiled=True),
        lax.all_to_all(live, "depth", split_axis=1, concat_axis=0, tiled=True),
    )
    every, narrow = col_live.shape
    col_q = (
        project_through(col_input, vertical_probe_proj)
        .astype(jnp.bfloat16)
        .reshape(every, narrow, H, HD)
    )
    col_k = (
        project_through(col_input, vertical_lookup_proj)
        .astype(jnp.bfloat16)
        .reshape(every, narrow, H, HD)
    )
    col_v = (
        project_through(col_input, vertical_content_proj)
        .astype(jnp.bfloat16)
        .reshape(every, narrow, H, HD)
    )
    col_logits = jnp.einsum("schd,tchd->chst", col_q, col_k, preferred_element_type=jnp.float32) * (
        1.0 / math.sqrt(HD)
    )
    allowed = (col_live > 0).T[:, None, None, :]
    col_logits = jnp.where(allowed, col_logits, -1000000000.0)
    col_weights = jax.nn.softmax(col_logits, axis=-1).astype(jnp.bfloat16)
    col_mixed = jnp.einsum(
        "chst,tchd->schd", col_weights, col_v, preferred_element_type=jnp.float32
    )
    col_mixed = col_mixed.astype(jnp.bfloat16).reshape(every, narrow, portion_extent)
    returned_value = lax.all_to_all(col_mixed, "depth", split_axis=0, concat_axis=1, tiled=True)
    alignment_output = (
        state_after_row_attention.astype(jnp.float32)
        + project_through(returned_value, vertical_result_proj)
    ).astype(jnp.bfloat16)
    standardized_features = standardize_features(alignment_output)
    left = (project_through(standardized_features, pairing_first_factor) * live[:, :, None]).astype(
        jnp.bfloat16
    )
    right = (
        project_through(standardized_features, pairing_second_factor) * live[:, :, None]
    ).astype(jnp.bfloat16)
    left_all, live_left = (
        lax.all_gather(left, "depth", axis=0, tiled=True),
        lax.all_gather(live, "depth", axis=0, tiled=True),
    )
    right_row, live_row = (
        lax.all_gather(right, "cols", axis=1, tiled=True),
        lax.all_gather(live, "cols", axis=1, tiled=True),
    )
    right_all, live_right = (
        lax.all_to_all(right_row, "depth", split_axis=1, concat_axis=0, tiled=True),
        lax.all_to_all(live_row, "depth", split_axis=1, concat_axis=0, tiled=True),
    )
    outer = jnp.einsum(
        "sic,sje->ijce", left_all, right_all, preferred_element_type=jnp.float32
    ).astype(jnp.bfloat16)
    rows_left, rows_right = (outer.shape[0], outer.shape[1])
    projected = jnp.dot(
        outer.reshape(rows_left, rows_right, -1),
        pairing_channel_proj,
        preferred_element_type=jnp.float32,
    )
    counted = jnp.dot(live_left.T, live_right, preferred_element_type=jnp.float32)
    pair = (projected / (counted[:, :, None] + 0.001)).astype(jnp.bfloat16)
    return (alignment_output, pair)


def solution(mesh):
    placed = (
        P("depth", "cols", None),
        P("depth", "cols"),
        P(),
        P(),
        P(),
        P(),
        P(),
        P(),
        P(),
        P(),
        P(),
        P(),
        P(),
    )
    return jax.shard_map(
        on_device,
        mesh=mesh,
        in_specs=placed,
        out_specs=(P("depth", "cols", None), P("cols", "depth", None)),
        check_vma=False,
    )
```

profile of v0, /device:TPU:4, one launch (start us, length us, event | category | flops | bytes accessed | tf_op | source)
XLA Modules:
  0.0 768.8 jit_solution(13659794021504043209)
XLA Ops:
  10.2 3.1 multiply_convert_fusion.1
  15.3 3.0 multiply_convert_fusion
  21.0 174.1 %all-gather.6.cloned.1.call-done = bf16[16,512,768]{2,1,0:T(8,128)(2,1)} async-done(((bf16[16,32,768]{2,1,0:T(8,128)(2,1)}), bf16[16,512,768]{2,1,0:T(8,128)(2,1)}) %all-gather.6.cloned.1.call-update) | async-done | bytes 12582928 | tf_op jit(solution)/shard_map/all_gather | solution.py:51
  195.1 16.7 %copy.99 = bf16[16,512,768]{1,2,0:T(8,128)(2,1)} copy(bf16[16,512,768]{2,1,0:T(8,128)(2,1)} %all-gather.6.cloned.1.call-done) | data formatting | bytes 25165824 | tf_op jit(solution)/shard_map/all_gather | solution.py:51
  211.8 7.6 fusion.43
  220.1 4.8 all-to-all-start.1
  224.9 148.9 %all-gather.4.cloned.1.call-done = bf16[16,512,768]{2,1,0:T(8,128)(2,1)} async-done(((bf16[16,32,768]{2,1,0:T(8,128)(2,1)}), bf16[16,512,768]{2,1,0:T(8,128)(2,1)}) %all-gather.4.cloned.1.call-update) | async-done | bytes 12582928 | tf_op jit(solution)/shard_map/all_gather | solution.py:59
  373.7 16.6 %copy.98 = bf16[16,512,768]{1,2,0:T(8,128)(2,1)} copy(bf16[16,512,768]{2,1,0:T(8,128)(2,1)} %all-gather.4.cloned.1.call-done) | data formatting | bytes 25165824 | tf_op jit(solution)/shard_map/all_gather | solution.py:59
  390.4 101.3 %all-reduce.2.cloned.1.call-done = f32[32,12,512]{2,0,1:T(8,128)} async-done(((f32[32,12,512]{2,0,1:T(8,128)}), f32[32,12,512]{2,0,1:T(8,128)}) %all-reduce.2.cloned.1.call-update) | async-done | bytes 786448 | tf_op jit(solution)/shard_map/psum | solution.py:57
  493.4 12.0 %fusion.31 = bf16[16,32,12,64]{3,1,0,2:T(8,128)(2,1)} fusion(bf16[16,512,12,64]{1,3,2,0:T(8,128)(2,1)} %bitcast.120, f32[32,12]{0,1:T(8,128)S(1)} %fusion.72, f32[32,12,512]{2,0,1:T(8,128)} %all-reduce.2.cloned.1.call-done), kind=kOutput, calls=%fused_computation.43 | convolution fusion | flops 403637120 | bytes 14157312 | tf_op jit(solution)/shard_map/ihj,sjhe->sihe/dot_general | solution.py:62
  514.1 10.7 %all-to-all-start = ((bf16[16,32,768]{2,0,1:T(8,128)(2,1)}), bf16[16,32,768]{2,0,1:T(8,128)(2,1)S(1)}, u32[]{:S(2)}, u32[]{:S(2)}) async-start(bf16[16,32,768]{2,0,1:T(8,128)(2,1)} %copy.103), calls=%async_computation | async-start | bytes 1572864 | tf_op jit(solution)/shard_map/all_to_all | solution.py:72
  524.7 44.1 %all-gather = bf16[16,32,16]{1,2,0:T(8,128)(2,1)S(1)} all-gather(bf16[1,32,16]{1,2,0:T(8,128)(2,1)S(1)} %bitcast.136), channel_id=1, replica_groups=mesh['depth'=16,'cols'=16] {'cols'}, dimensions={0}, use_global_device_ids=true | all-gather | bytes 17408 | tf_op jit(solution)/shard_map/all_gather | solution.py:119
  570.0 5.8 all-to-all-start.4
  578.1 2.9 convolution_convert_fusion
  586.8 5.0 fusion.73
  591.8 3.5 fusion.35
  597.1 5.7 all-to-all-start.2
  602.8 20.9 %all_gather.22 = bf16[256,32]{1,0:T(8,128)(2,1)S(1)} all-gather(bf16[16,32]{1,0:T(8,128)(2,1)S(1)} %get-tuple-element.3), channel_id=1, replica_groups=mesh['depth'=16,'cols'=16] {'depth'}, dimensions={0}, use_global_device_ids=true | all-gather | bytes 17408 | tf_op jit(solution)/shard_map/all_gather | solution.py:115
  628.1 61.6 %all_gather.20 = bf16[16,512,32]{2,1,0:T(8,128)(2,1)S(1)} all-gather(bf16[16,32,32]{2,1,0:T(8,128)(2,1)S(1)} %fusion.55), channel_id=1, replica_groups=mesh['depth'=16,'cols'=16] {'cols'}, dimensions={1}, use_global_device_ids=true | all-gather | bytes 557056 | tf_op jit(solution)/shard_map/all_gather | solution.py:118
  693.7 7.2 all-to-all-start.3
  702.5 25.2 %all_gather.21 = bf16[256,32,32]{2,1,0:T(8,128)(2,1)} all-gather(bf16[16,32,32]{2,1,0:T(8,128)(2,1)S(1)} %fusion.56), channel_id=1, replica_groups=mesh['depth'=16,'cols'=16] {'depth'}, dimensions={0}, use_global_device_ids=true | all-gather | bytes 557056 | tf_op jit(solution)/shard_map/all_gather | solution.py:114
  730.3 7.1 convert_bitcast_fusion
  737.4 12.0 %copy.118 = bf16[32,32,32,32]{3,2,1,0:T(8,128)(2,1)} copy(bf16[32,32,32,32]{2,3,0,1:T(8,128)(2,1)} %convert_bitcast_fusion) | data formatting | bytes 4194304 | tf_op jit(solution)/shard_map/convert_element_type | solution.py:127
  749.4 11.4 %reshape.92 = bf16[32,32,1024]{2,1,0:T(8,128)(2,1)S(1)} reshape(bf16[32,32,32,32]{3,2,1,0:T(8,128)(2,1)} %copy.118) | data formatting | bytes 4194304 | tf_op jit(solution)/shard_map/reshape | solution.py:130
  (79 shorter events, 43.6 us)
Async XLA Ops:
  7.2 502.7 %copy-start = (bf16[768,768]{1,0:T(8,128)(2,1)S(1)}, bf16[768,768]{1,0:T(8,128)(2,1)}, u32[]{:S(2)}) copy-start(bf16[768,768]{1,0:T(8,128)(2,1)} %param.18) | copy-start | bytes 3538948
  7.2 3.0 copy-start.3
  7.2 3.0 copy-start.5
  7.2 187.9 %all-gather.6.cloned.1.call-start = ((), (), s32[]{:S(2)}) async-start(), calls=%async_computation.6 | async-start | bytes 13369344 | tf_op jit(solution)/shard_map/all_gather | solution.py:51
  10.2 3.2 copy-start.6
  13.4 360.3 %all-gather.4.cloned.1.call-start = ((), (), s32[]{:S(2)}) async-start(), calls=%async_computation.5 | async-start | bytes 13369344 | tf_op jit(solution)/shard_map/all_gather | solution.py:59
  15.3 476.5 %all-reduce.2.cloned.1.call-start = ((), (), s32[]{:S(2)}) async-start(), calls=%async_computation.7 | async-start | bytes 1572864 | tf_op jit(solution)/shard_map/psum | solution.py:57
  220.1 294.0 %all-to-all-start.1 = ((bf16[16,16,2]{0,2,1:T(2,128)(2,1)}), bf16[16,16,2]{0,2,1:T(2,128)(2,1)S(1)}, u32[]{:S(2)}, u32[]{:S(2)}) async-start(bf16[16,16,2]{0,2,1:T(2,128)(2,1)} %bitcast.16), calls=%async_computation.1 | async-start | bytes 16384 | tf_op jit(solution)/shard_map/all_to_all | solution.py:73
  514.1 55.9 %all-to-all-start = ((bf16[16,32,768]{2,0,1:T(8,128)(2,1)}), bf16[16,32,768]{2,0,1:T(8,128)(2,1)S(1)}, u32[]{:S(2)}, u32[]{:S(2)}) async-start(bf16[16,32,768]{2,0,1:T(8,128)(2,1)} %copy.103), calls=%async_computation | async-start | bytes 1572864 | tf_op jit(solution)/shard_map/all_to_all | solution.py:72
  570.0 27.1 %all-to-all-start.4 = ((bf16[16,2,256]{2,1,0:T(2,128)(2,1)}), bf16[16,2,256]{2,1,0:T(2,128)(2,1)S(1)}, u32[]{:S(2)}, u32[]{:S(2)}) async-start(bf16[16,2,256]{2,1,0:T(2,128)(2,1)} %reshape.112), calls=%async_computation.4 | async-start | bytes 32768 | tf_op jit(solution)/shard_map/all_to_all | solution.py:123
  597.1 26.9 %all-to-all-start.2 = ((bf16[256,2,768]{2,1,0:T(2,128)(2,1)}), bf16[256,2,768]{2,1,0:T(2,128)(2,1)S(1)}, u32[]{:S(2)}, u32[]{:S(2)}) async-start(bf16[256,2,768]{2,1,0:T(2,128)(2,1)} %copy.111), calls=%async_computation.2 | async-start | bytes 1572864 | tf_op jit(solution)/shard_map/all_to_all | solution.py:101
  625.1 2.5 copy-start.8
  627.3 62.4 %copy-start.4 = (bf16[16,32,768]{2,1,0:T(8,128)(2,1)}, bf16[16,32,768]{2,1,0:T(8,128)(2,1)S(1)}, u32[]{:S(2)}) copy-start(bf16[16,32,768]{2,1,0:T(8,128)(2,1)S(1)} %get-tuple-element.9) | copy-start | bytes 2359300
  691.1 9.8 %copy-start.9 = (bf16[768,32]{0,1:T(8,128)(2,1)S(1)}, bf16[768,32]{0,1:T(8,128)(2,1)}, u32[]{:S(2)}) copy-start(bf16[768,32]{0,1:T(8,128)(2,1)} %param.23) | copy-start | bytes 147460
  693.7 34.0 %all-to-all-start.3 = ((bf16[16,2,8192]{2,1,0:T(2,128)(2,1)}), bf16[16,2,8192]{2,1,0:T(2,128)(2,1)S(1)}, u32[]{:S(2)}, u32[]{:S(2)}) async-start(bf16[16,2,8192]{2,1,0:T(2,128)(2,1)} %reshape.110), calls=%async_computation.3 | async-start | bytes 1048576 | tf_op jit(solution)/shard_map/all_to_all | solution.py:122
  728.7 1.6 copy-start.2
  749.4 11.4 %copy-start.7 = (bf16[1024,128]{1,0:T(8,128)(2,1)S(1)}, bf16[1024,128]{1,0:T(8,128)(2,1)}, u32[]{:S(2)}) copy-start(bf16[1024,128]{1,0:T(8,128)(2,1)} %param.25) | copy-start | bytes 786436
  749.4 12.9 %copy-start.1 = (bf16[768,768]{1,0:T(8,128)(2,1)S(1)}, bf16[768,768]{1,0:T(8,128)(2,1)}, u32[]{:S(2)}) copy-start(bf16[768,768]{1,0:T(8,128)(2,1)} %param.18) | copy-start | bytes 3538948
Sparse Core Ops, SparseCore 0:
  13.5 181.5 all-gather.5
  198.3 175.3 all-gather.3
  376.4 115.3 all-reduce.1
where the time goes:
time: 777 us; the launch traced here: 769 us
  waiting for transfers between devices  424 us (55%)
  blocking collectives  152 us (20%)
  local copies, waits for them, and re-layouts  79.9 us (10%)
  matrix products  58.8 us (8%)
  starting transfers between devices  34.3 us (4%)
  between operations  14.1 us (2%)
    all_gather x1, waiting for transfers between devices, on_device(): piece = lax.all_gather(keys, 'cols', axis=1, tiled=True)  174 us
    all_gather x1, waiting for transfers between devices, on_device(): piece = lax.all_gather(values, 'cols', axis=1, tiled=True)  149 us
    psum x1, waiting for transfers between devices, on_device(): logits = lax.psum(partial_logits, 'depth')  101 us
    all_gather x1, blocking collectives, on_device(): lax.all_gather(right, 'cols', axis=1, tiled=True)  61.6 us
    all_gather x1, blocking collectives, on_device(): lax.all_gather(live, 'cols', axis=1, tiled=True)  44.1 us
    all_gather x1, blocking collectives, on_device(): lax.all_gather(left, 'depth', axis=0, tiled=True)  25.2 us
    dot_general x10, matrix products, project_through(): return jnp.dot(values, weight, preferred_element_type=jnp.float32)  22.2 us
    all_gather x1, blocking collectives, on_device(): lax.all_gather(live, 'depth', axis=0, tiled=True)  20.9 us
  transfers between devices with their start and end apart: 8, of which 3 were waited for; matrix products, arithmetic and copies ran while one was open for 12% of the time, Pallas kernels for 0%

commit v1 on v0

v1 whole, which is shorter than its diff:
```python
import functools
import math

import jax
import jax.numpy as jnp
from jax import lax
from jax.experimental import pallas as pl
from jax.experimental.pallas import tpu as pltpu
from jax.sharding import PartitionSpec as P

f32 = jnp.float32
bf16 = jnp.bfloat16

S = 16
I = 32
E = 768
H = 12
N = 16
ROWS = S * I
SEQS = 256
SITES = 512
C = 32
PC = 128
LR = 80
VMEM = 60 * 1024 * 1024

NT = (((1,), (1,)), ((), ()))


def norm(wide):
    center = wide - jnp.mean(wide, axis=-1, keepdims=True)
    spread = jnp.mean(center * center, axis=-1, keepdims=True)
    return (center * lax.rsqrt(spread + 1e-05)).astype(bf16)


def mm(a, b):
    return jnp.dot(a, b, preferred_element_type=f32)


def mmt(a, b):
    return lax.dot_general(a, b, NT, preferred_element_type=f32)


def lanes_lo(a, b):
    return jnp.concatenate([a[:, :64], b[:, :64]], axis=1)


def lanes_hi(a, b):
    return jnp.concatenate([a[:, 64:], b[:, 64:]], axis=1)


def whole(n):
    return [pl.BlockSpec(memory_space=pltpu.VMEM)] * n


def params(**kw):
    return pltpu.CompilerParams(vmem_limit_bytes=VMEM, **kw)


def cost(flops, bytes_accessed, transcendentals=0):
    return pl.CostEstimate(
        flops=flops, bytes_accessed=bytes_accessed, transcendentals=transcendentals
    )


def row_proj_kernel(x_ref, live_ref, wq_ref, wk_ref, wv_ref, qk_ref, v_ref, xn_ref):
    @pl.when(pl.program_id(0) == 0)
    def _():
        xn_ref[...] = norm(x_ref[...].astype(f32))

    xn = xn_ref[...]
    live = live_ref[...]
    half = ROWS // 2

    def put(ref, w_ref, index, masked):
        y = mm(xn, w_ref[...])
        if masked:
            y = y * live
        y = y.astype(bf16)
        for t in range(2):
            a = y[:half, 128 * t : 128 * t + 128]
            b = y[half:, 128 * t : 128 * t + 128]
            for odd, pick in ((0, lanes_lo), (1, lanes_hi)):
                if index is None:
                    ref[2 * t + odd] = pick(a, b)
                else:
                    ref[2 * t + odd, index] = pick(a, b)

    put(qk_ref, wq_ref, 0, True)
    put(qk_ref, wk_ref, 1, True)
    put(v_ref, wv_ref, None, False)


def row_proj(x, live, wq, wk, wv):
    w = pl.BlockSpec((E, 256), lambda n: (0, n))
    return pl.pallas_call(
        row_proj_kernel,
        grid=(3,),
        in_specs=[
            pl.BlockSpec((ROWS, E), lambda n: (0, 0)),
            pl.BlockSpec((ROWS, 1), lambda n: (0, 0)),
            w,
            w,
            w,
        ],
        out_specs=[
            pl.BlockSpec((4, 2, 256, 128), lambda n: (n, 0, 0, 0)),
            pl.BlockSpec((4, 256, 128), lambda n: (n, 0, 0)),
        ],
        out_shape=[
            jax.ShapeDtypeStruct((N, 2, 256, 128), bf16),
            jax.ShapeDtypeStruct((N, 256, 128), bf16),
        ],
        scratch_shapes=[pltpu.VMEM((ROWS, E), bf16)],
        compiler_params=params(),
        cost_estimate=cost(3 * 2 * ROWS * E * E, 8_000_000),
    )(x, live, wq, wk, wv)


def turn_kernel(x_ref, live_ref, wp_ref, xr_ref, wk_ref):
    r = lax.broadcasted_iota(jnp.int32, (ROWS, ROWS), 0)
    o = lax.broadcasted_iota(jnp.int32, (ROWS, ROWS), 1)
    src = ((r & 15) << 5) + ((r >> 5) << 1) + ((r >> 4) & 1)
    perm = jnp.where(src == o, 1.0, 0.0).astype(bf16)
    xr_ref[:, :E] = mm(perm, x_ref[...]).astype(bf16)
    mask = jnp.broadcast_to(live_ref[...], (ROWS, 128)).astype(bf16)
    xr_ref[:, E:] = mm(perm, mask).astype(bf16)
    wk_ref[...] = jnp.zeros_like(wk_ref)
    for c in range(C):
        w = wp_ref[C * c : C * c + C, :]
        for j in range(4):
            wk_ref[128 * c + 32 * j : 128 * c + 32 * j + 32, 128 * j : 128 * j + 128] = w


def turn(x, live, wp):
    return pl.pallas_call(
        turn_kernel,
        in_specs=whole(3),
        out_specs=whole(2),
        out_shape=[
            jax.ShapeDtypeStruct((ROWS, E + 128), bf16),
            jax.ShapeDtypeStruct((4096, 512), bf16),
        ],
        compiler_params=params(),
        cost_estimate=cost(2 * ROWS * ROWS * E, 8_000_000),
    )(x, live, wp)


def logits_kernel(qk_ref, out_ref):
    def side(k):
        return jnp.concatenate(
            [
                qk_ref[:, k, I * s : I * s + I, :].reshape(SITES, 128)
                for s in range(S // 2)
            ],
            axis=1,
        )

    out_ref[...] = mmt(side(0), side(1)) * (1.0 / math.sqrt(64 * SEQS))


def partial_logits(qk):
    return pl.pallas_call(
        logits_kernel,
        in_specs=whole(1),
        out_specs=pl.BlockSpec(memory_space=pltpu.VMEM),
        out_shape=jax.ShapeDtypeStruct((SITES, SITES), f32),
        compiler_params=params(),
        cost_estimate=cost(2 * SITES * SITES * 1024, 3_000_000),
    )(qk)


def softmax_kernel(in_ref, out_ref):
    total = in_ref[0]
    for k in range(1, N):
        total = total + in_ref[k]
    top = jnp.max(total, axis=-1, keepdims=True)
    e = jnp.exp(total - top)
    p = (e / jnp.sum(e, axis=-1, keepdims=True)).astype(bf16)
    for k in range(N):
        out_ref[k] = p


def row_softmax(parts):
    return pl.pallas_call(
        softmax_kernel,
        in_specs=whole(1),
        out_specs=pl.BlockSpec(memory_space=pltpu.VMEM),
        out_shape=jax.ShapeDtypeStruct((N, I, SITES), bf16),
        compiler_params=params(),
        cost_estimate=cost(N * I * SITES, 1_500_000, I * SITES),
    )(parts)


def row_mix_kernel(p_ref, v_ref, out_ref):
    v = jnp.concatenate(
        [v_ref[:, I * s : I * s + I, :].reshape(SITES, 128) for s in range(S // 2)],
        axis=1,
    )
    mix = mm(p_ref[...], v).astype(bf16)
    r = lax.broadcasted_iota(jnp.int32, (256, 256), 0)
    o = lax.broadcasted_iota(jnp.int32, (256, 256), 1)
    perm = jnp.where(((r & 7) << 5) + (r >> 3) == o, 1.0, 0.0).astype(bf16)

    def block(b):
        part = mix[I * b : I * b + I, :]
        return jnp.concatenate(
            [part[:, 128 * s : 128 * s + 128] for s in range(8)], axis=0
        )

    for b in range(0, N, 2):
        pair = jnp.concatenate([block(b), block(b + 1)], axis=1)
        turned = mm(perm, pair).astype(bf16)
        out_ref[256 * b : 256 * b + 256, :] = turned[:, :128]
        out_ref[256 * b + 256 : 256 * b + 512, :] = turned[:, 128:]


def row_mix(p, v):
    return pl.pallas_call(
        row_mix_kernel,
        in_specs=whole(2),
        out_specs=pl.BlockSpec(memory_space=pltpu.VMEM),
        out_shape=jax.ShapeDtypeStruct((4096, 128), bf16),
        compiler_params=params(),
        cost_estimate=cost(2 * SITES * SITES * 1024, 3_000_000),
    )(p, v)


def column_kernel(
    mr_ref, xc_ref, wo_ref, cq_ref, ck_ref, cv_ref, co_ref, f_ref,
    ao_ref, l_ref, r_ref,
    ysc, xsc, qs, ks, vs, ms,
):
    halves = []
    for pick in (lanes_lo, lanes_hi):
        halves.append(
            jnp.concatenate(
                [
                    pick(mr_ref[512 * t : 512 * t + 256, :], mr_ref[512 * t + 256 : 512 * t + 512, :])
                    for t in range(H // 2)
                ],
                axis=1,
            )
        )
    mixed = jnp.concatenate(halves, axis=0)
    ysc[...] = mm(mixed, wo_ref[...]).reshape(2, N, 2, 8, E)
    xsc[...] = xc_ref[...].astype(f32).reshape(N, 2, 2, 8, E + 128)
    blocks = []
    masks = []
    for i in range(2):
        for s2 in range(2):
            blocks.append((ysc[s2, :, i] + xsc[:, i, s2, :, :E]).reshape(128, E))
            masks.append(xsc[:, i, s2, :, E:].reshape(128, 128))
    after_rows = jnp.concatenate(blocks, axis=0).astype(bf16)
    wide = after_rows.astype(f32)
    mask = jnp.concatenate(masks, axis=0).astype(bf16)
    lane0 = jnp.where(
        lax.broadcasted_iota(jnp.int32, (8, 128), 1) == 0, 1.0, 0.0
    ).astype(bf16)
    alive = mmt(lane0, mask)

    normed = norm(wide)
    qs[...] = mm(normed, cq_ref[...]).astype(bf16)
    ks[...] = mm(normed, ck_ref[...]).astype(bf16)
    vs[...] = mm(normed, cv_ref[...]).astype(bf16)
    low = lax.broadcasted_iota(jnp.int32, (SEQS, 128), 1) < 64
    for i in range(2):
        rows = slice(SEQS * i, SEQS * i + SEQS)
        keep = alive[0:1, rows] > 0
        for t in range(H // 2):
            lanes = slice(128 * t, 128 * t + 128)
            q, k, v = qs[rows, lanes], ks[rows, lanes], vs[rows, lanes]
            mixes = []
            for own in (low, jnp.logical_not(low)):
                logits = mmt(jnp.where(own, q, jnp.zeros_like(q)), k) * 0.125
                logits = jnp.where(keep, logits, -1000000000.0)
                e = jnp.exp(logits - jnp.max(logits, axis=-1, keepdims=True))
                p = (e * (1.0 / jnp.sum(e, axis=-1, keepdims=True))).astype(bf16)
                mixes.append(mm(p, v))
            ms[rows, lanes] = jnp.where(low, mixes[0], mixes[1]).astype(bf16)

    out = (wide + mm(ms[...], co_ref[...])).astype(bf16)
    out_wide = out.astype(f32)
    for i in range(2):
        for s2 in range(2):
            at = SEQS * i + 128 * s2
            xsc[:, i, s2, :, :E] = out_wide[at : at + 128].reshape(N, 8, E)
    ao_ref[...] = xsc[:, :, :, :, :E].reshape(ROWS, E).astype(bf16)

    factors = (mmt(f_ref[...], norm(out_wide)) * alive[0:1, :]).astype(bf16)
    for ref, at in ((l_ref, 0), (r_ref, C)):
        for i in range(2):
            ref[C * i : C * i + C, :] = factors[at : at + C, SEQS * i : SEQS * i + SEQS]
        counts = [
            jnp.sum(alive[0:1, SEQS * i : SEQS * i + SEQS], axis=-1, keepdims=True)
            for i in range(2)
        ]
        row = lax.broadcasted_iota(jnp.int32, (LR - 2 * C, SEQS), 0)
        ref[2 * C :, :] = jnp.where(row == 0, counts[0], counts[1]).astype(bf16)


def column_step(mr, xc, wo, cq, ck, cv, co, f):
    return pl.pallas_call(
        column_kernel,
        in_specs=whole(8),
        out_specs=whole(3),
        out_shape=[
            jax.ShapeDtypeStruct((ROWS, E), bf16),
            jax.ShapeDtypeStruct((LR, SEQS), bf16),
            jax.ShapeDtypeStruct((LR, SEQS), bf16),
        ],
        scratch_shapes=[
            pltpu.VMEM((2, N, 2, 8, E), f32),
            pltpu.VMEM((N, 2, 2, 8, E + 128), f32),
            pltpu.VMEM((ROWS, E), bf16),
            pltpu.VMEM((ROWS, E), bf16),
            pltpu.VMEM((ROWS, E), bf16),
            pltpu.VMEM((ROWS, E), bf16),
        ],
        compiler_params=params(),
        cost_estimate=cost(5 * 2 * ROWS * E * E, 9_000_000, 2 * H * SEQS * SEQS),
    )(mr, xc, wo, cq, ck, cv, co, f)


def back_kernel(in_ref, out_ref):
    o = lax.broadcasted_iota(jnp.int32, (ROWS, ROWS), 0)
    r = lax.broadcasted_iota(jnp.int32, (ROWS, ROWS), 1)
    src = (((o >> 1) & 15) << 5) + ((o & 1) << 4) + (o >> 5)
    perm = jnp.where(src == r, 1.0, 0.0).astype(bf16)
    out_ref[...] = mm(perm, in_ref[...]).astype(bf16)


def back(rows):
    return pl.pallas_call(
        back_kernel,
        in_specs=whole(1),
        out_specs=pl.BlockSpec(memory_space=pltpu.VMEM),
        out_shape=jax.ShapeDtypeStruct((ROWS, E), bf16),
        compiler_params=params(),
        cost_estimate=cost(2 * ROWS * ROWS * E, 2_000_000),
    )(rows)


def pair_kernel(l_ref, r_ref, wk_ref, out_ref, lf, lg, lp, lhs, osc):
    every = l_ref[...].reshape(N * LR, SEQS).astype(f32)
    for k, ref in enumerate((lf, lg)):
        ref[...] = every[:, 128 * k : 128 * k + 128]

    def across(ref, start):
        return jnp.concatenate(
            [ref[pl.ds(start + i, N, stride=LR), :] for i in (0, C)], axis=0
        )

    for c in range(C):
        lp[C * c : C * c + C, :128] = across(lf, c).astype(bf16)
        lp[C * c : C * c + C, 128:] = across(lg, c).astype(bf16)
    left_count = jnp.concatenate(
        [lf[pl.ds(2 * C + i, N, stride=LR), :] for i in range(2)], axis=0
    )
    right = r_ref[:, : 2 * C, :].reshape(N * 2 * C, SEQS)
    for c in range(0, C, 4):
        outer = mmt(lp[C * c : C * c + 4 * C, :], right).astype(bf16)
        for k in range(4):
            for j in range(8):
                lhs[C * j : C * j + C, 128 * (c + k) : 128 * (c + k) + 128] = outer[
                    C * k : C * k + C, 128 * j : 128 * j + 128
                ]
    acc = mm(lhs[...], wk_ref[...])
    for j in range(C):
        part = acc[C * (j // 4) : C * (j // 4) + C, 128 * (j % 4) : 128 * (j % 4) + 128]
        right_count = r_ref[j >> 1, 2 * C : LR, :128].astype(f32)[(j & 1) : (j & 1) + 1, :]
        part = part / (jnp.minimum(left_count, right_count) + 0.001)
        for i in range(2):
            osc[pl.ds(C * i + j, N, stride=2 * C), :] = part[N * i : N * i + N, :]
    out_ref[...] = osc[...].astype(bf16)


def pair_step(left, right, wk):
    return pl.pallas_call(
        pair_kernel,
        in_specs=whole(3),
        out_specs=pl.BlockSpec(memory_space=pltpu.VMEM),
        out_shape=jax.ShapeDtypeStruct((C * C, PC), bf16),
        scratch_shapes=[
            pltpu.VMEM((N * LR, 128), f32),
            pltpu.VMEM((N * LR, 128), f32),
            pltpu.VMEM((1024, SEQS), bf16),
            pltpu.VMEM((256, 4096), bf16),
            pltpu.VMEM((1024, PC), f32),
        ],
        compiler_params=params(),
        cost_estimate=cost(2 * 1024 * 1024 * 256 + 2 * 256 * 4096 * 512, 6_000_000),
    )(left, right, wk)


def exchange(x, axis):
    return lax.all_to_all(x, axis, split_axis=0, concat_axis=0, tiled=True)


def on_device(x, occupancy, wq, wk, wv, wo, cq, ck, cv, co, f1, f2, wp):
    x = x.reshape(ROWS, E)
    live = occupancy.astype(f32).reshape(ROWS, 1)
    factors = jnp.concatenate([f1.T, f2.T], axis=0)

    qk, v = row_proj(x, live, wq, wk, wv)
    qk = exchange(qk.reshape(N, 512, 128), "cols").reshape(N, 2, 256, 128)
    xr, pair_w = turn(x, live, wp)
    xc = exchange(xr.reshape(N, 32, E + 128), "depth").reshape(ROWS, E + 128)
    v, qk = lax.optimization_barrier((v, qk))
    v = exchange(v, "cols")

    parts = exchange(partial_logits(qk).reshape(N, I, SITES), "depth")
    p = exchange(row_softmax(parts), "depth").reshape(SITES, SITES)
    mix = row_mix(p, v)
    mr = exchange(mix.reshape(N * N, 16, 128), ("cols", "depth")).reshape(4096, 128)

    rows, left, right = column_step(mr, xc, wo, cq, ck, cv, co, factors)
    right = lax.ppermute(
        right, ("depth", "cols"), [(N * d + g, N * g + d) for d in range(N) for g in range(N)]
    )
    left = exchange(jnp.broadcast_to(left[None], (N, LR, SEQS)), "depth")
    right = exchange(jnp.broadcast_to(right[None], (N, LR, SEQS)), "cols")
    rows = exchange(rows.reshape(N, 32, E), "depth")
    out = back(rows.reshape(ROWS, E)).reshape(S, I, E)
    pair = pair_step(left, right, pair_w).reshape(C, C, PC)
    return out, pair


def solution(mesh):
    placed = (P("depth", "cols", None), P("depth", "cols")) + (P(),) * 11
    return jax.shard_map(
        on_device,
        mesh=mesh,
        in_specs=placed,
        out_specs=(P("depth", "cols", None), P("cols", "depth", None)),
        check_vma=False,
    )
```

time: 777 us -> 286 us (0.37)
  waiting for transfers between devices: 424 us -> 92.7 us
  local copies, waits for them, and re-layouts: 79.9 us -> 4.57 us
  matrix products: 58.8 us -> 0 us
  Pallas kernels: 0 us -> 40.4 us
  blocking collectives: 152 us -> 112 us
  between operations: 14.1 us -> 0.72 us
    all_gather x2 -> x0, waiting for transfers between devices: 323 us -> none  [the longest x1 174 us: on_device(): piece = lax.all_gather(keys, 'cols', axis=1, tiled=True)]
    all_gather x4 -> x0, blocking collectives: 152 us -> none  [the longest x1 61.6 us: on_device(): lax.all_gather(right, 'cols', axis=1, tiled=True)]
    all_to_all x0 -> x4, blocking collectives: none -> 112 us  [exchange(): return lax.all_to_all(x, axis, split_axis=0, concat_axis=0, tiled=True)]
    psum x1 -> x0, waiting for transfers between devices: 101 us -> none  [on_device(): logits = lax.psum(partial_logits, 'depth')]
    all_to_all x5, waiting for transfers between devices: 0.01 us -> 85.7 us  [exchange(): return lax.all_to_all(x, axis, split_axis=0, concat_axis=0, tiled=True)]
    dot_general x16 -> x0, matrix products: 53.8 us -> none  [the longest x10 22.2 us: project_through(): return jnp.dot(values, weight, preferred_element_type=jnp.float32)]
    pallas_call x0 -> x8, Pallas kernels: none -> 40.4 us  [the longest x1 11.6 us: column_step(): pl.pallas_call(column_kernel, in_specs=whole(8), out_specs=whole(3), out_...]
    all_gather x4 -> x0, local copies, waits for them, and re-layouts: 34.7 us -> none  [the longest x1 16.7 us: on_device(): piece = lax.all_gather(keys, 'cols', axis=1, tiled=True)]
  transfers between devices with their start and end apart: 8 -> 6, of which waited for: 3 -> 6; matrix products, arithmetic and copies ran while one was open for 12% -> 0% of each run, Pallas kernels for 0% -> 4%
where the time goes in v1:
time: 286 us; the launch traced here: 285 us
  blocking collectives  112 us (39%)
  waiting for transfers between devices  92.7 us (32%)
  Pallas kernels  40.4 us (14%)
  starting transfers between devices  32.9 us (12%)
  local copies, waits for them, and re-layouts  4.57 us (2%)
    all_to_all x4, blocking collectives, exchange(): return lax.all_to_all(x, axis, split_axis=0, concat_axis=0, tiled=True)  112 us
    all_to_all x5, waiting for transfers between devices, exchange(): return lax.all_to_all(x, axis, split_axis=0, concat_axis=0, tiled=True)  85.7 us
    all_to_all x5, starting transfers between devices, exchange(): return lax.all_to_all(x, axis, split_axis=0, concat_axis=0, tiled=True)  30.5 us
    pallas_call x1, Pallas kernels, column_step(): pl.pallas_call(column_kernel, in_specs=whole(8), out_specs=whole(3), out_...  11.6 us
    ppermute x1, waiting for transfers between devices, on_device(): lax.ppermute(right, ('depth', 'cols'), [(N * d + g, N * g + d) for d in r...  7 us
    pallas_call x1, Pallas kernels, pair_step(): pl.pallas_call(pair_kernel, in_specs=whole(3), out_specs=pl.BlockSpec(mem...  6.35 us
    pallas_call x1, Pallas kernels, row_proj(): pl.pallas_call(row_proj_kernel, grid=(3,), in_specs=[pl.BlockSpec((ROWS,...  6.3 us
  transfers between devices with their start and end apart: 6, of which 6 were waited for; matrix products, arithmetic and copies ran while one was open for 0% of the time, Pallas kernels for 4%

profile of v1, /device:TPU:4, one launch (start us, length us, event | category | flops | bytes accessed | tf_op | source)
XLA Modules:
  0.0 284.6 jit_solution(462146735126654371)
XLA Ops:
  2.3 6.3 %shard_map.140 = (bf16[16,2,256,128]{3,2,1,0:T(8,128)(2,1)}, bf16[16,256,128]{2,1,0:T(8,128)(2,1)}) custom-call(bf16[512,768]{1,0:T(8,128)(2,1)} %bitcast.27, f32[512,1]{1,0:T(8,128)} %reshape.62.live_ref, bf16[768,768]{1,0:T(8,128)(2,1)} %wq_ref.1, bf16[768,768]{1,0:T(8,128)(2,1)} %wk_ref.1, bf16[768,768]{1,0:T(8,128)(2,1)} %wv_ref.1), custom_call_target="tpu_custom_call" | custom-call | flops 1811939328 | bytes 8000000 | tf_op jit(solution)/shard_map/pallas_call | solution.py:96
  8.6 63.7 %all_to_all.45 = bf16[16,512,128]{2,1,0:T(8,128)(2,1)} all-to-all(bf16[16,512,128]{2,1,0:T(8,128)(2,1)} %bitcast.20), channel_id=1, replica_groups=mesh['depth'=16,'cols'=16] {'cols'}, dimensions={0} | all-to-all | bytes 4194304 | tf_op jit(solution)/shard_map/all_to_all | solution.py:397
  72.3 3.3 %shard_map.141 = f32[512,512]{1,0:T(8,128)} custom-call(bf16[16,2,256,128]{3,2,1,0:T(8,128)(2,1)} %bitcast.15), custom_call_target="tpu_custom_call" | custom-call | flops 536870912 | bytes 3000000 | tf_op jit(solution)/shard_map/pallas_call | solution.py:163
  75.6 18.2 %all_to_all.46.in_ref = f32[16,32,512]{2,1,0:T(8,128)} all-to-all(f32[16,32,512]{2,1,0:T(8,128)} %bitcast.16), channel_id=1, replica_groups=mesh['depth'=16,'cols'=16] {'depth'}, dimensions={0} | all-to-all | bytes 2097152 | tf_op jit(solution)/shard_map/all_to_all | solution.py:397
  93.7 2.3 shard_map.142
  96.0 15.0 %all_to_all.47 = bf16[16,32,512]{2,1,0:T(8,128)(2,1)} all-to-all(bf16[16,32,512]{2,1,0:T(8,128)(2,1)} %shard_map.142), channel_id=1, replica_groups=mesh['depth'=16,'cols'=16] {'depth'}, dimensions={0} | all-to-all | bytes 1048576 | tf_op jit(solution)/shard_map/all_to_all | solution.py:397
  111.0 3.7 %all-to-all-start.3 = ((bf16[16,256,128]{2,1,0:T(8,128)(2,1)}), bf16[16,256,128]{2,1,0:T(8,128)(2,1)S(1)}, u32[]{:S(2)}, u32[]{:S(2)}) async-start(bf16[16,256,128]{2,1,0:T(8,128)(2,1)} %get-tuple-element.14), calls=%async_computation.3 | async-start | bytes 2097152 | tf_op jit(solution)/shard_map/all_to_all | solution.py:397
  114.7 4.5 %shard_map.144 = (bf16[512,896]{1,0:T(8,128)(2,1)}, bf16[4096,512]{1,0:T(8,128)(2,1)}) custom-call(bf16[512,768]{1,0:T(8,128)(2,1)} %bitcast.28, f32[512,1]{1,0:T(8,128)} %reshape.62.live_ref, bf16[1024,128]{1,0:T(8,128)(2,1)} %wp_ref.1), custom_call_target="tpu_custom_call" | custom-call | flops 402653184 | bytes 8000000 | tf_op jit(solution)/shard_map/pallas_call | solution.py:136
  119.3 26.4 %all-to-all-done.3.v_ref = bf16[16,256,128]{2,1,0:T(8,128)(2,1)S(1)} async-done(((bf16[16,256,128]{2,1,0:T(8,128)(2,1)}), bf16[16,256,128]{2,1,0:T(8,128)(2,1)S(1)}, u32[]{:S(2)}, u32[]{:S(2)}) %all-to-all-start.3) | async-done | bytes 1048608 | tf_op jit(solution)/shard_map/all_to_all | solution.py:397
  145.7 6.2 %all-to-all-start.5 = ((bf16[16,32,896]{2,1,0:T(8,128)(2,1)}), bf16[16,32,896]{2,1,0:T(8,128)(2,1)S(1)}, u32[]{:S(2)}, u32[]{:S(2)}) async-start(bf16[16,32,896]{2,1,0:T(8,128)(2,1)} %bitcast.23), calls=%async_computation.5 | async-start | bytes 1835008 | tf_op jit(solution)/shard_map/all_to_all | solution.py:397
  151.8 3.4 %shard_map.143 = bf16[4096,128]{1,0:T(8,128)(2,1)} custom-call(bf16[512,512]{1,0:T(8,128)(2,1)} %bitcast.19, bf16[16,256,128]{2,1,0:T(8,128)(2,1)} %copy-done), custom_call_target="tpu_custom_call" | custom-call | flops 536870912 | bytes 3000000 | tf_op jit(solution)/shard_map/pallas_call | solution.py:219
  155.2 8.3 %all-to-all-done.5 = bf16[16,32,896]{2,1,0:T(8,128)(2,1)S(1)} async-done(((bf16[16,32,896]{2,1,0:T(8,128)(2,1)}), bf16[16,32,896]{2,1,0:T(8,128)(2,1)S(1)}, u32[]{:S(2)}, u32[]{:S(2)}) %all-to-all-start.5) | async-done | bytes 917536 | tf_op jit(solution)/shard_map/all_to_all | solution.py:397
  163.6 8.6 %all-to-all-start.4 = ((bf16[256,16,128]{2,1,0:T(8,128)(2,1)}), bf16[256,16,128]{2,1,0:T(8,128)(2,1)S(1)}, u32[]{:S(2)}, u32[]{:S(2)}) async-start(bf16[256,16,128]{2,1,0:T(8,128)(2,1)} %bitcast.17), calls=%async_computation.4 | async-start | bytes 2097152 | tf_op jit(solution)/shard_map/all_to_all | solution.py:397
  172.8 29.8 %all-to-all-done.4 = bf16[256,16,128]{2,1,0:T(8,128)(2,1)S(1)} async-done(((bf16[256,16,128]{2,1,0:T(8,128)(2,1)}), bf16[256,16,128]{2,1,0:T(8,128)(2,1)S(1)}, u32[]{:S(2)}, u32[]{:S(2)}) %all-to-all-start.4) | async-done | bytes 1048608 | tf_op jit(solution)/shard_map/all_to_all | solution.py:397
  203.5 11.6 %shard_map.145 = (bf16[512,768]{1,0:T(8,128)(2,1)}, bf16[80,256]{1,0:T(8,128)(2,1)}, bf16[80,256]{1,0:T(8,128)(2,1)}) custom-call(bf16[4096,128]{1,0:T(8,128)(2,1)} %bitcast.21, bf16[512,896]{1,0:T(8,128)(2,1)} %bitcast.22, bf16[768,768]{1,0:T(8,128)(2,1)} %wo_ref.1, bf16[768,768]{1,0:T(8,128)(2,1)} %cq_ref.1, bf16[768,768]{1,0:T(8,128)(2,1)} %ck_ref.1, ...), custom_call_target="tpu_custom_call" | custom-call | flops 3019898880 | bytes 9000000 | tf_op jit(solution)/shard_map/pallas_call | solution.py:303
  216.0 15.1 %all_to_all.48.l_ref = bf16[16,80,256]{2,1,0:T(8,128)(2,1)} all-to-all(bf16[16,80,256]{2,1,0:T(8,128)(2,1)S(1)} %broadcast_in_dim.4), channel_id=1, replica_groups=mesh['depth'=16,'cols'=16] {'depth'}, dimensions={0} | all-to-all | bytes 1310720 | tf_op jit(solution)/shard_map/all_to_all | solution.py:397
  231.1 5.8 %all-to-all-start.6 = ((bf16[16,32,768]{2,1,0:T(8,128)(2,1)}), bf16[16,32,768]{2,1,0:T(8,128)(2,1)S(1)}, u32[]{:S(2)}, u32[]{:S(2)}) async-start(bf16[16,32,768]{2,1,0:T(8,128)(2,1)} %bitcast.11), calls=%async_computation.6 | async-start | bytes 1572864 | tf_op jit(solution)/shard_map/all_to_all | solution.py:397
  236.9 2.4 collective-permute-start
  239.3 7.0 %collective-permute-done = bf16[80,256]{1,0:T(8,128)(2,1)S(1)} collective-permute-done((bf16[80,256]{1,0:T(8,128)(2,1)S(1)}, bf16[80,256]{1,0:T(8,128)(2,1)S(1)}, u32[]{:S(2)}, u32[]{:S(2)}) %collective-permute-start) | collective-permute-done | bytes 40992 | tf_op jit(solution)/shard_map/ppermute | solution.py:418
  246.3 1.3 all-to-all-done.6
  248.6 6.3 %all-to-all-start.8 = ((bf16[16,80,256]{2,1,0:T(8,128)(2,1)}), bf16[16,80,256]{2,1,0:T(8,128)(2,1)S(1)}, u32[]{:S(2)}, u32[]{:S(2)}) async-start(bf16[16,80,256]{2,1,0:T(8,128)(2,1)} %broadcast_in_dim.5), calls=%async_computation.8 | async-start | bytes 1310720 | tf_op jit(solution)/shard_map/all_to_all | solution.py:397
  254.9 2.6 shard_map.146
  257.5 19.9 %all-to-all-done.8.r_ref = bf16[16,80,256]{2,1,0:T(8,128)(2,1)S(1)} async-done(((bf16[16,80,256]{2,1,0:T(8,128)(2,1)}), bf16[16,80,256]{2,1,0:T(8,128)(2,1)S(1)}, u32[]{:S(2)}, u32[]{:S(2)}) %all-to-all-start.8) | async-done | bytes 655392 | tf_op jit(solution)/shard_map/all_to_all | solution.py:397
  278.3 6.3 %shard_map.147 = bf16[1024,128]{1,0:T(8,128)(2,1)} custom-call(bf16[16,80,256]{2,1,0:T(8,128)(2,1)} %all_to_all.48.l_ref, bf16[16,80,256]{2,1,0:T(8,128)(2,1)} %copy-done.4, bf16[4096,512]{1,0:T(8,128)(2,1)} %get-tuple-element.19.wk_ref), custom_call_target="tpu_custom_call" | custom-call | flops 1610612736 | bytes 6000000 | tf_op jit(solution)/shard_map/pallas_call | solution.py:379
  (21 shorter events, 5.9 us)
Async XLA Ops:
  111.0 34.6 %all-to-all-start.3 = ((bf16[16,256,128]{2,1,0:T(8,128)(2,1)}), bf16[16,256,128]{2,1,0:T(8,128)(2,1)S(1)}, u32[]{:S(2)}, u32[]{:S(2)}) async-start(bf16[16,256,128]{2,1,0:T(8,128)(2,1)} %get-tuple-element.14), calls=%async_computation.3 | async-start | bytes 2097152 | tf_op jit(solution)/shard_map/all_to_all | solution.py:397
  145.7 6.2 %copy-start = (bf16[16,256,128]{2,1,0:T(8,128)(2,1)}, bf16[16,256,128]{2,1,0:T(8,128)(2,1)S(1)}, u32[]{:S(2)}) copy-start(bf16[16,256,128]{2,1,0:T(8,128)(2,1)S(1)} %all-to-all-done.3.v_ref) | copy-start | bytes 3145732
  145.7 17.9 %all-to-all-start.5 = ((bf16[16,32,896]{2,1,0:T(8,128)(2,1)}), bf16[16,32,896]{2,1,0:T(8,128)(2,1)S(1)}, u32[]{:S(2)}, u32[]{:S(2)}) async-start(bf16[16,32,896]{2,1,0:T(8,128)(2,1)} %bitcast.23), calls=%async_computation.5 | async-start | bytes 1835008 | tf_op jit(solution)/shard_map/all_to_all | solution.py:397
  155.2 16.9 %copy-start.5 = (bf16[768,32]{0,1:T(8,128)(2,1)S(1)}, bf16[768,32]{0,1:T(8,128)(2,1)}, u32[]{:S(2)}) copy-start(bf16[768,32]{0,1:T(8,128)(2,1)} %param.24) | copy-start | bytes 147460
  155.2 16.9 %copy-start.6 = (bf16[768,32]{0,1:T(8,128)(2,1)S(1)}, bf16[768,32]{0,1:T(8,128)(2,1)}, u32[]{:S(2)}) copy-start(bf16[768,32]{0,1:T(8,128)(2,1)} %param.23) | copy-start | bytes 147460
  163.6 39.0 %copy-start.3 = (bf16[16,32,896]{2,1,0:T(8,128)(2,1)}, bf16[16,32,896]{2,1,0:T(8,128)(2,1)S(1)}, u32[]{:S(2)}) copy-start(bf16[16,32,896]{2,1,0:T(8,128)(2,1)S(1)} %all-to-all-done.5) | copy-start | bytes 2752516
  163.6 39.0 %all-to-all-start.4 = ((bf16[256,16,128]{2,1,0:T(8,128)(2,1)}), bf16[256,16,128]{2,1,0:T(8,128)(2,1)S(1)}, u32[]{:S(2)}, u32[]{:S(2)}) async-start(bf16[256,16,128]{2,1,0:T(8,128)(2,1)} %bitcast.17), calls=%async_computation.4 | async-start | bytes 2097152 | tf_op jit(solution)/shard_map/all_to_all | solution.py:397
  202.6 1.0 copy-start.2
  216.0 21.0 %copy-start.7 = (bf16[80,256]{1,0:T(8,128)(2,1)S(1)}, bf16[80,256]{1,0:T(8,128)(2,1)}, u32[]{:S(2)}) copy-start(bf16[80,256]{1,0:T(8,128)(2,1)} %get-tuple-element.18) | copy-start | bytes 122884
  231.1 16.5 %all-to-all-start.6 = ((bf16[16,32,768]{2,1,0:T(8,128)(2,1)}), bf16[16,32,768]{2,1,0:T(8,128)(2,1)S(1)}, u32[]{:S(2)}, u32[]{:S(2)}) async-start(bf16[16,32,768]{2,1,0:T(8,128)(2,1)} %bitcast.11), calls=%async_computation.6 | async-start | bytes 1572864 | tf_op jit(solution)/shard_map/all_to_all | solution.py:397
  236.9 9.4 %collective-permute-start = (bf16[80,256]{1,0:T(8,128)(2,1)S(1)}, bf16[80,256]{1,0:T(8,128)(2,1)S(1)}, u32[]{:S(2)}, u32[]{:S(2)}) collective-permute-start(bf16[80,256]{1,0:T(8,128)(2,1)S(1)} %copy-done.7), channel_id=1, source_target_pairs={{0,0},{1,16},{2,32},{3,48},{4,64},{5,80},{6,96},{7,112},{8,128},{9... | collective-permute-start | bytes 122888 | tf_op jit(solution)/shard_map/ppermute | solution.py:418
  247.6 7.2 %copy-start.1 = (bf16[16,32,768]{2,1,0:T(8,128)(2,1)}, bf16[16,32,768]{2,1,0:T(8,128)(2,1)S(1)}, u32[]{:S(2)}) copy-start(bf16[16,32,768]{2,1,0:T(8,128)(2,1)S(1)} %all-to-all-done.6) | copy-start | bytes 2359300
  248.6 28.8 %all-to-all-start.8 = ((bf16[16,80,256]{2,1,0:T(8,128)(2,1)}), bf16[16,80,256]{2,1,0:T(8,128)(2,1)S(1)}, u32[]{:S(2)}, u32[]{:S(2)}) async-start(bf16[16,80,256]{2,1,0:T(8,128)(2,1)} %broadcast_in_dim.5), calls=%async_computation.8 | async-start | bytes 1310720 | tf_op jit(solution)/shard_map/all_to_all | solution.py:397
  277.4 0.8 copy-start.4

commit v2 on v1

v2 whole, which is shorter than its diff:
```python
import functools
import math

import jax
import jax.numpy as jnp
from jax import lax
from jax.experimental import pallas as pl
from jax.experimental.pallas import tpu as pltpu
from jax.sharding import PartitionSpec as P

f32 = jnp.float32
bf16 = jnp.bfloat16

S = 16
I = 32
E = 768
H = 12
N = 16
ROWS = S * I
SEQS = 256
SITES = 512
C = 32
PC = 128
XW = E + 128

NT = (((1,), (1,)), ((), ()))


def norm(wide):
    center = wide - jnp.mean(wide, axis=-1, keepdims=True)
    spread = jnp.mean(center * center, axis=-1, keepdims=True)
    return (center * lax.rsqrt(spread + 1e-05)).astype(bf16)


def mm(a, b):
    return jnp.dot(a, b, preferred_element_type=f32)


def mmt(a, b):
    return lax.dot_general(a, b, NT, preferred_element_type=f32)


def lanes_lo(a, b):
    return jnp.concatenate([a[:, :64], b[:, :64]], axis=1)


def lanes_hi(a, b):
    return jnp.concatenate([a[:, 64:], b[:, 64:]], axis=1)


def whole(n):
    return [pl.BlockSpec(memory_space=pltpu.VMEM)] * n


def params(mib):
    return pltpu.CompilerParams(vmem_limit_bytes=mib * 1024 * 1024)


def cost(flops, bytes_accessed, transcendentals=0):
    return pl.CostEstimate(
        flops=flops, bytes_accessed=bytes_accessed, transcendentals=transcendentals
    )


def mask_rows(occupancy, width):
    s = lax.broadcasted_iota(jnp.int32, (ROWS, S), 0) // I
    own = s == lax.broadcasted_iota(jnp.int32, (ROWS, S), 1)
    spread = mm(jnp.where(own, 1.0, 0.0).astype(bf16), occupancy.astype(f32).astype(bf16))
    i = lax.broadcasted_iota(jnp.int32, (ROWS, I), 0) % I
    own = i == lax.broadcasted_iota(jnp.int32, (ROWS, I), 1)
    column = jnp.sum(jnp.where(own, spread, 0.0), axis=-1, keepdims=True)
    return jnp.broadcast_to(column, (ROWS, width))


def row_proj_kernel(x_ref, occ_ref, wq_ref, wk_ref, wv_ref, out_ref, xn_ref, live_ref):
    @pl.when(pl.program_id(0) == 0)
    def _():
        xn_ref[...] = norm(x_ref[...].astype(f32))
        live_ref[...] = mask_rows(occ_ref[...], 128)

    xn = xn_ref[...]
    live = live_ref[...]
    half = ROWS // 2
    for index, w_ref in enumerate((wq_ref, wk_ref, wv_ref)):
        y = mm(xn, w_ref[...])
        for t in range(2):
            part = y[:, 128 * t : 128 * t + 128]
            if index < 2:
                part = part * live
            part = part.astype(bf16)
            a, b = part[:half], part[half:]
            out_ref[2 * t, 256 * index : 256 * index + 256] = lanes_lo(a, b)
            out_ref[2 * t + 1, 256 * index : 256 * index + 256] = lanes_hi(a, b)


def row_proj(x, occupancy, wq, wk, wv):
    w = pl.BlockSpec((E, 256), lambda n: (0, n))
    return pl.pallas_call(
        row_proj_kernel,
        grid=(3,),
        in_specs=[
            pl.BlockSpec((ROWS, E), lambda n: (0, 0)),
            pl.BlockSpec((S, I), lambda n: (0, 0)),
            w,
            w,
            w,
        ],
        out_specs=pl.BlockSpec((4, 768, 128), lambda n: (n, 0, 0)),
        out_shape=jax.ShapeDtypeStruct((N, 768, 128), bf16),
        scratch_shapes=[pltpu.VMEM((ROWS, E), bf16), pltpu.VMEM((ROWS, 128), f32)],
        compiler_params=params(20),
        cost_estimate=cost(3 * 2 * ROWS * E * E, 8_000_000),
    )(x, occupancy, wq, wk, wv)


def turn_kernel(x_ref, occ_ref, wp_ref, xr_ref, wk_ref):
    r = lax.broadcasted_iota(jnp.int32, (ROWS, ROWS), 0)
    o = lax.broadcasted_iota(jnp.int32, (ROWS, ROWS), 1)
    src = ((r & 15) << 5) + ((r >> 5) << 1) + ((r >> 4) & 1)
    perm = jnp.where(src == o, 1.0, 0.0).astype(bf16)
    xr_ref[:, :E] = mm(perm, x_ref[...]).astype(bf16)
    xr_ref[:, E:] = mm(perm, mask_rows(occ_ref[...], 128).astype(bf16)).astype(bf16)
    wk_ref[...] = jnp.zeros_like(wk_ref)
    for c in range(C):
        w = wp_ref[C * c : C * c + C, :]
        for j in range(4):
            wk_ref[128 * c + 32 * j : 128 * c + 32 * j + 32, 128 * j : 128 * j + 128] = w


def turn(x, occupancy, wp):
    return pl.pallas_call(
        turn_kernel,
        in_specs=whole(3),
        out_specs=whole(2),
        out_shape=[
            jax.ShapeDtypeStruct((ROWS, XW), bf16),
            jax.ShapeDtypeStruct((4096, 512), bf16),
        ],
        compiler_params=params(16),
        cost_estimate=cost(2 * ROWS * ROWS * E, 8_000_000),
    )(x, occupancy, wp)


def logits_kernel(qk_ref, out_ref):
    def side(k):
        return jnp.concatenate(
            [
                qk_ref[:, 256 * k + I * s : 256 * k + I * s + I, :].reshape(SITES, 128)
                for s in range(S // 2)
            ],
            axis=1,
        )

    out_ref[...] = mmt(side(0), side(1)) * (1.0 / math.sqrt(64 * SEQS))


def partial_logits(qkv):
    return pl.pallas_call(
        logits_kernel,
        grid=(1,),
        in_specs=[pl.BlockSpec((N, 512, 128), lambda n: (0, 0, 0))],
        out_specs=pl.BlockSpec((SITES, SITES), lambda n: (0, 0)),
        out_shape=jax.ShapeDtypeStruct((SITES, SITES), f32),
        compiler_params=params(20),
        cost_estimate=cost(2 * SITES * SITES * 1024, 3_000_000),
    )(qkv)


def softmax_kernel(in_ref, xr_ref, out_ref):
    total = in_ref[0]
    for k in range(1, N):
        total = total + in_ref[k]
    top = jnp.max(total, axis=-1, keepdims=True)
    e = jnp.exp(total - top)
    p = (e / jnp.sum(e, axis=-1, keepdims=True)).astype(bf16)
    for k in range(N):
        out_ref[k, :, :SITES] = p
    out_ref[:, :, SITES:] = xr_ref[...].reshape(N, I, XW)


def row_softmax(parts, xr):
    return pl.pallas_call(
        softmax_kernel,
        in_specs=whole(2),
        out_specs=pl.BlockSpec(memory_space=pltpu.VMEM),
        out_shape=jax.ShapeDtypeStruct((N, I, SITES + XW), bf16),
        compiler_params=params(16),
        cost_estimate=cost(N * I * SITES, 4_000_000, I * SITES),
    )(parts, xr)


def row_mix_kernel(p_ref, v_ref, out_ref):
    v = jnp.concatenate(
        [v_ref[:, I * s : I * s + I, :].reshape(SITES, 128) for s in range(S // 2)],
        axis=1,
    )
    mix = mm(p_ref[...].reshape(SITES, SITES), v).astype(bf16)
    r = lax.broadcasted_iota(jnp.int32, (256, 256), 0)
    o = lax.broadcasted_iota(jnp.int32, (256, 256), 1)
    perm = jnp.where(((r & 7) << 5) + (r >> 3) == o, 1.0, 0.0).astype(bf16)

    def block(b):
        part = mix[I * b : I * b + I, :]
        return jnp.concatenate(
            [part[:, 128 * s : 128 * s + 128] for s in range(8)], axis=0
        )

    for b in range(0, N, 2):
        pair = jnp.concatenate([block(b), block(b + 1)], axis=1)
        turned = mm(perm, pair).astype(bf16)
        out_ref[256 * b : 256 * b + 256, :] = turned[:, :128]
        out_ref[256 * b + 256 : 256 * b + 512, :] = turned[:, 128:]


def row_mix(px, qkv):
    return pl.pallas_call(
        row_mix_kernel,
        grid=(1,),
        in_specs=[
            pl.BlockSpec((N, I, SITES), lambda n: (0, 0, 0)),
            pl.BlockSpec((N, 256, 128), lambda n: (0, 2, 0)),
        ],
        out_specs=pl.BlockSpec((4096, 128), lambda n: (0, 0)),
        out_shape=jax.ShapeDtypeStruct((4096, 128), bf16),
        compiler_params=params(20),
        cost_estimate=cost(2 * SITES * SITES * 1024, 3_000_000),
    )(px, qkv)


def column_kernel(
    mr_ref, px_ref, wo_ref, cq_ref, ck_ref, cv_ref, co_ref, f_ref,
    out_ref, r_ref,
    ysc, xsc, qs, ks, vs, ms,
):
    halves = []
    for pick in (lanes_lo, lanes_hi):
        halves.append(
            jnp.concatenate(
                [
                    pick(mr_ref[512 * t : 512 * t + 256, :], mr_ref[512 * t + 256 : 512 * t + 512, :])
                    for t in range(H // 2)
                ],
                axis=1,
            )
        )
    mixed = jnp.concatenate(halves, axis=0)
    ysc[...] = mm(mixed, wo_ref[...]).reshape(2, N, 2, 8, E)
    xsc[...] = px_ref[:, :, SITES:].astype(f32).reshape(N, 2, 2, 8, XW)
    blocks = []
    masks = []
    for i in range(2):
        for s2 in range(2):
            blocks.append((ysc[s2, :, i] + xsc[:, i, s2, :, :E]).reshape(128, E))
            masks.append(xsc[:, i, s2, :, E:].reshape(128, 128))
    after_rows = jnp.concatenate(blocks, axis=0).astype(bf16)
    wide = after_rows.astype(f32)
    mask = jnp.concatenate(masks, axis=0).astype(bf16)
    lane0 = jnp.where(
        lax.broadcasted_iota(jnp.int32, (8, 128), 1) == 0, 1.0, 0.0
    ).astype(bf16)
    alive = mmt(lane0, mask)

    normed = norm(wide)
    qs[...] = mm(normed, cq_ref[...]).astype(bf16)
    ks[...] = mm(normed, ck_ref[...]).astype(bf16)
    vs[...] = mm(normed, cv_ref[...]).astype(bf16)
    low = lax.broadcasted_iota(jnp.int32, (SEQS, 128), 1) < 64
    for i in range(2):
        rows = slice(SEQS * i, SEQS * i + SEQS)
        keep = alive[0:1, rows] > 0
        for t in range(H // 2):
            lanes = slice(128 * t, 128 * t + 128)
            q, k, v = qs[rows, lanes], ks[rows, lanes], vs[rows, lanes]
            mixes = []
            for own in (low, jnp.logical_not(low)):
                logits = mmt(jnp.where(own, q, jnp.zeros_like(q)), k) * 0.125
                logits = jnp.where(keep, logits, -1000000000.0)
                e = jnp.exp(logits - jnp.max(logits, axis=-1, keepdims=True))
                p = (e * (1.0 / jnp.sum(e, axis=-1, keepdims=True))).astype(bf16)
                mixes.append(mm(p, v))
            ms[rows, lanes] = jnp.where(low, mixes[0], mixes[1]).astype(bf16)

    out = (wide + mm(ms[...], co_ref[...])).astype(bf16)
    out_wide = out.astype(f32)
    for i in range(2):
        for s2 in range(2):
            at = SEQS * i + 128 * s2
            xsc[:, i, s2, :, :E] = out_wide[at : at + 128].reshape(N, 8, E)
    out_ref[:, :I, :] = xsc[:, :, :, :, :E].reshape(N, I, E).astype(bf16)

    factors = (mmt(f_ref[...], norm(out_wide)) * alive[0:1, :]).astype(bf16)
    for i in range(2):
        r_ref[C * i : C * i + C, :] = factors[C:, SEQS * i : SEQS * i + SEQS]
    counts = [
        jnp.sum(alive[0:1, SEQS * i : SEQS * i + SEQS], axis=-1, keepdims=True)
        for i in range(2)
    ]
    row = lax.broadcasted_iota(jnp.int32, (C, SEQS), 0)
    count = jnp.where(row == 0, counts[0], counts[1]).astype(bf16)
    left = jnp.concatenate([factors[:C, :], count], axis=1)
    for k in range(N):
        out_ref[k, I:, :] = left


def column_step(mr, px, wo, cq, ck, cv, co, f):
    return pl.pallas_call(
        column_kernel,
        in_specs=whole(8),
        out_specs=whole(2),
        out_shape=[
            jax.ShapeDtypeStruct((N, 2 * I, E), bf16),
            jax.ShapeDtypeStruct((2 * C, SEQS), bf16),
        ],
        scratch_shapes=[
            pltpu.VMEM((2, N, 2, 8, E), f32),
            pltpu.VMEM((N, 2, 2, 8, XW), f32),
            pltpu.VMEM((ROWS, E), bf16),
            pltpu.VMEM((ROWS, E), bf16),
            pltpu.VMEM((ROWS, E), bf16),
            pltpu.VMEM((ROWS, E), bf16),
        ],
        compiler_params=params(40),
        cost_estimate=cost(5 * 2 * ROWS * E * E, 9_000_000, 2 * H * SEQS * SEQS),
    )(mr, px, wo, cq, ck, cv, co, f)


def back_kernel(in_ref, out_ref):
    o = lax.broadcasted_iota(jnp.int32, (ROWS, ROWS), 0)
    r = lax.broadcasted_iota(jnp.int32, (ROWS, ROWS), 1)
    src = (((o >> 1) & 15) << 5) + ((o & 1) << 4) + (o >> 5)
    perm = jnp.where(src == r, 1.0, 0.0).astype(bf16)
    out_ref[...] = mm(perm, in_ref[...].reshape(ROWS, E)).astype(bf16)


def back(both):
    return pl.pallas_call(
        back_kernel,
        grid=(1,),
        in_specs=[pl.BlockSpec((N, I, E), lambda n: (0, 0, 0))],
        out_specs=pl.BlockSpec((ROWS, E), lambda n: (0, 0)),
        out_shape=jax.ShapeDtypeStruct((ROWS, E), bf16),
        compiler_params=params(16),
        cost_estimate=cost(2 * ROWS * ROWS * E, 2_000_000),
    )(both)


def pair_kernel(l_ref, r_ref, n_ref, wk_ref, out_ref, l0, l1, l2, l3, l4, lp, lhs, osc):
    every = l_ref[...].reshape(N * C, E).astype(f32)
    for k, ref in enumerate((l0, l1, l2, l3, l4)):
        ref[...] = every[:, 128 * k : 128 * k + 128]

    def across(ref, row):
        return ref[pl.ds(row, N, stride=C), :]

    for c in range(C):
        rows = slice(C * c, C * c + C)
        lp[rows, :128] = jnp.concatenate([across(l0, c), across(l2, c)], axis=0).astype(bf16)
        lp[rows, 128:] = jnp.concatenate([across(l1, c), across(l3, c)], axis=0).astype(bf16)
    left_count = jnp.concatenate([across(l4, 0), across(l4, 1)], axis=0)
    right = r_ref[...].reshape(N * 2 * C, SEQS)
    for c in range(0, C, 4):
        outer = mmt(lp[C * c : C * c + 4 * C, :], right).astype(bf16)
        for k in range(4):
            for j in range(8):
                lhs[C * j : C * j + C, 128 * (c + k) : 128 * (c + k) + 128] = outer[
                    C * k : C * k + C, 128 * j : 128 * j + 128
                ]
    acc = mm(lhs[...], wk_ref[...])
    right_count = n_ref[...].astype(f32)
    for j in range(C):
        part = acc[C * (j // 4) : C * (j // 4) + C, 128 * (j % 4) : 128 * (j % 4) + 128]
        part = part / (jnp.minimum(left_count, right_count[j : j + 1, :]) + 0.001)
        for i in range(2):
            osc[pl.ds(C * i + j, N, stride=2 * C), :] = part[N * i : N * i + N, :]
    out_ref[...] = osc[...].astype(bf16)


def pair_step(both, right, counts, wk):
    return pl.pallas_call(
        pair_kernel,
        grid=(1,),
        in_specs=[
            pl.BlockSpec((N, I, E), lambda n: (0, 1, 0)),
            pl.BlockSpec((N, 2 * C, SEQS), lambda n: (0, 0, 0)),
            pl.BlockSpec((C, 128), lambda n: (0, 0)),
            pl.BlockSpec((4096, 512), lambda n: (0, 0)),
        ],
        out_specs=pl.BlockSpec((C * C, PC), lambda n: (0, 0)),
        out_shape=jax.ShapeDtypeStruct((C * C, PC), bf16),
        scratch_shapes=[pltpu.VMEM((N * C, 128), f32)] * 5
        + [
            pltpu.VMEM((1024, SEQS), bf16),
            pltpu.VMEM((256, 4096), bf16),
            pltpu.VMEM((1024, PC), f32),
        ],
        compiler_params=params(24),
        cost_estimate=cost(2 * 1024 * 1024 * 256 + 2 * 256 * 4096 * 512, 6_000_000),
    )(both, right, counts, wk)


def exchange(x, axis):
    return lax.all_to_all(x, axis, split_axis=0, concat_axis=0, tiled=True)


def swap(x):
    pairs = [(N * d + g, N * g + d) for d in range(N) for g in range(N)]
    return lax.ppermute(x, ("depth", "cols"), pairs)


def on_device(x, occupancy, wq, wk, wv, wo, cq, ck, cv, co, f1, f2, wp):
    x = x.reshape(ROWS, E)
    factors = jnp.concatenate([f1.T, f2.T], axis=0)

    qkv = exchange(row_proj(x, occupancy, wq, wk, wv), "cols")
    xr, pair_w = turn(x, occupancy, wp)
    parts = exchange(partial_logits(qkv).reshape(N, I, SITES), "depth")
    px = exchange(row_softmax(parts, xr), "depth")
    mix = row_mix(px, qkv)
    mr = exchange(mix.reshape(N * N, 16, 128), ("cols", "depth")).reshape(4096, 128)

    both, right = column_step(mr, px, wo, cq, ck, cv, co, factors)
    right = swap(right)
    both = exchange(both, "depth")
    counts = swap(both[:, I : I + 2, 512:640].reshape(C, 128))
    right = exchange(jnp.broadcast_to(right[None], (N, 2 * C, SEQS)), "cols")
    out = back(both).reshape(S, I, E)
    pair = pair_step(both, right, counts, pair_w).reshape(C, C, PC)
    return out, pair


def solution(mesh):
    placed = (P("depth", "cols", None), P("depth", "cols")) + (P(),) * 11
    return jax.shard_map(
        on_device,
        mesh=mesh,
        in_specs=placed,
        out_specs=(P("depth", "cols", None), P("cols", "depth", None)),
        check_vma=False,
    )
```

time: 286 us -> 257 us (0.90)
  waiting for transfers between devices: 92.7 us -> 68.1 us
  Pallas kernels: 40.4 us -> 22.3 us
  local copies, waits for them, and re-layouts: 4.57 us -> 22.3 us
  blocking collectives: 112 us -> 109 us
    all_to_all x5 -> x4, waiting for transfers between devices: 85.7 us -> 61 us  [exchange(): return lax.all_to_all(x, axis, split_axis=0, concat_axis=0, tiled=True)]
    unnamed x16 -> x46, local copies, waits for them, and re-layouts: 1.84 us -> 21.4 us
    pallas_call x6, Pallas kernels: 29.5 us -> 17.6 us  [the longest x1 8.92 us: column_step(): pl.pallas_call(column_kernel, in_specs=whole(8), out_specs=whole(2), out_...]
    ppermute x1 -> x2, starting transfers between devices: 2.35 us -> 8.39 us  [swap(): return lax.ppermute(x, ('depth', 'cols'), pairs)]
    all_to_all x5 -> x4, starting transfers between devices: 30.5 us -> 24.9 us  [exchange(): return lax.all_to_all(x, axis, split_axis=0, concat_axis=0, tiled=True)]
    pallas_call x1, Pallas kernels: 4.53 us -> 1.22 us  [turn(): pl.pallas_call(turn_kernel, in_specs=whole(3), out_specs=whole(2), out_sh...]
    all_to_all x4 -> x2, blocking collectives: 112 us -> 109 us  [exchange(): return lax.all_to_all(x, axis, split_axis=0, concat_axis=0, tiled=True)]
    ppermute x1 -> x2, waiting for transfers between devices: 7 us -> 7.12 us  [swap(): return lax.ppermute(x, ('depth', 'cols'), pairs)]
  transfers between devices with their start and end apart: 6 -> 6, of which waited for: 6 -> 5; matrix products, arithmetic and copies ran while one was open for 0% -> 0% of each run, Pallas kernels for 4% -> 1%
where the time goes in v2:
time: 257 us; the launch traced here: 256 us
  blocking collectives  109 us (42%)
  waiting for transfers between devices  68.1 us (26%)
  starting transfers between devices  33.3 us (13%)
  local copies, waits for them, and re-layouts  22.3 us (9%)
  Pallas kernels  22.3 us (9%)
    all_to_all x2, blocking collectives, exchange(): return lax.all_to_all(x, axis, split_axis=0, concat_axis=0, tiled=True)  109 us
    all_to_all x4, waiting for transfers between devices, exchange(): return lax.all_to_all(x, axis, split_axis=0, concat_axis=0, tiled=True)  61 us
    all_to_all x4, starting transfers between devices, exchange(): return lax.all_to_all(x, axis, split_axis=0, concat_axis=0, tiled=True)  24.9 us
    unnamed x46, local copies, waits for them, and re-layouts  21.4 us
    pallas_call x1, Pallas kernels, column_step(): pl.pallas_call(column_kernel, in_specs=whole(8), out_specs=whole(2), out_...  8.92 us
    ppermute x2, starting transfers between devices, swap(): return lax.ppermute(x, ('depth', 'cols'), pairs)  8.39 us
    ppermute x2, waiting for transfers between devices, swap(): return lax.ppermute(x, ('depth', 'cols'), pairs)  7.12 us
  transfers between devices with their start and end apart: 6, of which 5 were waited for; matrix products, arithmetic and copies ran while one was open for 0% of the time, Pallas kernels for 1%

profile of v2, /device:TPU:4, one launch (start us, length us, event | category | flops | bytes accessed | tf_op | source)
XLA Modules:
  0.0 255.7 jit_solution(12190649715438176148)
XLA Ops:
  1.9 1.3 copy-done.7
  3.2 1.3 copy-done.8
  6.3 3.5 %shard_map.140 = bf16[16,768,128]{2,1,0:T(8,128)(2,1)S(1)} custom-call(bf16[512,768]{1,0:T(8,128)(2,1)S(1)} %bitcast.12, s32[16,32]{1,0:T(8,128)S(1)} %copy-done.13, bf16[768,768]{1,0:T(8,128)(2,1)S(1)} %copy-done.6, bf16[768,768]{1,0:T(8,128)(2,1)S(1)} %copy-done.7, bf16[768,768]{1,0:T(8,128)(2,1)S(1)} %copy-done.8), custom_call_target="tpu_custom_call" | custom-call | flops 1811939328 | bytes 8000000 | tf_op jit(solution)/shard_map/pallas_call | solution.py:98
  9.8 85.8 %all_to_all.30.qk_ref.v_ref = bf16[16,768,128]{2,1,0:T(8,128)(2,1)S(1)} all-to-all(bf16[16,768,128]{2,1,0:T(8,128)(2,1)S(1)} %shard_map.140), channel_id=1, replica_groups=mesh['depth'=16,'cols'=16] {'cols'}, dimensions={0} | all-to-all | bytes 6291456 | tf_op jit(solution)/shard_map/all_to_all | solution.py:402
  97.4 5.1 %all-to-all-start.1 = ((f32[16,32,512]{2,1,0:T(8,128)}), f32[16,32,512]{2,1,0:T(8,128)}, u32[]{:S(2)}, u32[]{:S(2)}) async-start(f32[16,32,512]{2,1,0:T(8,128)} %bitcast.9), calls=%async_computation.1 | async-start | bytes 2097152 | tf_op jit(solution)/shard_map/all_to_all | solution.py:402
  104.9 1.9 copy-done.2
  107.7 8.1 %all-to-all-done.1.in_ref = f32[16,32,512]{2,1,0:T(8,128)} async-done(((f32[16,32,512]{2,1,0:T(8,128)}), f32[16,32,512]{2,1,0:T(8,128)}, u32[]{:S(2)}, u32[]{:S(2)}) %all-to-all-start.1) | async-done | bytes 1048608 | tf_op jit(solution)/shard_map/all_to_all | solution.py:402
  117.1 1.5 shard_map.143
  118.5 23.1 %all_to_all.31.p_ref.px_ref = bf16[16,32,1408]{2,1,0:T(8,128)(2,1)S(1)} all-to-all(bf16[16,32,1408]{2,1,0:T(8,128)(2,1)S(1)} %shard_map.143), channel_id=1, replica_groups=mesh['depth'=16,'cols'=16] {'depth'}, dimensions={0} | all-to-all | bytes 2883584 | tf_op jit(solution)/shard_map/all_to_all | solution.py:402
  143.8 8.5 %all-to-all-start.3 = ((bf16[256,16,128]{2,1,0:T(8,128)(2,1)}), bf16[256,16,128]{2,1,0:T(8,128)(2,1)S(1)}, u32[]{:S(2)}, u32[]{:S(2)}) async-start(bf16[256,16,128]{2,1,0:T(8,128)(2,1)} %bitcast.10), calls=%async_computation.3 | async-start | bytes 2097152 | tf_op jit(solution)/shard_map/all_to_all | solution.py:402
  152.3 30.4 %all-to-all-done.3 = bf16[256,16,128]{2,1,0:T(8,128)(2,1)S(1)} async-done(((bf16[256,16,128]{2,1,0:T(8,128)(2,1)}), bf16[256,16,128]{2,1,0:T(8,128)(2,1)S(1)}, u32[]{:S(2)}, u32[]{:S(2)}) %all-to-all-start.3) | async-done | bytes 1048608 | tf_op jit(solution)/shard_map/all_to_all | solution.py:402
  182.7 1.3 copy-done.15
  183.9 1.3 copy-done.16
  189.0 8.9 %shard_map.145 = (bf16[16,64,768]{2,1,0:T(8,128)(2,1)}, bf16[64,256]{1,0:T(8,128)(2,1)S(1)}) custom-call(bf16[4096,128]{1,0:T(8,128)(2,1)S(1)} %bitcast.11, bf16[16,32,1408]{2,1,0:T(8,128)(2,1)S(1)} %copy-done.1, bf16[768,768]{1,0:T(8,128)(2,1)S(1)} %copy-done.15, bf16[768,768]{1,0:T(8,128)(2,1)S(1)} %copy-done.16, bf16[768,768]{1,0:T(8,128)(2,1)S(1)} %copy-done.17, ...), custom_call_target="tpu_custom_call" | custom-call | flops 3019898880 | bytes 9000000 | tf_op jit(solution)/shard_map/pallas_call | solution.py:306
  197.9 5.5 %all-to-all-start.4 = ((bf16[16,64,768]{2,1,0:T(8,128)(2,1)}), bf16[16,64,768]{2,1,0:T(8,128)(2,1)S(1)}, u32[]{:S(2)}, u32[]{:S(2)}) async-start(bf16[16,64,768]{2,1,0:T(8,128)(2,1)} %get-tuple-element.7), calls=%async_computation.4 | async-start | bytes 3145728 | tf_op jit(solution)/shard_map/all_to_all | solution.py:402
  203.5 2.2 collective-permute-start
  205.7 7.1 %collective-permute-done = bf16[64,256]{1,0:T(8,128)(2,1)S(1)} collective-permute-done((bf16[64,256]{1,0:T(8,128)(2,1)S(1)}, bf16[64,256]{1,0:T(8,128)(2,1)S(1)}, u32[]{:S(2)}, u32[]{:S(2)}) %collective-permute-start) | collective-permute-done | bytes 32800 | tf_op jit(solution)/shard_map/ppermute | solution.py:407
  212.8 10.4 %all-to-all-done.4.in_ref.l_ref = bf16[16,64,768]{2,1,0:T(8,128)(2,1)S(1)} async-done(((bf16[16,64,768]{2,1,0:T(8,128)(2,1)}), bf16[16,64,768]{2,1,0:T(8,128)(2,1)S(1)}, u32[]{:S(2)}, u32[]{:S(2)}) %all-to-all-start.4) | async-done | bytes 1572896 | tf_op jit(solution)/shard_map/all_to_all | solution.py:402
  224.1 5.8 %all-to-all-start.5 = ((bf16[16,64,256]{2,1,0:T(8,128)(2,1)}), bf16[16,64,256]{2,1,0:T(8,128)(2,1)S(1)}, u32[]{:S(2)}, u32[]{:S(2)}) async-start(bf16[16,64,256]{2,1,0:T(8,128)(2,1)} %broadcast_in_dim.2), calls=%async_computation.5 | async-start | bytes 1048576 | tf_op jit(solution)/shard_map/all_to_all | solution.py:402
  230.0 6.1 %collective-permute-start.1 = (bf16[32,128]{1,0:T(8,128)(2,1)S(1)}, bf16[32,128]{1,0:T(8,128)(2,1)S(1)}, u32[]{:S(2)}, u32[]{:S(2)}) collective-permute-start(bf16[32,128]{1,0:T(8,128)(2,1)S(1)} %bitcast.18), channel_id=1, source_target_pairs={{0,0},{1,16},{2,32},{3,48},{4,64},{5,80},{6,96},{7,112},{8,128},{9... | collective-permute-start | bytes 24584 | tf_op jit(solution)/shard_map/ppermute | solution.py:407
  236.1 1.5 shard_map.146
  237.6 12.0 %all-to-all-done.5.r_ref = bf16[16,64,256]{2,1,0:T(8,128)(2,1)S(1)} async-done(((bf16[16,64,256]{2,1,0:T(8,128)(2,1)}), bf16[16,64,256]{2,1,0:T(8,128)(2,1)S(1)}, u32[]{:S(2)}, u32[]{:S(2)}) %all-to-all-start.5) | async-done | bytes 524320 | tf_op jit(solution)/shard_map/all_to_all | solution.py:402
  249.7 2.2 copy-done.3
  251.8 3.9 %shard_map.147 = bf16[1024,128]{1,0:T(8,128)(2,1)} custom-call(bf16[16,64,768]{2,1,0:T(8,128)(2,1)S(1)} %all-to-all-done.4.in_ref.l_ref, bf16[16,64,256]{2,1,0:T(8,128)(2,1)S(1)} %all-to-all-done.5.r_ref, bf16[32,128]{1,0:T(8,128)(2,1)S(1)} %collective-permute-done.1.n_ref, bf16[4096,512]{1,0:T(8,128)(2,1)S(1)} %copy-done.3), custom_call_target="tpu_custom_call" | custom-call | flops 1610612736 | bytes 6000000 | tf_op jit(solution)/shard_map/pallas_call | solution.py:379
  (47 shorter events, 16.2 us)
Async XLA Ops:
  0.6 1.3 copy-start.6
  1.9 1.3 copy-start.7
  3.2 1.3 copy-start.8
  97.4 5.1 %copy-start.14 = (s32[16,32]{1,0:T(8,128)S(1)}, s32[16,32]{1,0:T(8,128)}, u32[]{:S(2)}) copy-start(s32[16,32]{1,0:T(8,128)} %occ_ref.3) | copy-start | bytes 6148
  97.4 5.1 %copy-start.20 = (bf16[1024,128]{1,0:T(8,128)(2,1)S(1)}, bf16[1024,128]{1,0:T(8,128)(2,1)}, u32[]{:S(2)}) copy-start(bf16[1024,128]{1,0:T(8,128)(2,1)} %wp_ref.1) | copy-start | bytes 786436
  97.4 18.5 %all-to-all-start.1 = ((f32[16,32,512]{2,1,0:T(8,128)}), f32[16,32,512]{2,1,0:T(8,128)}, u32[]{:S(2)}, u32[]{:S(2)}) async-start(f32[16,32,512]{2,1,0:T(8,128)} %bitcast.9), calls=%async_computation.1 | async-start | bytes 2097152 | tf_op jit(solution)/shard_map/all_to_all | solution.py:402
  102.5 1.1 copy-start.12
  104.9 2.0 copy-start.2
  115.9 1.2 copy-start.10
  141.6 1.1 copy-start
  143.8 8.5 %copy-start.21 = (bf16[768,32]{0,1:T(8,128)(2,1)S(1)}, bf16[768,32]{0,1:T(8,128)(2,1)}, u32[]{:S(2)}) copy-start(bf16[768,32]{0,1:T(8,128)(2,1)} %param.24) | copy-start | bytes 147460
  143.8 8.5 %copy-start.22 = (bf16[768,32]{0,1:T(8,128)(2,1)S(1)}, bf16[768,32]{0,1:T(8,128)(2,1)}, u32[]{:S(2)}) copy-start(bf16[768,32]{0,1:T(8,128)(2,1)} %param.23) | copy-start | bytes 147460
  143.8 38.9 %copy-start.1 = (bf16[16,32,1408]{2,1,0:T(8,128)(2,1)S(1)}, bf16[16,32,1408]{2,1,0:T(8,128)(2,1)}, u32[]{:S(2)}) copy-start(bf16[16,32,1408]{2,1,0:T(8,128)(2,1)} %copy-done) | copy-start | bytes 4325380
  143.8 38.9 %all-to-all-start.3 = ((bf16[256,16,128]{2,1,0:T(8,128)(2,1)}), bf16[256,16,128]{2,1,0:T(8,128)(2,1)S(1)}, u32[]{:S(2)}, u32[]{:S(2)}) async-start(bf16[256,16,128]{2,1,0:T(8,128)(2,1)} %bitcast.10), calls=%async_computation.3 | async-start | bytes 2097152 | tf_op jit(solution)/shard_map/all_to_all | solution.py:402
  182.7 1.3 copy-start.15
  183.9 1.3 copy-start.16
  185.2 1.3 copy-start.17
  186.5 1.3 copy-start.18
  187.8 1.3 copy-start.19
  197.9 25.3 %all-to-all-start.4 = ((bf16[16,64,768]{2,1,0:T(8,128)(2,1)}), bf16[16,64,768]{2,1,0:T(8,128)(2,1)S(1)}, u32[]{:S(2)}, u32[]{:S(2)}) async-start(bf16[16,64,768]{2,1,0:T(8,128)(2,1)} %get-tuple-element.7), calls=%async_computation.4 | async-start | bytes 3145728 | tf_op jit(solution)/shard_map/all_to_all | solution.py:402
  203.5 9.4 %collective-permute-start = (bf16[64,256]{1,0:T(8,128)(2,1)S(1)}, bf16[64,256]{1,0:T(8,128)(2,1)S(1)}, u32[]{:S(2)}, u32[]{:S(2)}) collective-permute-start(bf16[64,256]{1,0:T(8,128)(2,1)S(1)} %get-tuple-element.8), channel_id=1, source_target_pairs={{0,0},{1,16},{2,32},{3,48},{4,64},{5,80},{6,96},{7,112},{8,128},{9... | collective-permute-start | bytes 98312 | tf_op jit(solution)/shard_map/ppermute | solution.py:407
  224.1 25.5 %all-to-all-start.5 = ((bf16[16,64,256]{2,1,0:T(8,128)(2,1)}), bf16[16,64,256]{2,1,0:T(8,128)(2,1)S(1)}, u32[]{:S(2)}, u32[]{:S(2)}) async-start(bf16[16,64,256]{2,1,0:T(8,128)(2,1)} %broadcast_in_dim.2), calls=%async_computation.5 | async-start | bytes 1048576 | tf_op jit(solution)/shard_map/all_to_all | solution.py:402
  230.0 19.7 %collective-permute-start.1 = (bf16[32,128]{1,0:T(8,128)(2,1)S(1)}, bf16[32,128]{1,0:T(8,128)(2,1)S(1)}, u32[]{:S(2)}, u32[]{:S(2)}) collective-permute-start(bf16[32,128]{1,0:T(8,128)(2,1)S(1)} %bitcast.18), channel_id=1, source_target_pairs={{0,0},{1,16},{2,32},{3,48},{4,64},{5,80},{6,96},{7,112},{8,128},{9... | collective-permute-start | bytes 24584 | tf_op jit(solution)/shard_map/ppermute | solution.py:407
  249.7 2.2 copy-start.3
  (5 other events, 4.7 us)

commit v3 on v2

--- a/solution.py
+++ b/solution.py
@@ -48,12 +48,15 @@
     return jnp.concatenate([a[:, 64:], b[:, 64:]], axis=1)
 
 
+HBM = pl.BlockSpec(memory_space=pltpu.HBM)
+
+
 def whole(n):
     return [pl.BlockSpec(memory_space=pltpu.VMEM)] * n
 
 
 def params(mib):
-    return pltpu.CompilerParams(vmem_limit_bytes=mib * 1024 * 1024)
+    return pltpu.CompilerParams(vmem_limit_bytes=int(mib * 1024 * 1024))
 
 
 def cost(flops, bytes_accessed, transcendentals=0):
@@ -72,73 +75,85 @@
     return jnp.broadcast_to(column, (ROWS, width))
 
 
-def row_proj_kernel(x_ref, occ_ref, wq_ref, wk_ref, wv_ref, out_ref, xn_ref, live_ref):
-    @pl.when(pl.program_id(0) == 0)
-    def _():
-        xn_ref[...] = norm(x_ref[...].astype(f32))
-        live_ref[...] = mask_rows(occ_ref[...], 128)
-
-    xn = xn_ref[...]
-    live = live_ref[...]
-    half = ROWS // 2
-    for index, w_ref in enumerate((wq_ref, wk_ref, wv_ref)):
-        y = mm(xn, w_ref[...])
-        for t in range(2):
-            part = y[:, 128 * t : 128 * t + 128]
-            if index < 2:
-                part = part * live
-            part = part.astype(bf16)
-            a, b = part[:half], part[half:]
-            out_ref[2 * t, 256 * index : 256 * index + 256] = lanes_lo(a, b)
-            out_ref[2 * t + 1, 256 * index : 256 * index + 256] = lanes_hi(a, b)
-
-
-def row_proj(x, occupancy, wq, wk, wv):
-    w = pl.BlockSpec((E, 256), lambda n: (0, n))
-    return pl.pallas_call(
-        row_proj_kernel,
-        grid=(3,),
-        in_specs=[
-            pl.BlockSpec((ROWS, E), lambda n: (0, 0)),
-            pl.BlockSpec((S, I), lambda n: (0, 0)),
-            w,
-            w,
-            w,
-        ],
-        out_specs=pl.BlockSpec((4, 768, 128), lambda n: (n, 0, 0)),
-        out_shape=jax.ShapeDtypeStruct((N, 768, 128), bf16),
-        scratch_shapes=[pltpu.VMEM((ROWS, E), bf16), pltpu.VMEM((ROWS, 128), f32)],
-        compiler_params=params(20),
-        cost_estimate=cost(3 * 2 * ROWS * E * E, 8_000_000),
-    )(x, occupancy, wq, wk, wv)
-
-
-def turn_kernel(x_ref, occ_ref, wp_ref, xr_ref, wk_ref):
+def row_proj_kernel(
+    x_hbm, occ_hbm, wq_hbm, wk_hbm, wv_hbm, out_hbm, xr_hbm,
+    xv, occ, wv, xn_ref, out, xr, sems,
+):
+    first = [pltpu.make_async_copy(occ_hbm, occ, sems.at[0])]
+    for k in range(4):
+        rows = pl.ds(128 * k, 128)
+        first.append(pltpu.make_async_copy(x_hbm.at[rows], xv.at[rows], sems.at[1 + k]))
+    for copy in first:
+        copy.start()
+    tiles = [
+        pltpu.make_async_copy(w, wv.at[k], sems.at[5 + k])
+        for k, w in enumerate((wq_hbm, wk_hbm, wv_hbm))
+    ]
+    first[0].wait()
+    live = mask_rows(occ[...], 128)
+    for k in range(4):
+        first[1 + k].wait()
+        if k == 0:
+            tiles[0].start()
+        rows = slice(128 * k, 128 * k + 128)
+        xn_ref[rows] = norm(xv[rows].astype(f32))
+    for copy in tiles[1:]:
+        copy.start()
     r = lax.broadcasted_iota(jnp.int32, (ROWS, ROWS), 0)
     o = lax.broadcasted_iota(jnp.int32, (ROWS, ROWS), 1)
     src = ((r & 15) << 5) + ((r >> 5) << 1) + ((r >> 4) & 1)
     perm = jnp.where(src == o, 1.0, 0.0).astype(bf16)
-    xr_ref[:, :E] = mm(perm, x_ref[...]).astype(bf16)
-    xr_ref[:, E:] = mm(perm, mask_rows(occ_ref[...], 128).astype(bf16)).astype(bf16)
-    wk_ref[...] = jnp.zeros_like(wk_ref)
-    for c in range(C):
-        w = wp_ref[C * c : C * c + C, :]
-        for j in range(4):
-            wk_ref[128 * c + 32 * j : 128 * c + 32 * j + 32, 128 * j : 128 * j + 128] = w
-
-
-def turn(x, occupancy, wp):
-    return pl.pallas_call(
-        turn_kernel,
-        in_specs=whole(3),
-        out_specs=whole(2),
+    xr[:, :E] = mm(perm, xv[...]).astype(bf16)
+    xr[:, E:] = mm(perm, live.astype(bf16)).astype(bf16)
+    sent = [pltpu.make_async_copy(xr, xr_hbm, sems.at[8])]
+    sent[0].start()
+    xn = xn_ref[...]
+    half = ROWS // 2
+    for index in range(3):
+        tiles[index].wait()
+        rows = slice(256 * index, 256 * index + 256)
+        for n in range(3):
+            y = mm(xn, wv[index, :, 256 * n : 256 * n + 256])
+            for t in range(2):
+                part = y[:, 128 * t : 128 * t + 128]
+                if index < 2:
+                    part = part * live
+                part = part.astype(bf16)
+                a, b = part[:half], part[half:]
+                out[4 * n + 2 * t, rows] = lanes_lo(a, b)
+                out[4 * n + 2 * t + 1, rows] = lanes_hi(a, b)
+        at = pl.ds(256 * index, 256)
+        sent.append(
+            pltpu.make_async_copy(
+                out.at[:, at], out_hbm.at[pl.ds(0, H), at], sems.at[9 + index]
+            )
+        )
+        sent[-1].start()
+    for copy in sent:
+        copy.wait()
+
+
+def row_proj(x, occupancy, wq, wk, wv):
+    return pl.pallas_call(
+        row_proj_kernel,
+        in_specs=[HBM] * 5,
+        out_specs=[HBM] * 2,
         out_shape=[
+            jax.ShapeDtypeStruct((N, 768, 128), bf16),
             jax.ShapeDtypeStruct((ROWS, XW), bf16),
-            jax.ShapeDtypeStruct((4096, 512), bf16),
-        ],
-        compiler_params=params(16),
-        cost_estimate=cost(2 * ROWS * ROWS * E, 8_000_000),
-    )(x, occupancy, wp)
+        ],
+        scratch_shapes=[
+            pltpu.VMEM((ROWS, E), bf16),
+            pltpu.VMEM((S, I), jnp.int32),
+            pltpu.VMEM((3, E, E), bf16),
+            pltpu.VMEM((ROWS, E), bf16),
+            pltpu.VMEM((H, 768, 128), bf16),
+            pltpu.VMEM((ROWS, XW), bf16),
+            pltpu.SemaphoreType.DMA((12,)),
+        ],
+        compiler_params=params(61),
+        cost_estimate=cost(3 * 2 * ROWS * E * E, 8_000_000),
+    )(x, occupancy, wq, wk, wv)
 
 
 def logits_kernel(qk_ref, out_ref):
@@ -166,7 +181,9 @@
     )(qkv)
 
 
-def softmax_kernel(in_ref, xr_ref, out_ref):
+def softmax_kernel(in_ref, xr_hbm, out_ref, sem):
+    copy = pltpu.make_async_copy(xr_hbm, out_ref.at[:, :, pl.ds(SITES, XW)], sem)
+    copy.start()
     total = in_ref[0]
     for k in range(1, N):
         total = total + in_ref[k]
@@ -175,15 +192,16 @@
     p = (e / jnp.sum(e, axis=-1, keepdims=True)).astype(bf16)
     for k in range(N):
         out_ref[k, :, :SITES] = p
-    out_ref[:, :, SITES:] = xr_ref[...].reshape(N, I, XW)
+    copy.wait()
 
 
 def row_softmax(parts, xr):
     return pl.pallas_call(
         softmax_kernel,
-        in_specs=whole(2),
+        in_specs=whole(1) + [HBM],
         out_specs=pl.BlockSpec(memory_space=pltpu.VMEM),
         out_shape=jax.ShapeDtypeStruct((N, I, SITES + XW), bf16),
+        scratch_shapes=[pltpu.SemaphoreType.DMA],
         compiler_params=params(16),
         cost_estimate=cost(N * I * SITES, 4_000_000, I * SITES),
     )(parts, xr)
@@ -228,10 +246,23 @@
 
 
 def column_kernel(
-    mr_ref, px_ref, wo_ref, cq_ref, ck_ref, cv_ref, co_ref, f_ref,
-    out_ref, r_ref,
-    ysc, xsc, qs, ks, vs, ms,
+    mr_ref, px_hbm, f1_ref, f2_ref, wo_hbm, cq_hbm, ck_hbm, cv_hbm, co_hbm,
+    out_hbm, r_ref,
+    ysc, xsc, qs, ks, vs, ms, weights, xb, ao, left, sems, out_sems,
 ):
+    copies = []
+    for k, w in enumerate((wo_hbm, cq_hbm, ck_hbm, cv_hbm, co_hbm)):
+        copies.append(pltpu.make_async_copy(w, weights.at[k], sems.at[k]))
+    fetch = pltpu.make_async_copy(px_hbm.at[:, :, pl.ds(SITES, XW)], xb, sems.at[5])
+    copies[0].start()
+    fetch.start()
+
+    def weight(k):
+        copies[k].wait()
+        for more in ((1, 2), (3,), (4,), (), ())[k]:
+            copies[more].start()
+        return weights[k]
+
     halves = []
     for pick in (lanes_lo, lanes_hi):
         halves.append(
@@ -244,8 +275,9 @@
             )
         )
     mixed = jnp.concatenate(halves, axis=0)
-    ysc[...] = mm(mixed, wo_ref[...]).reshape(2, N, 2, 8, E)
-    xsc[...] = px_ref[:, :, SITES:].astype(f32).reshape(N, 2, 2, 8, XW)
+    ysc[...] = mm(mixed, weight(0)).reshape(2, N, 2, 8, E)
+    fetch.wait()
+    xsc[...] = xb[...].astype(f32).reshape(N, 2, 2, 8, XW)
     blocks = []
     masks = []
     for i in range(2):
@@ -261,9 +293,9 @@
     alive = mmt(lane0, mask)
 
     normed = norm(wide)
-    qs[...] = mm(normed, cq_ref[...]).astype(bf16)
-    ks[...] = mm(normed, ck_ref[...]).astype(bf16)
-    vs[...] = mm(normed, cv_ref[...]).astype(bf16)
+    qs[...] = mm(normed, weight(1)).astype(bf16)
+    ks[...] = mm(normed, weight(2)).astype(bf16)
+    vs[...] = mm(normed, weight(3)).astype(bf16)
     low = lax.broadcasted_iota(jnp.int32, (SEQS, 128), 1) < 64
     for i in range(2):
         rows = slice(SEQS * i, SEQS * i + SEQS)
@@ -280,15 +312,18 @@
                 mixes.append(mm(p, v))
             ms[rows, lanes] = jnp.where(low, mixes[0], mixes[1]).astype(bf16)
 
-    out = (wide + mm(ms[...], co_ref[...])).astype(bf16)
+    out = (wide + mm(ms[...], weight(4))).astype(bf16)
     out_wide = out.astype(f32)
     for i in range(2):
         for s2 in range(2):
             at = SEQS * i + 128 * s2
             xsc[:, i, s2, :, :E] = out_wide[at : at + 128].reshape(N, 8, E)
-    out_ref[:, :I, :] = xsc[:, :, :, :, :E].reshape(N, I, E).astype(bf16)
-
-    factors = (mmt(f_ref[...], norm(out_wide)) * alive[0:1, :]).astype(bf16)
+    ao[...] = xsc[:, :, :, :, :E].reshape(N, I, E).astype(bf16)
+    sent = [pltpu.make_async_copy(ao, out_hbm.at[:, pl.ds(0, I)], out_sems.at[N])]
+    sent[0].start()
+
+    f = jnp.concatenate([f1_ref[...], f2_ref[...]], axis=0)
+    factors = (mmt(f, norm(out_wide)) * alive[0:1, :]).astype(bf16)
     for i in range(2):
         r_ref[C * i : C * i + C, :] = factors[C:, SEQS * i : SEQS * i + SEQS]
     counts = [
@@ -297,16 +332,19 @@
     ]
     row = lax.broadcasted_iota(jnp.int32, (C, SEQS), 0)
     count = jnp.where(row == 0, counts[0], counts[1]).astype(bf16)
-    left = jnp.concatenate([factors[:C, :], count], axis=1)
+    left[...] = jnp.concatenate([factors[:C, :], count], axis=1)
     for k in range(N):
-        out_ref[k, I:, :] = left
-
-
-def column_step(mr, px, wo, cq, ck, cv, co, f):
+        sent.append(pltpu.make_async_copy(left, out_hbm.at[k, pl.ds(I, C)], out_sems.at[k]))
+        sent[-1].start()
+    for copy in sent:
+        copy.wait()
+
+
+def column_step(mr, px, f1, f2, wo, cq, ck, cv, co):
     return pl.pallas_call(
         column_kernel,
-        in_specs=whole(8),
-        out_specs=whole(2),
+        in_specs=whole(1) + [HBM] + whole(2) + [HBM] * 5,
+        out_specs=[HBM, pl.BlockSpec(memory_space=pltpu.VMEM)],
         out_shape=[
             jax.ShapeDtypeStruct((N, 2 * I, E), bf16),
             jax.ShapeDtypeStruct((2 * C, SEQS), bf16),
@@ -318,10 +356,16 @@
             pltpu.VMEM((ROWS, E), bf16),
             pltpu.VMEM((ROWS, E), bf16),
             pltpu.VMEM((ROWS, E), bf16),
-        ],
-        compiler_params=params(40),
+            pltpu.VMEM((5, E, E), bf16),
+            pltpu.VMEM((N, I, XW), bf16),
+            pltpu.VMEM((N, I, E), bf16),
+            pltpu.VMEM((C, E), bf16),
+            pltpu.SemaphoreType.DMA((6,)),
+            pltpu.SemaphoreType.DMA((N + 1,)),
+        ],
+        compiler_params=params(59),
         cost_estimate=cost(5 * 2 * ROWS * E * E, 9_000_000, 2 * H * SEQS * SEQS),
-    )(mr, px, wo, cq, ck, cv, co, f)
+    )(mr, px, f1, f2, wo, cq, ck, cv, co)
 
 
 def back_kernel(in_ref, out_ref):
@@ -339,12 +383,20 @@
         in_specs=[pl.BlockSpec((N, I, E), lambda n: (0, 0, 0))],
         out_specs=pl.BlockSpec((ROWS, E), lambda n: (0, 0)),
         out_shape=jax.ShapeDtypeStruct((ROWS, E), bf16),
-        compiler_params=params(16),
+        compiler_params=params(24),
         cost_estimate=cost(2 * ROWS * ROWS * E, 2_000_000),
     )(both)
 
 
-def pair_kernel(l_ref, r_ref, n_ref, wk_ref, out_ref, l0, l1, l2, l3, l4, lp, lhs, osc):
+def pair_kernel(
+    l_ref, r_ref, n_ref, wp_ref, out_ref, l0, l1, l2, l3, l4, lp, lhs, osc, wk
+):
+    wk[...] = jnp.zeros_like(wk)
+    for c in range(C):
+        w = wp_ref[C * c : C * c + C, :]
+        for j in range(4):
+            at = 128 * c + C * j
+            wk[at : at + C, 128 * j : 128 * j + 128] = w
     every = l_ref[...].reshape(N * C, E).astype(f32)
     for k, ref in enumerate((l0, l1, l2, l3, l4)):
         ref[...] = every[:, 128 * k : 128 * k + 128]
@@ -365,7 +417,7 @@
                 lhs[C * j : C * j + C, 128 * (c + k) : 128 * (c + k) + 128] = outer[
                     C * k : C * k + C, 128 * j : 128 * j + 128
                 ]
-    acc = mm(lhs[...], wk_ref[...])
+    acc = mm(lhs[...], wk[...])
     right_count = n_ref[...].astype(f32)
     for j in range(C):
         part = acc[C * (j // 4) : C * (j // 4) + C, 128 * (j % 4) : 128 * (j % 4) + 128]
@@ -375,7 +427,7 @@
     out_ref[...] = osc[...].astype(bf16)
 
 
-def pair_step(both, right, counts, wk):
+def pair_step(both, right, counts, wp):
     return pl.pallas_call(
         pair_kernel,
         grid=(1,),
@@ -383,7 +435,7 @@
             pl.BlockSpec((N, I, E), lambda n: (0, 1, 0)),
             pl.BlockSpec((N, 2 * C, SEQS), lambda n: (0, 0, 0)),
             pl.BlockSpec((C, 128), lambda n: (0, 0)),
-            pl.BlockSpec((4096, 512), lambda n: (0, 0)),
+            pl.BlockSpec((C * C, PC), lambda n: (0, 0)),
         ],
         out_specs=pl.BlockSpec((C * C, PC), lambda n: (0, 0)),
         out_shape=jax.ShapeDtypeStruct((C * C, PC), bf16),
@@ -392,10 +444,11 @@
             pltpu.VMEM((1024, SEQS), bf16),
             pltpu.VMEM((256, 4096), bf16),
             pltpu.VMEM((1024, PC), f32),
+            pltpu.VMEM((4096, 512), bf16),
         ],
         compiler_params=params(24),
         cost_estimate=cost(2 * 1024 * 1024 * 256 + 2 * 256 * 4096 * 512, 6_000_000),
-    )(both, right, counts, wk)
+    )(both, right, counts, wp)
 
 
 def exchange(x, axis):
@@ -409,23 +462,22 @@
 
 def on_device(x, occupancy, wq, wk, wv, wo, cq, ck, cv, co, f1, f2, wp):
     x = x.reshape(ROWS, E)
-    factors = jnp.concatenate([f1.T, f2.T], axis=0)
-
-    qkv = exchange(row_proj(x, occupancy, wq, wk, wv), "cols")
-    xr, pair_w = turn(x, occupancy, wp)
+
+    qkv, xr = row_proj(x, occupancy, wq, wk, wv)
+    qkv = exchange(qkv, "cols")
     parts = exchange(partial_logits(qkv).reshape(N, I, SITES), "depth")
-    px = exchange(row_softmax(parts, xr), "depth")
+    px = exchange(row_softmax(parts, xr.reshape(N, I, XW)), "depth")
     mix = row_mix(px, qkv)
     mr = exchange(mix.reshape(N * N, 16, 128), ("cols", "depth")).reshape(4096, 128)
 
-    both, right = column_step(mr, px, wo, cq, ck, cv, co, factors)
+    both, right = column_step(mr, px, f1.T, f2.T, wo, cq, ck, cv, co)
     right = swap(right)
     both = exchange(both, "depth")
     counts = swap(both[:, I : I + 2, 512:640].reshape(C, 128))
     right = exchange(jnp.broadcast_to(right[None], (N, 2 * C, SEQS)), "cols")
-    out = back(both).reshape(S, I, E)
-    pair = pair_step(both, right, counts, pair_w).reshape(C, C, PC)
-    return out, pair
+    out = back(both)
+    pair = pair_step(both, right, counts, wp)
+    return out.reshape(S, I, E), pair.reshape(C, C, PC)
 
 
 def solution(mesh):

time: 257 us -> 247 us (0.961)
  blocking collectives: 109 us -> 166 us
  waiting for transfers between devices: 68.1 us -> 29.4 us
  local copies, waits for them, and re-layouts: 22.3 us -> 0.91 us
  starting transfers between devices: 33.3 us -> 19.9 us
  Pallas kernels: 22.3 us -> 28.3 us
    all_to_all x2 -> x4, blocking collectives: 109 us -> 166 us  [exchange(): return lax.all_to_all(x, axis, split_axis=0, concat_axis=0, tiled=True)]
    all_to_all x4 -> x2, waiting for transfers between devices: 61 us -> 22.3 us  [exchange(): return lax.all_to_all(x, axis, split_axis=0, concat_axis=0, tiled=True)]
    unnamed x46 -> x8, local copies, waits for them, and re-layouts: 21.4 us -> 0.06 us
    all_to_all x4 -> x2, starting transfers between devices: 24.9 us -> 11.4 us  [exchange(): return lax.all_to_all(x, axis, split_axis=0, concat_axis=0, tiled=True)]
    pallas_call x4 -> x3, Pallas kernels: 15.1 us -> 20.9 us  [the longest x1 13.9 us: column_step(): pl.pallas_call(column_kernel, in_specs=whole(1) + [HBM] + whole(2) + [HBM...]
  transfers between devices with their start and end apart: 6 -> 4, of which waited for: 5 -> 3; matrix products, arithmetic and copies ran while one was open for 0% -> 0% of each run, Pallas kernels for 1% -> 1%
where the time goes in v3:
time: 247 us; the launch traced here: 246 us
  blocking collectives  166 us (67%)
  waiting for transfers between devices  29.4 us (12%)
  Pallas kernels  28.3 us (11%)
  starting transfers between devices  19.9 us (8%)
    all_to_all x4, blocking collectives, exchange(): return lax.all_to_all(x, axis, split_axis=0, concat_axis=0, tiled=True)  166 us
    all_to_all x2, waiting for transfers between devices, exchange(): return lax.all_to_all(x, axis, split_axis=0, concat_axis=0, tiled=True)  22.3 us
    pallas_call x1, Pallas kernels, column_step(): pl.pallas_call(column_kernel, in_specs=whole(1) + [HBM] + whole(2) + [HBM...  13.9 us
    all_to_all x2, starting transfers between devices, exchange(): return lax.all_to_all(x, axis, split_axis=0, concat_axis=0, tiled=True)  11.4 us
    ppermute x2, starting transfers between devices, swap(): return lax.ppermute(x, ('depth', 'cols'), pairs)  8.52 us
    ppermute x2, waiting for transfers between devices, swap(): return lax.ppermute(x, ('depth', 'cols'), pairs)  7.14 us
    pallas_call x1, Pallas kernels, row_proj(): pl.pallas_call(row_proj_kernel, in_specs=[HBM] * 5, out_specs=[HBM] * 2,...  6.74 us
  transfers between devices with their start and end apart: 4, of which 3 were waited for; matrix products, arithmetic and copies ran while one was open for 0% of the time, Pallas kernels for 1%

profile of v3, /device:TPU:4, one launch (start us, length us, event | category | flops | bytes accessed | tf_op | source)
XLA Modules:
  0.0 245.7 jit_solution(6066630092713381314)
XLA Ops:
  0.6 6.7 %shard_map.140 = (bf16[16,768,128]{2,1,0:T(8,128)(2,1)}, bf16[512,896]{1,0:T(8,128)(2,1)}) custom-call(bf16[512,768]{1,0:T(8,128)(2,1)} %bitcast.16, s32[16,32]{1,0:T(8,128)} %occ_hbm.1, bf16[768,768]{1,0:T(8,128)(2,1)} %wq_hbm.1, bf16[768,768]{1,0:T(8,128)(2,1)} %wk_hbm.1, bf16[768,768]{1,0:T(8,128)(2,1)} %wv_hbm.1), custom_call_target="tpu_custom_call" | custom-call | flops 1811939328 | bytes 8000000 | tf_op jit(solution)/shard_map/pallas_call | solution.py:137
  7.4 86.1 %all_to_all.30.qk_ref.v_ref = bf16[16,768,128]{2,1,0:T(8,128)(2,1)S(1)} all-to-all(bf16[16,768,128]{2,1,0:T(8,128)(2,1)} %get-tuple-element.6), channel_id=1, replica_groups=mesh['depth'=16,'cols'=16] {'cols'}, dimensions={0} | all-to-all | bytes 6291456 | tf_op jit(solution)/shard_map/all_to_all | solution.py:455
  93.4 0.8 shard_map.141
  94.2 0.0 copy-start.1
  94.3 18.0 %all_to_all.31.in_ref = f32[16,32,512]{2,1,0:T(8,128)S(1)} all-to-all(f32[16,32,512]{2,1,0:T(8,128)S(1)} %bitcast.11), channel_id=1, replica_groups=mesh['depth'=16,'cols'=16] {'depth'}, dimensions={0} | all-to-all | bytes 2097152 | tf_op jit(solution)/shard_map/all_to_all | solution.py:455
  112.2 0.3 shard_map.142
  112.6 23.3 %all_to_all.32.p_ref.px_hbm = bf16[16,32,1408]{2,1,0:T(8,128)(2,1)S(1)} all-to-all(bf16[16,32,1408]{2,1,0:T(8,128)(2,1)S(1)} %shard_map.142), channel_id=1, replica_groups=mesh['depth'=16,'cols'=16] {'depth'}, dimensions={0} | all-to-all | bytes 2883584 | tf_op jit(solution)/shard_map/all_to_all | solution.py:455
  135.8 1.1 shard_map.143
  136.9 0.0 copy-done
  137.0 39.1 %all_to_all.33 = bf16[256,16,128]{2,1,0:T(8,128)(2,1)} all-to-all(bf16[256,16,128]{2,1,0:T(8,128)(2,1)S(1)} %bitcast.10), channel_id=1, replica_groups=mesh['depth'=16,'cols'=16] {'cols','depth'}, dimensions={0} | all-to-all | bytes 2097152 | tf_op jit(solution)/shard_map/all_to_all | solution.py:455
  176.1 13.9 %shard_map.144 = (bf16[16,64,768]{2,1,0:T(8,128)(2,1)}, bf16[64,256]{1,0:T(8,128)(2,1)}) custom-call(bf16[4096,128]{1,0:T(8,128)(2,1)} %bitcast.13, bf16[16,32,1408]{2,1,0:T(8,128)(2,1)} %copy-done, bf16[32,768]{1,0:T(8,128)(2,1)} %bitcast.17, bf16[32,768]{1,0:T(8,128)(2,1)} %bitcast.18, bf16[768,768]{1,0:T(8,128)(2,1)} %wo_hbm.1, bf16[768,768]{1,0:T(8,128)(2,1)} %cq_hbm.1, ...), custom_call_target="tpu_custom_call" | custom-call | flops 3019898880 | bytes 9000000 | tf_op jit(solution)/shard_map/pallas_call | solution.py:344
  189.9 0.0 copy-start.3
  190.0 5.5 %all-to-all-start.4 = ((bf16[16,64,768]{2,1,0:T(8,128)(2,1)}), bf16[16,64,768]{2,1,0:T(8,128)(2,1)S(1)}, u32[]{:S(2)}, u32[]{:S(2)}) async-start(bf16[16,64,768]{2,1,0:T(8,128)(2,1)} %get-tuple-element.8), calls=%async_computation.4 | async-start | bytes 3145728 | tf_op jit(solution)/shard_map/all_to_all | solution.py:455
  195.5 2.2 collective-permute-start
  197.8 7.1 %collective-permute-done = bf16[64,256]{1,0:T(8,128)(2,1)S(1)} collective-permute-done((bf16[64,256]{1,0:T(8,128)(2,1)S(1)}, bf16[64,256]{1,0:T(8,128)(2,1)S(1)}, u32[]{:S(2)}, u32[]{:S(2)}) %collective-permute-start) | collective-permute-done | bytes 32800 | tf_op jit(solution)/shard_map/ppermute | solution.py:460
  204.9 10.4 %all-to-all-done.4.in_ref.l_ref = bf16[16,64,768]{2,1,0:T(8,128)(2,1)S(1)} async-done(((bf16[16,64,768]{2,1,0:T(8,128)(2,1)}), bf16[16,64,768]{2,1,0:T(8,128)(2,1)S(1)}, u32[]{:S(2)}, u32[]{:S(2)}) %all-to-all-start.4) | async-done | bytes 1572896 | tf_op jit(solution)/shard_map/all_to_all | solution.py:455
  215.3 0.8 broadcast_in_dim.2
  216.1 5.8 %all-to-all-start.5 = ((bf16[16,64,256]{2,1,0:T(8,128)(2,1)}), bf16[16,64,256]{2,1,0:T(8,128)(2,1)S(1)}, u32[]{:S(2)}, u32[]{:S(2)}) async-start(bf16[16,64,256]{2,1,0:T(8,128)(2,1)} %broadcast_in_dim.2), calls=%async_computation.5 | async-start | bytes 1048576 | tf_op jit(solution)/shard_map/all_to_all | solution.py:455
  222.0 0.0 copy-start.2
  222.0 6.3 %collective-permute-start.1 = (bf16[32,128]{1,0:T(8,128)(2,1)S(1)}, bf16[32,128]{1,0:T(8,128)(2,1)S(1)}, u32[]{:S(2)}, u32[]{:S(2)}) collective-permute-start(bf16[32,128]{1,0:T(8,128)(2,1)S(1)} %bitcast.15), channel_id=1, source_target_pairs={{0,0},{1,16},{2,32},{3,48},{4,64},{5,80},{6,96},{7,112},{8,128},{9... | collective-permute-start | bytes 24584 | tf_op jit(solution)/shard_map/ppermute | solution.py:460
  228.3 1.5 shard_map.145
  229.8 11.9 %all-to-all-done.5.r_ref = bf16[16,64,256]{2,1,0:T(8,128)(2,1)S(1)} async-done(((bf16[16,64,256]{2,1,0:T(8,128)(2,1)}), bf16[16,64,256]{2,1,0:T(8,128)(2,1)S(1)}, u32[]{:S(2)}, u32[]{:S(2)}) %all-to-all-start.5) | async-done | bytes 524320 | tf_op jit(solution)/shard_map/all_to_all | solution.py:455
  241.7 0.0 collective-permute-done.1.n_ref
  241.7 4.0 %shard_map.146 = bf16[1024,128]{1,0:T(8,128)(2,1)} custom-call(bf16[16,64,768]{2,1,0:T(8,128)(2,1)S(1)} %all-to-all-done.4.in_ref.l_ref, bf16[16,64,256]{2,1,0:T(8,128)(2,1)S(1)} %all-to-all-done.5.r_ref, bf16[32,128]{1,0:T(8,128)(2,1)S(1)} %collective-permute-done.1.n_ref, bf16[1024,128]{1,0:T(8,128)(2,1)S(1)} %copy-done.2), custom_call_target="tpu_custom_call" | custom-call | flops 1610612736 | bytes 6000000 | tf_op jit(solution)/shard_map/pallas_call | solution.py:431
  (5 shorter events, 0.0 us)
Async XLA Ops:
  94.2 18.0 %copy-start.1 = (bf16[512,896]{1,0:T(8,128)(2,1)S(1)}, bf16[512,896]{1,0:T(8,128)(2,1)}, u32[]{:S(2)}) copy-start(bf16[512,896]{1,0:T(8,128)(2,1)} %get-tuple-element.7) | copy-start | bytes 2752516
  135.8 1.1 copy-start
  189.9 5.6 %copy-start.3 = (bf16[64,256]{1,0:T(8,128)(2,1)S(1)}, bf16[64,256]{1,0:T(8,128)(2,1)}, u32[]{:S(2)}) copy-start(bf16[64,256]{1,0:T(8,128)(2,1)} %get-tuple-element.9) | copy-start | bytes 98308
  190.0 25.3 %all-to-all-start.4 = ((bf16[16,64,768]{2,1,0:T(8,128)(2,1)}), bf16[16,64,768]{2,1,0:T(8,128)(2,1)S(1)}, u32[]{:S(2)}, u32[]{:S(2)}) async-start(bf16[16,64,768]{2,1,0:T(8,128)(2,1)} %get-tuple-element.8), calls=%async_computation.4 | async-start | bytes 3145728 | tf_op jit(solution)/shard_map/all_to_all | solution.py:455
  195.5 9.4 %collective-permute-start = (bf16[64,256]{1,0:T(8,128)(2,1)S(1)}, bf16[64,256]{1,0:T(8,128)(2,1)S(1)}, u32[]{:S(2)}, u32[]{:S(2)}) collective-permute-start(bf16[64,256]{1,0:T(8,128)(2,1)S(1)} %copy-done.3), channel_id=1, source_target_pairs={{0,0},{1,16},{2,32},{3,48},{4,64},{5,80},{6,96},{7,112},{8,128},{9... | collective-permute-start | bytes 98312 | tf_op jit(solution)/shard_map/ppermute | solution.py:460
  216.1 25.5 %all-to-all-start.5 = ((bf16[16,64,256]{2,1,0:T(8,128)(2,1)}), bf16[16,64,256]{2,1,0:T(8,128)(2,1)S(1)}, u32[]{:S(2)}, u32[]{:S(2)}) async-start(bf16[16,64,256]{2,1,0:T(8,128)(2,1)} %broadcast_in_dim.2), calls=%async_computation.5 | async-start | bytes 1048576 | tf_op jit(solution)/shard_map/all_to_all | solution.py:455
  222.0 19.7 %copy-start.2 = (bf16[1024,128]{1,0:T(8,128)(2,1)S(1)}, bf16[1024,128]{1,0:T(8,128)(2,1)}, u32[]{:S(2)}) copy-start(bf16[1024,128]{1,0:T(8,128)(2,1)} %wp_ref.1) | copy-start | bytes 786436
  222.0 19.7 %collective-permute-start.1 = (bf16[32,128]{1,0:T(8,128)(2,1)S(1)}, bf16[32,128]{1,0:T(8,128)(2,1)S(1)}, u32[]{:S(2)}, u32[]{:S(2)}) collective-permute-start(bf16[32,128]{1,0:T(8,128)(2,1)S(1)} %bitcast.15), channel_id=1, source_target_pairs={{0,0},{1,16},{2,32},{3,48},{4,64},{5,80},{6,96},{7,112},{8,128},{9... | collective-permute-start | bytes 24584 | tf_op jit(solution)/shard_map/ppermute | solution.py:460

commit v4 on v3

--- a/solution.py
+++ b/solution.py
@@ -22,6 +22,7 @@
 C = 32
 PC = 128
 XW = E + 128
+PARTS = 2
 
 NT = (((1,), (1,)), ((), ()))
 
@@ -76,8 +77,8 @@
 
 
 def row_proj_kernel(
-    x_hbm, occ_hbm, wq_hbm, wk_hbm, wv_hbm, out_hbm, xr_hbm,
-    xv, occ, wv, xn_ref, out, xr, sems,
+    x_hbm, occ_hbm, wq_hbm, wk_hbm, wv_hbm, out_hbm,
+    xv, occ, wv, xn_ref, out, sems,
 ):
     first = [pltpu.make_async_copy(occ_hbm, occ, sems.at[0])]
     for k in range(4):
@@ -99,14 +100,7 @@
         xn_ref[rows] = norm(xv[rows].astype(f32))
     for copy in tiles[1:]:
         copy.start()
-    r = lax.broadcasted_iota(jnp.int32, (ROWS, ROWS), 0)
-    o = lax.broadcasted_iota(jnp.int32, (ROWS, ROWS), 1)
-    src = ((r & 15) << 5) + ((r >> 5) << 1) + ((r >> 4) & 1)
-    perm = jnp.where(src == o, 1.0, 0.0).astype(bf16)
-    xr[:, :E] = mm(perm, xv[...]).astype(bf16)
-    xr[:, E:] = mm(perm, live.astype(bf16)).astype(bf16)
-    sent = [pltpu.make_async_copy(xr, xr_hbm, sems.at[8])]
-    sent[0].start()
+    sent = []
     xn = xn_ref[...]
     half = ROWS // 2
     for index in range(3):
@@ -137,23 +131,43 @@
     return pl.pallas_call(
         row_proj_kernel,
         in_specs=[HBM] * 5,
-        out_specs=[HBM] * 2,
-        out_shape=[
-            jax.ShapeDtypeStruct((N, 768, 128), bf16),
-            jax.ShapeDtypeStruct((ROWS, XW), bf16),
-        ],
+        out_specs=HBM,
+        out_shape=jax.ShapeDtypeStruct((N, 768, 128), bf16),
         scratch_shapes=[
             pltpu.VMEM((ROWS, E), bf16),
             pltpu.VMEM((S, I), jnp.int32),
             pltpu.VMEM((3, E, E), bf16),
             pltpu.VMEM((ROWS, E), bf16),
             pltpu.VMEM((H, 768, 128), bf16),
-            pltpu.VMEM((ROWS, XW), bf16),
             pltpu.SemaphoreType.DMA((12,)),
         ],
         compiler_params=params(61),
         cost_estimate=cost(3 * 2 * ROWS * E * E, 8_000_000),
     )(x, occupancy, wq, wk, wv)
+
+
+def turn_kernel(me_ref, x_ref, occ_ref, *out_refs):
+    r = lax.broadcasted_iota(jnp.int32, (ROWS, ROWS), 0)
+    o = lax.broadcasted_iota(jnp.int32, (ROWS, ROWS), 1)
+    d = jnp.bitwise_xor(r >> 5, me_ref[0])
+    src = ((r & 15) << 5) + (d << 1) + ((r >> 4) & 1)
+    perm = jnp.where(src == o, 1.0, 0.0).astype(bf16)
+    x = mm(perm, x_ref[...]).astype(bf16)
+    mask = mm(perm, mask_rows(occ_ref[...], 128).astype(bf16)).astype(bf16)
+    for k in range(N):
+        out_refs[k][:, :E] = x[I * k : I * k + I]
+        out_refs[k][:, E:] = mask[I * k : I * k + I]
+
+
+def turn(me, x, occupancy):
+    return pl.pallas_call(
+        turn_kernel,
+        in_specs=[pl.BlockSpec(memory_space=pltpu.SMEM)] + whole(2),
+        out_specs=whole(N),
+        out_shape=[jax.ShapeDtypeStruct((I, XW), bf16)] * N,
+        compiler_params=params(16),
+        cost_estimate=cost(2 * ROWS * ROWS * E, 3_000_000),
+    )(me, x, occupancy)
 
 
 def logits_kernel(qk_ref, out_ref):
@@ -181,9 +195,7 @@
     )(qkv)
 
 
-def softmax_kernel(in_ref, xr_hbm, out_ref, sem):
-    copy = pltpu.make_async_copy(xr_hbm, out_ref.at[:, :, pl.ds(SITES, XW)], sem)
-    copy.start()
+def softmax_kernel(in_ref, out_ref):
     total = in_ref[0]
     for k in range(1, N):
         total = total + in_ref[k]
@@ -191,20 +203,18 @@
     e = jnp.exp(total - top)
     p = (e / jnp.sum(e, axis=-1, keepdims=True)).astype(bf16)
     for k in range(N):
-        out_ref[k, :, :SITES] = p
-    copy.wait()
-
-
-def row_softmax(parts, xr):
+        out_ref[k] = p
+
+
+def row_softmax(parts):
     return pl.pallas_call(
         softmax_kernel,
-        in_specs=whole(1) + [HBM],
+        in_specs=whole(1),
         out_specs=pl.BlockSpec(memory_space=pltpu.VMEM),
-        out_shape=jax.ShapeDtypeStruct((N, I, SITES + XW), bf16),
-        scratch_shapes=[pltpu.SemaphoreType.DMA],
+        out_shape=jax.ShapeDtypeStruct((N, I, SITES), bf16),
         compiler_params=params(16),
         cost_estimate=cost(N * I * SITES, 4_000_000, I * SITES),
-    )(parts, xr)
+    )(parts)
 
 
 def row_mix_kernel(p_ref, v_ref, out_ref):
@@ -230,7 +240,7 @@
         out_ref[256 * b + 256 : 256 * b + 512, :] = turned[:, 128:]
 
 
-def row_mix(px, qkv):
+def row_mix(p, qkv):
     return pl.pallas_call(
         row_mix_kernel,
         grid=(1,),
@@ -242,25 +252,34 @@
         out_shape=jax.ShapeDtypeStruct((4096, 128), bf16),
         compiler_params=params(20),
         cost_estimate=cost(2 * SITES * SITES * 1024, 3_000_000),
-    )(px, qkv)
+    )(p, qkv)
 
 
 def column_kernel(
-    mr_ref, px_hbm, f1_ref, f2_ref, wo_hbm, cq_hbm, ck_hbm, cv_hbm, co_hbm,
-    out_hbm, r_ref,
-    ysc, xsc, qs, ks, vs, ms, weights, xb, ao, left, sems, out_sems,
+    me_ref, mr_ref, f1_ref, f2_ref, wo_hbm, cq_hbm, ck_hbm, cv_hbm, co_hbm, *refs
 ):
+    x_hbm, refs = refs[:N], refs[N:]
+    out_hbm, r_ref, ysc, xsc, qs, ks, vs, ms, weights, xb, ao, left, sems, out_sems = refs
     copies = []
     for k, w in enumerate((wo_hbm, cq_hbm, ck_hbm, cv_hbm, co_hbm)):
-        copies.append(pltpu.make_async_copy(w, weights.at[k], sems.at[k]))
-    fetch = pltpu.make_async_copy(px_hbm.at[:, :, pl.ds(SITES, XW)], xb, sems.at[5])
-    copies[0].start()
-    fetch.start()
+        for part in range(PARTS):
+            rows = pl.ds(E // PARTS * part, E // PARTS)
+            copies.append(
+                pltpu.make_async_copy(w.at[rows], weights.at[k, rows], sems.at[PARTS * k + part])
+            )
+    fetch = []
+    for k in range(N):
+        fetch.append(
+            pltpu.make_async_copy(
+                x_hbm[k], xb.at[jnp.bitwise_xor(me_ref[0], k)], sems.at[5 * PARTS + k]
+            )
+        )
+    for copy in copies[:PARTS] + fetch + copies[PARTS:]:
+        copy.start()
 
     def weight(k):
-        copies[k].wait()
-        for more in ((1, 2), (3,), (4,), (), ())[k]:
-            copies[more].start()
+        for copy in copies[PARTS * k : PARTS * k + PARTS]:
+            copy.wait()
         return weights[k]
 
     halves = []
@@ -276,7 +295,8 @@
         )
     mixed = jnp.concatenate(halves, axis=0)
     ysc[...] = mm(mixed, weight(0)).reshape(2, N, 2, 8, E)
-    fetch.wait()
+    for copy in fetch:
+        copy.wait()
     xsc[...] = xb[...].astype(f32).reshape(N, 2, 2, 8, XW)
     blocks = []
     masks = []
@@ -340,10 +360,10 @@
         copy.wait()
 
 
-def column_step(mr, px, f1, f2, wo, cq, ck, cv, co):
+def column_step(me, mr, f1, f2, wo, cq, ck, cv, co, xs):
     return pl.pallas_call(
         column_kernel,
-        in_specs=whole(1) + [HBM] + whole(2) + [HBM] * 5,
+        in_specs=[pl.BlockSpec(memory_space=pltpu.SMEM)] + whole(3) + [HBM] * (5 + N),
         out_specs=[HBM, pl.BlockSpec(memory_space=pltpu.VMEM)],
         out_shape=[
             jax.ShapeDtypeStruct((N, 2 * I, E), bf16),
@@ -360,12 +380,12 @@
             pltpu.VMEM((N, I, XW), bf16),
             pltpu.VMEM((N, I, E), bf16),
             pltpu.VMEM((C, E), bf16),
-            pltpu.SemaphoreType.DMA((6,)),
+            pltpu.SemaphoreType.DMA((5 * PARTS + N,)),
             pltpu.SemaphoreType.DMA((N + 1,)),
         ],
         compiler_params=params(59),
         cost_estimate=cost(5 * 2 * ROWS * E * E, 9_000_000, 2 * H * SEQS * SEQS),
-    )(mr, px, f1, f2, wo, cq, ck, cv, co)
+    )(me, mr, f1, f2, wo, cq, ck, cv, co, *xs)
 
 
 def back_kernel(in_ref, out_ref):
@@ -463,14 +483,22 @@
 def on_device(x, occupancy, wq, wk, wv, wo, cq, ck, cv, co, f1, f2, wp):
     x = x.reshape(ROWS, E)
 
-    qkv, xr = row_proj(x, occupancy, wq, wk, wv)
-    qkv = exchange(qkv, "cols")
+    me = lax.axis_index("depth").astype(jnp.int32).reshape(1)
+
+    sent = row_proj(x, occupancy, wq, wk, wv)
+    qkv = exchange(sent, "cols")
+    later, _ = lax.optimization_barrier((x, sent))
+    xs = list(turn(me, later, occupancy))
+    for k in range(1, N):
+        xs[k] = lax.ppermute(xs[k], "depth", [(d, d ^ k) for d in range(N)])
+    qkv, xs = lax.optimization_barrier((qkv, xs))
+
     parts = exchange(partial_logits(qkv).reshape(N, I, SITES), "depth")
-    px = exchange(row_softmax(parts, xr.reshape(N, I, XW)), "depth")
-    mix = row_mix(px, qkv)
+    p = exchange(row_softmax(parts), "depth")
+    mix = row_mix(p, qkv)
     mr = exchange(mix.reshape(N * N, 16, 128), ("cols", "depth")).reshape(4096, 128)
 
-    both, right = column_step(mr, px, f1.T, f2.T, wo, cq, ck, cv, co)
+    both, right = column_step(me, mr, f1.T, f2.T, wo, cq, ck, cv, co, xs)
     right = swap(right)
     both = exchange(both, "depth")
     counts = swap(both[:, I : I + 2, 512:640].reshape(C, 128))

time: 247 us -> 237 us (0.960)
  blocking collectives: 166 us -> 70.6 us
  waiting for transfers between devices: 29.4 us -> 83.2 us
  starting transfers between devices: 19.9 us -> 48.8 us
    all_to_all x4 -> x3, blocking collectives: 166 us -> 70.6 us  [exchange(): return lax.all_to_all(x, axis, split_axis=0, concat_axis=0, tiled=True)]
    all_to_all x2 -> x3, waiting for transfers between devices: 22.3 us -> 71 us  [exchange(): return lax.all_to_all(x, axis, split_axis=0, concat_axis=0, tiled=True)]
    ppermute x0 -> x15, starting transfers between devices: none -> 17.5 us  [on_device(): xs[k] = lax.ppermute(xs[k], 'depth', [(d, d ^ k) for d in range(N)])]
    all_to_all x2 -> x3, starting transfers between devices: 11.4 us -> 22.6 us  [exchange(): return lax.all_to_all(x, axis, split_axis=0, concat_axis=0, tiled=True)]
    ppermute x0 -> x15, waiting for transfers between devices: none -> 5.12 us  [on_device(): xs[k] = lax.ppermute(xs[k], 'depth', [(d, d ^ k) for d in range(N)])]
    pallas_call x3 -> x4, Pallas kernels: 20.9 us -> 21.6 us  [the longest x1 14.1 us: column_step(): pl.pallas_call(column_kernel, in_specs=[pl.BlockSpec(memory_space=pltpu.S...]
  transfers between devices with their start and end apart: 4 -> 20, of which waited for: 3 -> 9; matrix products, arithmetic and copies ran while one was open for 0% -> 0% of each run, Pallas kernels for 1% -> 1%
where the time goes in v4:
time: 237 us; the launch traced here: 236 us
  waiting for transfers between devices  83.2 us (35%)
  blocking collectives  70.6 us (30%)
  starting transfers between devices  48.8 us (21%)
  Pallas kernels  29 us (12%)
  local copies, waits for them, and re-layouts  3.27 us (1%)
    all_to_all x3, waiting for transfers between devices, exchange(): return lax.all_to_all(x, axis, split_axis=0, concat_axis=0, tiled=True)  71 us
    all_to_all x3, blocking collectives, exchange(): return lax.all_to_all(x, axis, split_axis=0, concat_axis=0, tiled=True)  70.6 us
    all_to_all x3, starting transfers between devices, exchange(): return lax.all_to_all(x, axis, split_axis=0, concat_axis=0, tiled=True)  22.6 us
    ppermute x15, starting transfers between devices, on_device(): xs[k] = lax.ppermute(xs[k], 'depth', [(d, d ^ k) for d in range(N)])  17.5 us
    pallas_call x1, Pallas kernels, column_step(): pl.pallas_call(column_kernel, in_specs=[pl.BlockSpec(memory_space=pltpu.S...  14.1 us
    ppermute x2, starting transfers between devices, swap(): return lax.ppermute(x, ('depth', 'cols'), pairs)  8.73 us
    ppermute x2, waiting for transfers between devices, swap(): return lax.ppermute(x, ('depth', 'cols'), pairs)  7.14 us
    pallas_call x1, Pallas kernels, row_proj(): pl.pallas_call(row_proj_kernel, in_specs=[HBM] * 5, out_specs=HBM, out_sh...  6.35 us
  transfers between devices with their start and end apart: 20, of which 9 were waited for; matrix products, arithmetic and copies ran while one was open for 0% of the time, Pallas kernels for 1%

profile of v4, /device:TPU:4, one launch (start us, length us, event | category | flops | bytes accessed | tf_op | source)
XLA Modules:
  0.0 235.8 jit_solution(3425140495882716749)
XLA Ops:
  0.6 6.3 %shard_map.140 = bf16[16,768,128]{2,1,0:T(8,128)(2,1)} custom-call(bf16[512,768]{1,0:T(8,128)(2,1)} %bitcast.12, s32[16,32]{1,0:T(8,128)} %occ_ref.1, bf16[768,768]{1,0:T(8,128)(2,1)} %wq_hbm.1, bf16[768,768]{1,0:T(8,128)(2,1)} %wk_hbm.1, bf16[768,768]{1,0:T(8,128)(2,1)} %wv_hbm.1), custom_call_target="tpu_custom_call" | custom-call | flops 1811939328 | bytes 8000000 | tf_op jit(solution)/shard_map/pallas_call | solution.py:131
  7.0 11.2 %all-to-all-start = ((bf16[16,768,128]{2,1,0:T(8,128)(2,1)}), bf16[16,768,128]{2,1,0:T(8,128)(2,1)S(1)}, u32[]{:S(2)}, u32[]{:S(2)}) async-start(bf16[16,768,128]{2,1,0:T(8,128)(2,1)} %shard_map.140), calls=%async_computation | async-start | bytes 6291456 | tf_op jit(solution)/shard_map/all_to_all | solution.py:475
  23.3 2.6 %collective-permute-start.4 = (bf16[32,896]{1,0:T(8,128)(2,1)S(1)}, bf16[32,896]{1,0:T(8,128)(2,1)S(1)}, u32[]{:S(2)}, u32[]{:S(2)}) collective-permute-start(bf16[32,896]{1,0:T(8,128)(2,1)S(1)} %get-tuple-element.44), channel_id=1, source_target_pairs={{0,80},{16,64},{32,112},{48,96},{64,16},{80,0},{96,48},{112,32},{1... | collective-permute-start | bytes 172040 | tf_op jit(solution)/shard_map/ppermute | solution.py:493
  26.5 1.3 collective-permute-start.6
  29.4 2.5 %collective-permute-start.9 = (bf16[32,896]{1,0:T(8,128)(2,1)S(1)}, bf16[32,896]{1,0:T(8,128)(2,1)S(1)}, u32[]{:S(2)}, u32[]{:S(2)}) collective-permute-start(bf16[32,896]{1,0:T(8,128)(2,1)S(1)} %get-tuple-element.49), channel_id=1, source_target_pairs={{0,160},{16,176},{32,128},{48,144},{64,224},{80,240},{96,192},{112... | collective-permute-start | bytes 172040 | tf_op jit(solution)/shard_map/ppermute | solution.py:493
  32.2 2.4 %collective-permute-start.11 = (bf16[32,896]{1,0:T(8,128)(2,1)S(1)}, bf16[32,896]{1,0:T(8,128)(2,1)S(1)}, u32[]{:S(2)}, u32[]{:S(2)}) collective-permute-start(bf16[32,896]{1,0:T(8,128)(2,1)S(1)} %get-tuple-element.51), channel_id=1, source_target_pairs={{0,192},{16,208},{32,224},{48,240},{64,128},{80,144},{96,160},{112... | collective-permute-start | bytes 172040 | tf_op jit(solution)/shard_map/ppermute | solution.py:493
  34.6 2.5 %collective-permute-start.12 = (bf16[32,896]{1,0:T(8,128)(2,1)S(1)}, bf16[32,896]{1,0:T(8,128)(2,1)S(1)}, u32[]{:S(2)}, u32[]{:S(2)}) collective-permute-start(bf16[32,896]{1,0:T(8,128)(2,1)S(1)} %get-tuple-element.52), channel_id=1, source_target_pairs={{0,208},{16,192},{32,240},{48,224},{64,144},{80,128},{96,176},{112... | collective-permute-start | bytes 172040 | tf_op jit(solution)/shard_map/ppermute | solution.py:493
  37.0 1.5 collective-permute-start.13
  39.3 1.9 collective-permute-done.12.refs_13_
  41.2 2.1 collective-permute-done.13.refs_14_
  44.2 48.9 %all-to-all-done.qk_ref.v_ref = bf16[16,768,128]{2,1,0:T(8,128)(2,1)S(1)} async-done(((bf16[16,768,128]{2,1,0:T(8,128)(2,1)}), bf16[16,768,128]{2,1,0:T(8,128)(2,1)S(1)}, u32[]{:S(2)}, u32[]{:S(2)}) %all-to-all-start) | async-done | bytes 3145760 | tf_op jit(solution)/shard_map/all_to_all | solution.py:475
  94.0 17.9 %all_to_all.30.in_ref = f32[16,32,512]{2,1,0:T(8,128)S(1)} all-to-all(f32[16,32,512]{2,1,0:T(8,128)S(1)} %bitcast.11), channel_id=1, replica_groups=mesh['depth'=16,'cols'=16] {'depth'}, dimensions={0} | all-to-all | bytes 2097152 | tf_op jit(solution)/shard_map/all_to_all | solution.py:475
  112.1 13.4 %all_to_all.31.p_ref = bf16[16,32,512]{2,1,0:T(8,128)(2,1)S(1)} all-to-all(bf16[16,32,512]{2,1,0:T(8,128)(2,1)S(1)} %shard_map.143), channel_id=1, replica_groups=mesh['depth'=16,'cols'=16] {'depth'}, dimensions={0} | all-to-all | bytes 1048576 | tf_op jit(solution)/shard_map/all_to_all | solution.py:475
  126.6 39.4 %all_to_all.32 = bf16[256,16,128]{2,1,0:T(8,128)(2,1)} all-to-all(bf16[256,16,128]{2,1,0:T(8,128)(2,1)S(1)} %bitcast.10), channel_id=1, replica_groups=mesh['depth'=16,'cols'=16] {'cols','depth'}, dimensions={0} | all-to-all | bytes 2097152 | tf_op jit(solution)/shard_map/all_to_all | solution.py:475
  166.0 14.1 %shard_map.145 = (bf16[16,64,768]{2,1,0:T(8,128)(2,1)}, bf16[64,256]{1,0:T(8,128)(2,1)}) custom-call(s32[1]{0:T(128)} %bitcast.me_ref, bf16[4096,128]{1,0:T(8,128)(2,1)} %bitcast.14, bf16[32,768]{1,0:T(8,128)(2,1)} %bitcast.17, bf16[32,768]{1,0:T(8,128)(2,1)} %bitcast.18, bf16[768,768]{1,0:T(8,128)(2,1)} %wo_hbm.1, bf16[768,768]{1,0:T(8,128)(2,1)} %cq_hbm.1, ...), custom_call_target="tpu_custom_call" | custom-call | flops 3019898880 | bytes 9000000 | tf_op jit(solution)/shard_map/pallas_call | solution.py:364
  180.1 5.5 %all-to-all-start.4 = ((bf16[16,64,768]{2,1,0:T(8,128)(2,1)}), bf16[16,64,768]{2,1,0:T(8,128)(2,1)S(1)}, u32[]{:S(2)}, u32[]{:S(2)}) async-start(bf16[16,64,768]{2,1,0:T(8,128)(2,1)} %get-tuple-element.72), calls=%async_computation.4 | async-start | bytes 3145728 | tf_op jit(solution)/shard_map/all_to_all | solution.py:475
  185.6 2.2 collective-permute-start.15
  187.9 7.1 %collective-permute-done.15 = bf16[64,256]{1,0:T(8,128)(2,1)S(1)} collective-permute-done((bf16[64,256]{1,0:T(8,128)(2,1)S(1)}, bf16[64,256]{1,0:T(8,128)(2,1)S(1)}, u32[]{:S(2)}, u32[]{:S(2)}) %collective-permute-start.15) | collective-permute-done | bytes 32800 | tf_op jit(solution)/shard_map/ppermute | solution.py:480
  195.0 10.4 %all-to-all-done.4.in_ref.l_ref = bf16[16,64,768]{2,1,0:T(8,128)(2,1)S(1)} async-done(((bf16[16,64,768]{2,1,0:T(8,128)(2,1)}), bf16[16,64,768]{2,1,0:T(8,128)(2,1)S(1)}, u32[]{:S(2)}, u32[]{:S(2)}) %all-to-all-start.4) | async-done | bytes 1572896 | tf_op jit(solution)/shard_map/all_to_all | solution.py:475
  206.2 5.8 %all-to-all-start.5 = ((bf16[16,64,256]{2,1,0:T(8,128)(2,1)}), bf16[16,64,256]{2,1,0:T(8,128)(2,1)S(1)}, u32[]{:S(2)}, u32[]{:S(2)}) async-start(bf16[16,64,256]{2,1,0:T(8,128)(2,1)} %broadcast_in_dim.2), calls=%async_computation.5 | async-start | bytes 1048576 | tf_op jit(solution)/shard_map/all_to_all | solution.py:475
  212.1 6.5 %collective-permute-start.16 = (bf16[32,128]{1,0:T(8,128)(2,1)S(1)}, bf16[32,128]{1,0:T(8,128)(2,1)S(1)}, u32[]{:S(2)}, u32[]{:S(2)}) collective-permute-start(bf16[32,128]{1,0:T(8,128)(2,1)S(1)} %bitcast.16), channel_id=1, source_target_pairs={{0,0},{1,16},{2,32},{3,48},{4,64},{5,80},{6,96},{7,112},{8,128},{9... | collective-permute-start | bytes 24584 | tf_op jit(solution)/shard_map/ppermute | solution.py:480
  218.6 1.5 shard_map.146
  220.1 11.7 %all-to-all-done.5.r_ref = bf16[16,64,256]{2,1,0:T(8,128)(2,1)S(1)} async-done(((bf16[16,64,256]{2,1,0:T(8,128)(2,1)}), bf16[16,64,256]{2,1,0:T(8,128)(2,1)S(1)}, u32[]{:S(2)}, u32[]{:S(2)}) %all-to-all-start.5) | async-done | bytes 524320 | tf_op jit(solution)/shard_map/all_to_all | solution.py:475
  231.8 4.0 %shard_map.147 = bf16[1024,128]{1,0:T(8,128)(2,1)} custom-call(bf16[16,64,768]{2,1,0:T(8,128)(2,1)S(1)} %all-to-all-done.4.in_ref.l_ref, bf16[16,64,256]{2,1,0:T(8,128)(2,1)S(1)} %all-to-all-done.5.r_ref, bf16[32,128]{1,0:T(8,128)(2,1)S(1)} %collective-permute-done.16.n_ref, bf16[1024,128]{1,0:T(8,128)(2,1)S(1)} %copy-done.2), custom_call_target="tpu_custom_call" | custom-call | flops 1610612736 | bytes 6000000 | tf_op jit(solution)/shard_map/pallas_call | solution.py:451
  (67 shorter events, 12.1 us)
Async XLA Ops:
  7.0 86.1 %all-to-all-start = ((bf16[16,768,128]{2,1,0:T(8,128)(2,1)}), bf16[16,768,128]{2,1,0:T(8,128)(2,1)S(1)}, u32[]{:S(2)}, u32[]{:S(2)}) async-start(bf16[16,768,128]{2,1,0:T(8,128)(2,1)} %shard_map.140), calls=%async_computation | async-start | bytes 6291456 | tf_op jit(solution)/shard_map/all_to_all | solution.py:475
  20.9 5.0 %collective-permute-start = (bf16[32,896]{1,0:T(8,128)(2,1)S(1)}, bf16[32,896]{1,0:T(8,128)(2,1)S(1)}, u32[]{:S(2)}, u32[]{:S(2)}) collective-permute-start(bf16[32,896]{1,0:T(8,128)(2,1)S(1)} %get-tuple-element.40), channel_id=1, source_target_pairs={{0,16},{16,0},{32,48},{48,32},{64,80},{80,64},{96,112},{112,96},{1... | collective-permute-start | bytes 172040 | tf_op jit(solution)/shard_map/ppermute | solution.py:493
  20.9 5.5 %collective-permute-start.1 = (bf16[32,896]{1,0:T(8,128)(2,1)S(1)}, bf16[32,896]{1,0:T(8,128)(2,1)S(1)}, u32[]{:S(2)}, u32[]{:S(2)}) collective-permute-start(bf16[32,896]{1,0:T(8,128)(2,1)S(1)} %get-tuple-element.41), channel_id=1, source_target_pairs={{0,32},{16,48},{32,0},{48,16},{64,96},{80,112},{96,64},{112,80},{1... | collective-permute-start | bytes 172040 | tf_op jit(solution)/shard_map/ppermute | solution.py:493
  22.1 5.7 %collective-permute-start.2 = (bf16[32,896]{1,0:T(8,128)(2,1)S(1)}, bf16[32,896]{1,0:T(8,128)(2,1)S(1)}, u32[]{:S(2)}, u32[]{:S(2)}) collective-permute-start(bf16[32,896]{1,0:T(8,128)(2,1)S(1)} %get-tuple-element.42), channel_id=1, source_target_pairs={{0,48},{16,32},{32,16},{48,0},{64,112},{80,96},{96,80},{112,64},{1... | collective-permute-start | bytes 172040 | tf_op jit(solution)/shard_map/ppermute | solution.py:493
  22.8 6.2 %collective-permute-start.3 = (bf16[32,896]{1,0:T(8,128)(2,1)S(1)}, bf16[32,896]{1,0:T(8,128)(2,1)S(1)}, u32[]{:S(2)}, u32[]{:S(2)}) collective-permute-start(bf16[32,896]{1,0:T(8,128)(2,1)S(1)} %get-tuple-element.43), channel_id=1, source_target_pairs={{0,64},{16,80},{32,96},{48,112},{64,0},{80,16},{96,32},{112,48},{1... | collective-permute-start | bytes 172040 | tf_op jit(solution)/shard_map/ppermute | solution.py:493
  23.3 6.1 %collective-permute-start.4 = (bf16[32,896]{1,0:T(8,128)(2,1)S(1)}, bf16[32,896]{1,0:T(8,128)(2,1)S(1)}, u32[]{:S(2)}, u32[]{:S(2)}) collective-permute-start(bf16[32,896]{1,0:T(8,128)(2,1)S(1)} %get-tuple-element.44), channel_id=1, source_target_pairs={{0,80},{16,64},{32,112},{48,96},{64,16},{80,0},{96,48},{112,32},{1... | collective-permute-start | bytes 172040 | tf_op jit(solution)/shard_map/ppermute | solution.py:493
  25.9 68.0 %copy-start.4 = (bf16[32,896]{1,0:T(8,128)(2,1)}, bf16[32,896]{1,0:T(8,128)(2,1)S(1)}, u32[]{:S(2)}) copy-start(bf16[32,896]{1,0:T(8,128)(2,1)S(1)} %collective-permute-done.refs_1_) | copy-start | bytes 172036
  25.9 6.0 %collective-permute-start.5 = (bf16[32,896]{1,0:T(8,128)(2,1)S(1)}, bf16[32,896]{1,0:T(8,128)(2,1)S(1)}, u32[]{:S(2)}, u32[]{:S(2)}) collective-permute-start(bf16[32,896]{1,0:T(8,128)(2,1)S(1)} %get-tuple-element.45), channel_id=1, source_target_pairs={{0,96},{16,112},{32,64},{48,80},{64,32},{80,48},{96,0},{112,16},{1... | collective-permute-start | bytes 172040 | tf_op jit(solution)/shard_map/ppermute | solution.py:493
  26.5 67.5 %copy-start.5 = (bf16[32,896]{1,0:T(8,128)(2,1)}, bf16[32,896]{1,0:T(8,128)(2,1)S(1)}, u32[]{:S(2)}) copy-start(bf16[32,896]{1,0:T(8,128)(2,1)S(1)} %collective-permute-done.1.refs_2_) | copy-start | bytes 172036
  26.5 5.7 %collective-permute-start.6 = (bf16[32,896]{1,0:T(8,128)(2,1)S(1)}, bf16[32,896]{1,0:T(8,128)(2,1)S(1)}, u32[]{:S(2)}, u32[]{:S(2)}) collective-permute-start(bf16[32,896]{1,0:T(8,128)(2,1)S(1)} %get-tuple-element.46), channel_id=1, source_target_pairs={{0,112},{16,96},{32,80},{48,64},{64,48},{80,32},{96,16},{112,0},{1... | collective-permute-start | bytes 172040 | tf_op jit(solution)/shard_map/ppermute | solution.py:493
  27.8 66.2 %copy-start.6 = (bf16[32,896]{1,0:T(8,128)(2,1)}, bf16[32,896]{1,0:T(8,128)(2,1)S(1)}, u32[]{:S(2)}) copy-start(bf16[32,896]{1,0:T(8,128)(2,1)S(1)} %collective-permute-done.2.refs_3_) | copy-start | bytes 172036
  27.8 6.8 %collective-permute-start.7 = (bf16[32,896]{1,0:T(8,128)(2,1)S(1)}, bf16[32,896]{1,0:T(8,128)(2,1)S(1)}, u32[]{:S(2)}, u32[]{:S(2)}) collective-permute-start(bf16[32,896]{1,0:T(8,128)(2,1)S(1)} %get-tuple-element.47), channel_id=1, source_target_pairs={{0,128},{16,144},{32,160},{48,176},{64,192},{80,208},{96,224},{112... | collective-permute-start | bytes 172040 | tf_op jit(solution)/shard_map/ppermute | solution.py:493
  29.0 65.0 %copy-start.7 = (bf16[32,896]{1,0:T(8,128)(2,1)}, bf16[32,896]{1,0:T(8,128)(2,1)S(1)}, u32[]{:S(2)}) copy-start(bf16[32,896]{1,0:T(8,128)(2,1)S(1)} %collective-permute-done.3.refs_4_) | copy-start | bytes 172036
  29.0 8.0 %collective-permute-start.8 = (bf16[32,896]{1,0:T(8,128)(2,1)S(1)}, bf16[32,896]{1,0:T(8,128)(2,1)S(1)}, u32[]{:S(2)}, u32[]{:S(2)}) collective-permute-start(bf16[32,896]{1,0:T(8,128)(2,1)S(1)} %get-tuple-element.48), channel_id=1, source_target_pairs={{0,144},{16,128},{32,176},{48,160},{64,208},{80,192},{96,240},{112... | collective-permute-start | bytes 172040 | tf_op jit(solution)/shard_map/ppermute | solution.py:493
  29.4 9.1 %collective-permute-start.9 = (bf16[32,896]{1,0:T(8,128)(2,1)S(1)}, bf16[32,896]{1,0:T(8,128)(2,1)S(1)}, u32[]{:S(2)}, u32[]{:S(2)}) collective-permute-start(bf16[32,896]{1,0:T(8,128)(2,1)S(1)} %get-tuple-element.49), channel_id=1, source_target_pairs={{0,160},{16,176},{32,128},{48,144},{64,224},{80,240},{96,192},{112... | collective-permute-start | bytes 172040 | tf_op jit(solution)/shard_map/ppermute | solution.py:493
  32.0 7.1 %collective-permute-start.10 = (bf16[32,896]{1,0:T(8,128)(2,1)S(1)}, bf16[32,896]{1,0:T(8,128)(2,1)S(1)}, u32[]{:S(2)}, u32[]{:S(2)}) collective-permute-start(bf16[32,896]{1,0:T(8,128)(2,1)S(1)} %get-tuple-element.50), channel_id=1, source_target_pairs={{0,176},{16,160},{32,144},{48,128},{64,240},{80,224},{96,208},{112... | collective-permute-start | bytes 172040 | tf_op jit(solution)/shard_map/ppermute | solution.py:493
  32.2 7.1 %collective-permute-start.11 = (bf16[32,896]{1,0:T(8,128)(2,1)S(1)}, bf16[32,896]{1,0:T(8,128)(2,1)S(1)}, u32[]{:S(2)}, u32[]{:S(2)}) collective-permute-start(bf16[32,896]{1,0:T(8,128)(2,1)S(1)} %get-tuple-element.51), channel_id=1, source_target_pairs={{0,192},{16,208},{32,224},{48,240},{64,128},{80,144},{96,160},{112... | collective-permute-start | bytes 172040 | tf_op jit(solution)/shard_map/ppermute | solution.py:493
  34.6 6.6 %collective-permute-start.12 = (bf16[32,896]{1,0:T(8,128)(2,1)S(1)}, bf16[32,896]{1,0:T(8,128)(2,1)S(1)}, u32[]{:S(2)}, u32[]{:S(2)}) collective-permute-start(bf16[32,896]{1,0:T(8,128)(2,1)S(1)} %get-tuple-element.52), channel_id=1, source_target_pairs={{0,208},{16,192},{32,240},{48,224},{64,144},{80,128},{96,176},{112... | collective-permute-start | bytes 172040 | tf_op jit(solution)/shard_map/ppermute | solution.py:493
  37.0 6.2 %collective-permute-start.13 = (bf16[32,896]{1,0:T(8,128)(2,1)S(1)}, bf16[32,896]{1,0:T(8,128)(2,1)S(1)}, u32[]{:S(2)}, u32[]{:S(2)}) collective-permute-start(bf16[32,896]{1,0:T(8,128)(2,1)S(1)} %get-tuple-element.53), channel_id=1, source_target_pairs={{0,224},{16,240},{32,192},{48,208},{64,160},{80,176},{96,128},{112... | collective-permute-start | bytes 172040 | tf_op jit(solution)/shard_map/ppermute | solution.py:493
  38.6 5.7 %collective-permute-start.14 = (bf16[32,896]{1,0:T(8,128)(2,1)S(1)}, bf16[32,896]{1,0:T(8,128)(2,1)}, u32[]{:S(2)}, u32[]{:S(2)}) collective-permute-start(bf16[32,896]{1,0:T(8,128)(2,1)S(1)} %get-tuple-element.54), channel_id=1, source_target_pairs={{0,240},{16,224},{32,208},{48,192},{64,176},{80,160},{96,144},{112... | collective-permute-start | bytes 172040 | tf_op jit(solution)/shard_map/ppermute | solution.py:493
  180.1 25.3 %all-to-all-start.4 = ((bf16[16,64,768]{2,1,0:T(8,128)(2,1)}), bf16[16,64,768]{2,1,0:T(8,128)(2,1)S(1)}, u32[]{:S(2)}, u32[]{:S(2)}) async-start(bf16[16,64,768]{2,1,0:T(8,128)(2,1)} %get-tuple-element.72), calls=%async_computation.4 | async-start | bytes 3145728 | tf_op jit(solution)/shard_map/all_to_all | solution.py:475
  185.6 9.4 %collective-permute-start.15 = (bf16[64,256]{1,0:T(8,128)(2,1)S(1)}, bf16[64,256]{1,0:T(8,128)(2,1)S(1)}, u32[]{:S(2)}, u32[]{:S(2)}) collective-permute-start(bf16[64,256]{1,0:T(8,128)(2,1)S(1)} %copy-done.18), channel_id=1, source_target_pairs={{0,0},{1,16},{2,32},{3,48},{4,64},{5,80},{6,96},{7,112},{8,128},{9... | collective-permute-start | bytes 98312 | tf_op jit(solution)/shard_map/ppermute | solution.py:480
  206.2 25.5 %all-to-all-start.5 = ((bf16[16,64,256]{2,1,0:T(8,128)(2,1)}), bf16[16,64,256]{2,1,0:T(8,128)(2,1)S(1)}, u32[]{:S(2)}, u32[]{:S(2)}) async-start(bf16[16,64,256]{2,1,0:T(8,128)(2,1)} %broadcast_in_dim.2), calls=%async_computation.5 | async-start | bytes 1048576 | tf_op jit(solution)/shard_map/all_to_all | solution.py:475
  212.1 19.7 %collective-permute-start.16 = (bf16[32,128]{1,0:T(8,128)(2,1)S(1)}, bf16[32,128]{1,0:T(8,128)(2,1)S(1)}, u32[]{:S(2)}, u32[]{:S(2)}) collective-permute-start(bf16[32,128]{1,0:T(8,128)(2,1)S(1)} %bitcast.16), channel_id=1, source_target_pairs={{0,0},{1,16},{2,32},{3,48},{4,64},{5,80},{6,96},{7,112},{8,128},{9... | collective-permute-start | bytes 24584 | tf_op jit(solution)/shard_map/ppermute | solution.py:480
  (15 other events, 257.2 us)

commit v5 on v4

--- a/solution.py
+++ b/solution.py
@@ -22,6 +22,7 @@
 C = 32
 PC = 128
 XW = E + 128
+RW = 80
 PARTS = 2
 
 NT = (((1,), (1,)), ((), ()))
@@ -180,7 +181,7 @@
             axis=1,
         )
 
-    out_ref[...] = mmt(side(0), side(1)) * (1.0 / math.sqrt(64 * SEQS))
+    out_ref[...] = (mmt(side(0), side(1)) * (1.0 / math.sqrt(64 * SEQS))).astype(bf16)
 
 
 def partial_logits(qkv):
@@ -189,16 +190,16 @@
         grid=(1,),
         in_specs=[pl.BlockSpec((N, 512, 128), lambda n: (0, 0, 0))],
         out_specs=pl.BlockSpec((SITES, SITES), lambda n: (0, 0)),
-        out_shape=jax.ShapeDtypeStruct((SITES, SITES), f32),
+        out_shape=jax.ShapeDtypeStruct((SITES, SITES), bf16),
         compiler_params=params(20),
         cost_estimate=cost(2 * SITES * SITES * 1024, 3_000_000),
     )(qkv)
 
 
 def softmax_kernel(in_ref, out_ref):
-    total = in_ref[0]
+    total = in_ref[0].astype(f32)
     for k in range(1, N):
-        total = total + in_ref[k]
+        total = total + in_ref[k].astype(f32)
     top = jnp.max(total, axis=-1, keepdims=True)
     e = jnp.exp(total - top)
     p = (e / jnp.sum(e, axis=-1, keepdims=True)).astype(bf16)
@@ -352,6 +353,7 @@
     ]
     row = lax.broadcasted_iota(jnp.int32, (C, SEQS), 0)
     count = jnp.where(row == 0, counts[0], counts[1]).astype(bf16)
+    r_ref[2 * C :, :] = count[: RW - 2 * C, :]
     left[...] = jnp.concatenate([factors[:C, :], count], axis=1)
     for k in range(N):
         sent.append(pltpu.make_async_copy(left, out_hbm.at[k, pl.ds(I, C)], out_sems.at[k]))
@@ -367,7 +369,7 @@
         out_specs=[HBM, pl.BlockSpec(memory_space=pltpu.VMEM)],
         out_shape=[
             jax.ShapeDtypeStruct((N, 2 * I, E), bf16),
-            jax.ShapeDtypeStruct((2 * C, SEQS), bf16),
+            jax.ShapeDtypeStruct((RW, SEQS), bf16),
         ],
         scratch_shapes=[
             pltpu.VMEM((2, N, 2, 8, E), f32),
@@ -409,8 +411,12 @@
 
 
 def pair_kernel(
-    l_ref, r_ref, n_ref, wp_ref, out_ref, l0, l1, l2, l3, l4, lp, lhs, osc, wk
+    me_ref, l_ref, r0, r1, r2, r3, wp_ref, out_ref,
+    l0, l1, l2, l3, l4, lp, lhs, osc, wk, r_ref,
 ):
+    for near, ref in enumerate((r0, r1, r2, r3)):
+        for far in range(4):
+            r_ref[jnp.bitwise_xor(me_ref[1], 4 * far + near)] = ref[RW * far : RW * far + RW]
     wk[...] = jnp.zeros_like(wk)
     for c in range(C):
         w = wp_ref[C * c : C * c + C, :]
@@ -429,7 +435,7 @@
         lp[rows, :128] = jnp.concatenate([across(l0, c), across(l2, c)], axis=0).astype(bf16)
         lp[rows, 128:] = jnp.concatenate([across(l1, c), across(l3, c)], axis=0).astype(bf16)
     left_count = jnp.concatenate([across(l4, 0), across(l4, 1)], axis=0)
-    right = r_ref[...].reshape(N * 2 * C, SEQS)
+    right = r_ref[:, : 2 * C, :].reshape(N * 2 * C, SEQS)
     for c in range(0, C, 4):
         outer = mmt(lp[C * c : C * c + 4 * C, :], right).astype(bf16)
         for k in range(4):
@@ -438,25 +444,26 @@
                     C * k : C * k + C, 128 * j : 128 * j + 128
                 ]
     acc = mm(lhs[...], wk[...])
-    right_count = n_ref[...].astype(f32)
+    right_count = r_ref[:, 2 * C :, :128].astype(f32)
     for j in range(C):
         part = acc[C * (j // 4) : C * (j // 4) + C, 128 * (j % 4) : 128 * (j % 4) + 128]
-        part = part / (jnp.minimum(left_count, right_count[j : j + 1, :]) + 0.001)
+        count = right_count[j // 2, j % 2 : j % 2 + 1, :]
+        part = part / (jnp.minimum(left_count, count) + 0.001)
         for i in range(2):
             osc[pl.ds(C * i + j, N, stride=2 * C), :] = part[N * i : N * i + N, :]
     out_ref[...] = osc[...].astype(bf16)
 
 
-def pair_step(both, right, counts, wp):
+def pair_step(me, both, rights, wp):
     return pl.pallas_call(
         pair_kernel,
         grid=(1,),
         in_specs=[
+            pl.BlockSpec(memory_space=pltpu.SMEM),
             pl.BlockSpec((N, I, E), lambda n: (0, 1, 0)),
-            pl.BlockSpec((N, 2 * C, SEQS), lambda n: (0, 0, 0)),
-            pl.BlockSpec((C, 128), lambda n: (0, 0)),
-            pl.BlockSpec((C * C, PC), lambda n: (0, 0)),
-        ],
+        ]
+        + [pl.BlockSpec((4 * RW, SEQS), lambda n: (0, 0))] * 4
+        + [pl.BlockSpec((C * C, PC), lambda n: (0, 0))],
         out_specs=pl.BlockSpec((C * C, PC), lambda n: (0, 0)),
         out_shape=jax.ShapeDtypeStruct((C * C, PC), bf16),
         scratch_shapes=[pltpu.VMEM((N * C, 128), f32)] * 5
@@ -465,10 +472,11 @@
             pltpu.VMEM((256, 4096), bf16),
             pltpu.VMEM((1024, PC), f32),
             pltpu.VMEM((4096, 512), bf16),
+            pltpu.VMEM((N, RW, SEQS), bf16),
         ],
         compiler_params=params(24),
         cost_estimate=cost(2 * 1024 * 1024 * 256 + 2 * 256 * 4096 * 512, 6_000_000),
-    )(both, right, counts, wp)
+    )(me, both, *rights, wp)
 
 
 def exchange(x, axis):
@@ -480,17 +488,21 @@
     return lax.ppermute(x, ("depth", "cols"), pairs)
 
 
+def mirror(x, k, axis):
+    return lax.ppermute(x, axis, [(d, d ^ k) for d in range(N)])
+
+
 def on_device(x, occupancy, wq, wk, wv, wo, cq, ck, cv, co, f1, f2, wp):
     x = x.reshape(ROWS, E)
 
-    me = lax.axis_index("depth").astype(jnp.int32).reshape(1)
+    me = jnp.stack([lax.axis_index("depth"), lax.axis_index("cols")]).astype(jnp.int32)
 
     sent = row_proj(x, occupancy, wq, wk, wv)
     qkv = exchange(sent, "cols")
     later, _ = lax.optimization_barrier((x, sent))
     xs = list(turn(me, later, occupancy))
     for k in range(1, N):
-        xs[k] = lax.ppermute(xs[k], "depth", [(d, d ^ k) for d in range(N)])
+        xs[k] = mirror(xs[k], k, "depth")
     qkv, xs = lax.optimization_barrier((qkv, xs))
 
     parts = exchange(partial_logits(qkv).reshape(N, I, SITES), "depth")
@@ -499,12 +511,13 @@
     mr = exchange(mix.reshape(N * N, 16, 128), ("cols", "depth")).reshape(4096, 128)
 
     both, right = column_step(me, mr, f1.T, f2.T, wo, cq, ck, cv, co, xs)
+    both = exchange(both, "depth")
     right = swap(right)
-    both = exchange(both, "depth")
-    counts = swap(both[:, I : I + 2, 512:640].reshape(C, 128))
-    right = exchange(jnp.broadcast_to(right[None], (N, 2 * C, SEQS)), "cols")
+    far = [right] + [mirror(right, 4 * k, "cols") for k in range(1, 4)]
+    far = jnp.concatenate(far, axis=0)
+    rights = [far] + [mirror(far, k, "cols") for k in range(1, 4)]
     out = back(both)
-    pair = pair_step(both, right, counts, wp)
+    pair = pair_step(me, both, rights, wp)
     return out.reshape(S, I, E), pair.reshape(C, C, PC)
 
 

time: 237 us -> 225 us (0.949)
  waiting for transfers between devices: 83.2 us -> 71 us
  starting transfers between devices: 48.8 us -> 55.2 us
  blocking collectives: 70.6 us -> 65 us
    all_to_all x3 -> x2, waiting for transfers between devices: 71 us -> 48.5 us  [exchange(): return lax.all_to_all(x, axis, split_axis=0, concat_axis=0, tiled=True)]
    ppermute x15 -> x21, starting transfers between devices: 17.5 us -> 36.2 us  [mirror(): return lax.ppermute(x, axis, [(d, d ^ k) for d in range(N)])]
    ppermute x15 -> x21, waiting for transfers between devices: 5.12 us -> 15.5 us  [mirror(): return lax.ppermute(x, axis, [(d, d ^ k) for d in range(N)])]
    ppermute x2 -> x1, starting transfers between devices: 8.73 us -> 2.25 us  [swap(): return lax.ppermute(x, ('depth', 'cols'), pairs)]
    all_to_all x3 -> x2, starting transfers between devices: 22.6 us -> 16.7 us  [exchange(): return lax.all_to_all(x, axis, split_axis=0, concat_axis=0, tiled=True)]
    all_to_all x3, blocking collectives: 70.6 us -> 65 us  [exchange(): return lax.all_to_all(x, axis, split_axis=0, concat_axis=0, tiled=True)]
    ppermute x2 -> x1, waiting for transfers between devices: 7.14 us -> 7.04 us  [swap(): return lax.ppermute(x, ('depth', 'cols'), pairs)]
  transfers between devices with their start and end apart: 20 -> 24, of which waited for: 9 -> 11; matrix products, arithmetic and copies ran while one was open for 0% -> 0% of each run, Pallas kernels for 1% -> 1%
where the time goes in v5:
time: 225 us
  waiting for transfers between devices  71 us (32%)
  blocking collectives  65 us (29%)
  starting transfers between devices  55.2 us (25%)
  Pallas kernels  30.1 us (13%)
  local copies, waits for them, and re-layouts  2.46 us (1%)
    all_to_all x3, blocking collectives, exchange(): return lax.all_to_all(x, axis, split_axis=0, concat_axis=0, tiled=True)  65 us
    all_to_all x2, waiting for transfers between devices, exchange(): return lax.all_to_all(x, axis, split_axis=0, concat_axis=0, tiled=True)  48.5 us
    ppermute x21, starting transfers between devices, mirror(): return lax.ppermute(x, axis, [(d, d ^ k) for d in range(N)])  36.2 us
    all_to_all x2, starting transfers between devices, exchange(): return lax.all_to_all(x, axis, split_axis=0, concat_axis=0, tiled=True)  16.7 us
    ppermute x21, waiting for transfers between devices, mirror(): return lax.ppermute(x, axis, [(d, d ^ k) for d in range(N)])  15.5 us
    pallas_call x1, Pallas kernels, column_step(): pl.pallas_call(column_kernel, in_specs=[pl.BlockSpec(memory_space=pltpu.S...  14.1 us
    ppermute x1, waiting for transfers between devices, swap(): return lax.ppermute(x, ('depth', 'cols'), pairs)  7.04 us
    pallas_call x1, Pallas kernels, row_proj(): pl.pallas_call(row_proj_kernel, in_specs=[HBM] * 5, out_specs=HBM, out_sh...  6.3 us
  transfers between devices with their start and end apart: 24, of which 11 were waited for; matrix products, arithmetic and copies ran while one was open for 0% of the time, Pallas kernels for 1%

profile of v5, /device:TPU:4, one launch (start us, length us, event | category | flops | bytes accessed | tf_op | source)
XLA Modules:
  0.0 224.8 jit_solution(13657366103403541318)
XLA Ops:
  0.6 6.3 %shard_map.140 = bf16[16,768,128]{2,1,0:T(8,128)(2,1)} custom-call(bf16[512,768]{1,0:T(8,128)(2,1)} %bitcast.12, s32[16,32]{1,0:T(8,128)} %occ_ref.1, bf16[768,768]{1,0:T(8,128)(2,1)} %wq_hbm.1, bf16[768,768]{1,0:T(8,128)(2,1)} %wk_hbm.1, bf16[768,768]{1,0:T(8,128)(2,1)} %wv_hbm.1), custom_call_target="tpu_custom_call" | custom-call | flops 1811939328 | bytes 8000000 | tf_op jit(solution)/shard_map/pallas_call | solution.py:132
  6.9 11.2 %all-to-all-start = ((bf16[16,768,128]{2,1,0:T(8,128)(2,1)}), bf16[16,768,128]{2,1,0:T(8,128)(2,1)S(1)}, u32[]{:S(2)}, u32[]{:S(2)}) async-start(bf16[16,768,128]{2,1,0:T(8,128)(2,1)} %shard_map.140), calls=%async_computation | async-start | bytes 6291456 | tf_op jit(solution)/shard_map/all_to_all | solution.py:483
  23.9 2.6 %collective-permute-start.4 = (bf16[32,896]{1,0:T(8,128)(2,1)S(1)}, bf16[32,896]{1,0:T(8,128)(2,1)S(1)}, u32[]{:S(2)}, u32[]{:S(2)}) collective-permute-start(bf16[32,896]{1,0:T(8,128)(2,1)S(1)} %get-tuple-element.44), channel_id=1, source_target_pairs={{0,80},{16,64},{32,112},{48,96},{64,16},{80,0},{96,48},{112,32},{1... | collective-permute-start | bytes 172040 | tf_op jit(solution)/shard_map/ppermute | solution.py:492
  30.0 2.5 %collective-permute-start.9 = (bf16[32,896]{1,0:T(8,128)(2,1)S(1)}, bf16[32,896]{1,0:T(8,128)(2,1)S(1)}, u32[]{:S(2)}, u32[]{:S(2)}) collective-permute-start(bf16[32,896]{1,0:T(8,128)(2,1)S(1)} %get-tuple-element.49), channel_id=1, source_target_pairs={{0,160},{16,176},{32,128},{48,144},{64,224},{80,240},{96,192},{112... | collective-permute-start | bytes 172040 | tf_op jit(solution)/shard_map/ppermute | solution.py:492
  32.8 2.4 %collective-permute-start.11 = (bf16[32,896]{1,0:T(8,128)(2,1)S(1)}, bf16[32,896]{1,0:T(8,128)(2,1)S(1)}, u32[]{:S(2)}, u32[]{:S(2)}) collective-permute-start(bf16[32,896]{1,0:T(8,128)(2,1)S(1)} %get-tuple-element.51), channel_id=1, source_target_pairs={{0,192},{16,208},{32,224},{48,240},{64,128},{80,144},{96,160},{112... | collective-permute-start | bytes 172040 | tf_op jit(solution)/shard_map/ppermute | solution.py:492
  35.1 2.5 %collective-permute-start.12 = (bf16[32,896]{1,0:T(8,128)(2,1)S(1)}, bf16[32,896]{1,0:T(8,128)(2,1)S(1)}, u32[]{:S(2)}, u32[]{:S(2)}) collective-permute-start(bf16[32,896]{1,0:T(8,128)(2,1)S(1)} %get-tuple-element.52), channel_id=1, source_target_pairs={{0,208},{16,192},{32,240},{48,224},{64,144},{80,128},{96,176},{112... | collective-permute-start | bytes 172040 | tf_op jit(solution)/shard_map/ppermute | solution.py:492
  39.9 1.8 collective-permute-done.12.refs_13_
  41.7 2.0 collective-permute-done.13.refs_14_
  44.6 48.5 %all-to-all-done.qk_ref.v_ref = bf16[16,768,128]{2,1,0:T(8,128)(2,1)S(1)} async-done(((bf16[16,768,128]{2,1,0:T(8,128)(2,1)}), bf16[16,768,128]{2,1,0:T(8,128)(2,1)S(1)}, u32[]{:S(2)}, u32[]{:S(2)}) %all-to-all-start) | async-done | bytes 3145760 | tf_op jit(solution)/shard_map/all_to_all | solution.py:483
  94.0 12.2 %all_to_all.25.in_ref = bf16[16,32,512]{2,1,0:T(8,128)(2,1)S(1)} all-to-all(bf16[16,32,512]{2,1,0:T(8,128)(2,1)S(1)} %bitcast.11), channel_id=1, replica_groups=mesh['depth'=16,'cols'=16] {'depth'}, dimensions={0} | all-to-all | bytes 1048576 | tf_op jit(solution)/shard_map/all_to_all | solution.py:483
  106.5 13.4 %all_to_all.26.p_ref = bf16[16,32,512]{2,1,0:T(8,128)(2,1)S(1)} all-to-all(bf16[16,32,512]{2,1,0:T(8,128)(2,1)S(1)} %shard_map.143), channel_id=1, replica_groups=mesh['depth'=16,'cols'=16] {'depth'}, dimensions={0} | all-to-all | bytes 1048576 | tf_op jit(solution)/shard_map/all_to_all | solution.py:483
  121.0 39.4 %all_to_all.27 = bf16[256,16,128]{2,1,0:T(8,128)(2,1)} all-to-all(bf16[256,16,128]{2,1,0:T(8,128)(2,1)S(1)} %bitcast.10), channel_id=1, replica_groups=mesh['depth'=16,'cols'=16] {'cols','depth'}, dimensions={0} | all-to-all | bytes 2097152 | tf_op jit(solution)/shard_map/all_to_all | solution.py:483
  160.4 14.1 %shard_map.145 = (bf16[16,64,768]{2,1,0:T(8,128)(2,1)}, bf16[80,256]{1,0:T(8,128)(2,1)}) custom-call(s32[2]{0:T(128)} %copy-done.3, bf16[4096,128]{1,0:T(8,128)(2,1)} %bitcast.14, bf16[32,768]{1,0:T(8,128)(2,1)} %bitcast.16, bf16[32,768]{1,0:T(8,128)(2,1)} %bitcast.17, bf16[768,768]{1,0:T(8,128)(2,1)} %wo_hbm.1, bf16[768,768]{1,0:T(8,128)(2,1)} %cq_hbm.1, ...), custom_call_target="tpu_custom_call" | custom-call | flops 3019898880 | bytes 9000000 | tf_op jit(solution)/shard_map/pallas_call | solution.py:366
  174.4 5.5 %all-to-all-start.4 = ((bf16[16,64,768]{2,1,0:T(8,128)(2,1)}), bf16[16,64,768]{2,1,0:T(8,128)(2,1)S(1)}, u32[]{:S(2)}, u32[]{:S(2)}) async-start(bf16[16,64,768]{2,1,0:T(8,128)(2,1)} %get-tuple-element.72), calls=%async_computation.4 | async-start | bytes 3145728 | tf_op jit(solution)/shard_map/all_to_all | solution.py:483
  180.0 2.3 %collective-permute-start.15 = (bf16[80,256]{1,0:T(8,128)(2,1)S(1)}, bf16[80,256]{1,0:T(8,128)(2,1)S(1)}, u32[]{:S(2)}, u32[]{:S(2)}) collective-permute-start(bf16[80,256]{1,0:T(8,128)(2,1)S(1)} %copy-done.20), channel_id=1, source_target_pairs={{0,0},{1,16},{2,32},{3,48},{4,64},{5,80},{6,96},{7,112},{8,128},{9... | collective-permute-start | bytes 122888 | tf_op jit(solution)/shard_map/ppermute | solution.py:488
  182.2 7.0 %collective-permute-done.15 = bf16[80,256]{1,0:T(8,128)(2,1)S(1)} collective-permute-done((bf16[80,256]{1,0:T(8,128)(2,1)S(1)}, bf16[80,256]{1,0:T(8,128)(2,1)S(1)}, u32[]{:S(2)}, u32[]{:S(2)}) %collective-permute-start.15) | collective-permute-done | bytes 40992 | tf_op jit(solution)/shard_map/ppermute | solution.py:488
  189.3 3.4 %collective-permute-start.18 = (bf16[80,256]{1,0:T(8,128)(2,1)S(1)}, bf16[80,256]{1,0:T(8,128)(2,1)S(1)}, u32[]{:S(2)}, u32[]{:S(2)}) collective-permute-start(bf16[80,256]{1,0:T(8,128)(2,1)S(1)} %collective-permute-done.15), channel_id=1, source_target_pairs={{0,12},{1,13},{2,14},{3,15},{4,8},{5,9},{6,10},{7,11},{8,4},{9,5},... | collective-permute-start | bytes 122888 | tf_op jit(solution)/shard_map/ppermute | solution.py:492
  193.2 2.6 %collective-permute-start.16 = (bf16[80,256]{1,0:T(8,128)(2,1)S(1)}, bf16[80,256]{1,0:T(8,128)(2,1)S(1)}, u32[]{:S(2)}, u32[]{:S(2)}) collective-permute-start(bf16[80,256]{1,0:T(8,128)(2,1)S(1)} %collective-permute-done.15), channel_id=1, source_target_pairs={{0,4},{1,5},{2,6},{3,7},{4,0},{5,1},{6,2},{7,3},{8,12},{9,13},{10,... | collective-permute-start | bytes 122888 | tf_op jit(solution)/shard_map/ppermute | solution.py:492
  195.8 4.0 %collective-permute-done.16 = bf16[80,256]{1,0:T(8,128)(2,1)S(1)} collective-permute-done((bf16[80,256]{1,0:T(8,128)(2,1)S(1)}, bf16[80,256]{1,0:T(8,128)(2,1)S(1)}, u32[]{:S(2)}, u32[]{:S(2)}) %collective-permute-start.16) | collective-permute-done | bytes 40992 | tf_op jit(solution)/shard_map/ppermute | solution.py:492
  201.1 1.9 collective-permute-start.21
  203.0 10.3 %collective-permute-start.20 = (bf16[320,256]{1,0:T(8,128)(2,1)S(1)}, bf16[320,256]{1,0:T(8,128)(2,1)S(1)}, u32[]{:S(2)}, u32[]{:S(2)}) collective-permute-start(bf16[320,256]{1,0:T(8,128)(2,1)S(1)} %constant_dynamic-update-slice_fusion.r0), channel_id=1, source_target_pairs={{0,2},{1,3},{2,0},{3,1},{4,6},{5,7},{6,4},{7,5},{8,10},{9,11},{10,... | collective-permute-start | bytes 491528 | tf_op jit(solution)/shard_map/ppermute | solution.py:492
  214.8 3.6 %collective-permute-done.20.r2 = bf16[320,256]{1,0:T(8,128)(2,1)S(1)} collective-permute-done((bf16[320,256]{1,0:T(8,128)(2,1)S(1)}, bf16[320,256]{1,0:T(8,128)(2,1)S(1)}, u32[]{:S(2)}, u32[]{:S(2)}) %collective-permute-start.20) | collective-permute-done | bytes 163872 | tf_op jit(solution)/shard_map/ppermute | solution.py:492
  218.4 1.7 collective-permute-done.19.r1
  220.2 4.6 %shard_map.147 = bf16[1024,128]{1,0:T(8,128)(2,1)} custom-call(s32[2]{0:T(128)S(1)} %copy-done.4, bf16[16,64,768]{2,1,0:T(8,128)(2,1)S(1)} %all-to-all-done.4.in_ref.l_ref, bf16[320,256]{1,0:T(8,128)(2,1)S(1)} %constant_dynamic-update-slice_fusion.r0, bf16[320,256]{1,0:T(8,128)(2,1)S(1)} %collective-permute-done.19.r1, ...), custom_call_target="tpu_custom_call" | custom-call | flops 1610612736 | bytes 6000000 | tf_op jit(solution)/shard_map/pallas_call | solution.py:458
  (82 shorter events, 18.1 us)
Async XLA Ops:
  6.9 86.1 %all-to-all-start = ((bf16[16,768,128]{2,1,0:T(8,128)(2,1)}), bf16[16,768,128]{2,1,0:T(8,128)(2,1)S(1)}, u32[]{:S(2)}, u32[]{:S(2)}) async-start(bf16[16,768,128]{2,1,0:T(8,128)(2,1)} %shard_map.140), calls=%async_computation | async-start | bytes 6291456 | tf_op jit(solution)/shard_map/all_to_all | solution.py:483
  21.5 5.0 %collective-permute-start = (bf16[32,896]{1,0:T(8,128)(2,1)S(1)}, bf16[32,896]{1,0:T(8,128)(2,1)S(1)}, u32[]{:S(2)}, u32[]{:S(2)}) collective-permute-start(bf16[32,896]{1,0:T(8,128)(2,1)S(1)} %get-tuple-element.40), channel_id=1, source_target_pairs={{0,16},{16,0},{32,48},{48,32},{64,80},{80,64},{96,112},{112,96},{1... | collective-permute-start | bytes 172040 | tf_op jit(solution)/shard_map/ppermute | solution.py:492
  21.5 5.5 %collective-permute-start.1 = (bf16[32,896]{1,0:T(8,128)(2,1)S(1)}, bf16[32,896]{1,0:T(8,128)(2,1)S(1)}, u32[]{:S(2)}, u32[]{:S(2)}) collective-permute-start(bf16[32,896]{1,0:T(8,128)(2,1)S(1)} %get-tuple-element.41), channel_id=1, source_target_pairs={{0,32},{16,48},{32,0},{48,16},{64,96},{80,112},{96,64},{112,80},{1... | collective-permute-start | bytes 172040 | tf_op jit(solution)/shard_map/ppermute | solution.py:492
  22.7 5.7 %collective-permute-start.2 = (bf16[32,896]{1,0:T(8,128)(2,1)S(1)}, bf16[32,896]{1,0:T(8,128)(2,1)S(1)}, u32[]{:S(2)}, u32[]{:S(2)}) collective-permute-start(bf16[32,896]{1,0:T(8,128)(2,1)S(1)} %get-tuple-element.42), channel_id=1, source_target_pairs={{0,48},{16,32},{32,16},{48,0},{64,112},{80,96},{96,80},{112,64},{1... | collective-permute-start | bytes 172040 | tf_op jit(solution)/shard_map/ppermute | solution.py:492
  23.3 6.2 %collective-permute-start.3 = (bf16[32,896]{1,0:T(8,128)(2,1)S(1)}, bf16[32,896]{1,0:T(8,128)(2,1)S(1)}, u32[]{:S(2)}, u32[]{:S(2)}) collective-permute-start(bf16[32,896]{1,0:T(8,128)(2,1)S(1)} %get-tuple-element.43), channel_id=1, source_target_pairs={{0,64},{16,80},{32,96},{48,112},{64,0},{80,16},{96,32},{112,48},{1... | collective-permute-start | bytes 172040 | tf_op jit(solution)/shard_map/ppermute | solution.py:492
  23.9 6.1 %collective-permute-start.4 = (bf16[32,896]{1,0:T(8,128)(2,1)S(1)}, bf16[32,896]{1,0:T(8,128)(2,1)S(1)}, u32[]{:S(2)}, u32[]{:S(2)}) collective-permute-start(bf16[32,896]{1,0:T(8,128)(2,1)S(1)} %get-tuple-element.44), channel_id=1, source_target_pairs={{0,80},{16,64},{32,112},{48,96},{64,16},{80,0},{96,48},{112,32},{1... | collective-permute-start | bytes 172040 | tf_op jit(solution)/shard_map/ppermute | solution.py:492
  26.5 6.0 %collective-permute-start.5 = (bf16[32,896]{1,0:T(8,128)(2,1)S(1)}, bf16[32,896]{1,0:T(8,128)(2,1)S(1)}, u32[]{:S(2)}, u32[]{:S(2)}) collective-permute-start(bf16[32,896]{1,0:T(8,128)(2,1)S(1)} %get-tuple-element.45), channel_id=1, source_target_pairs={{0,96},{16,112},{32,64},{48,80},{64,32},{80,48},{96,0},{112,16},{1... | collective-permute-start | bytes 172040 | tf_op jit(solution)/shard_map/ppermute | solution.py:492
  27.0 5.7 %collective-permute-start.6 = (bf16[32,896]{1,0:T(8,128)(2,1)S(1)}, bf16[32,896]{1,0:T(8,128)(2,1)S(1)}, u32[]{:S(2)}, u32[]{:S(2)}) collective-permute-start(bf16[32,896]{1,0:T(8,128)(2,1)S(1)} %get-tuple-element.46), channel_id=1, source_target_pairs={{0,112},{16,96},{32,80},{48,64},{64,48},{80,32},{96,16},{112,0},{1... | collective-permute-start | bytes 172040 | tf_op jit(solution)/shard_map/ppermute | solution.py:492
  28.4 6.8 %collective-permute-start.7 = (bf16[32,896]{1,0:T(8,128)(2,1)S(1)}, bf16[32,896]{1,0:T(8,128)(2,1)S(1)}, u32[]{:S(2)}, u32[]{:S(2)}) collective-permute-start(bf16[32,896]{1,0:T(8,128)(2,1)S(1)} %get-tuple-element.47), channel_id=1, source_target_pairs={{0,128},{16,144},{32,160},{48,176},{64,192},{80,208},{96,224},{112... | collective-permute-start | bytes 172040 | tf_op jit(solution)/shard_map/ppermute | solution.py:492
  29.6 8.0 %collective-permute-start.8 = (bf16[32,896]{1,0:T(8,128)(2,1)S(1)}, bf16[32,896]{1,0:T(8,128)(2,1)S(1)}, u32[]{:S(2)}, u32[]{:S(2)}) collective-permute-start(bf16[32,896]{1,0:T(8,128)(2,1)S(1)} %get-tuple-element.48), channel_id=1, source_target_pairs={{0,144},{16,128},{32,176},{48,160},{64,208},{80,192},{96,240},{112... | collective-permute-start | bytes 172040 | tf_op jit(solution)/shard_map/ppermute | solution.py:492
  30.0 9.1 %collective-permute-start.9 = (bf16[32,896]{1,0:T(8,128)(2,1)S(1)}, bf16[32,896]{1,0:T(8,128)(2,1)S(1)}, u32[]{:S(2)}, u32[]{:S(2)}) collective-permute-start(bf16[32,896]{1,0:T(8,128)(2,1)S(1)} %get-tuple-element.49), channel_id=1, source_target_pairs={{0,160},{16,176},{32,128},{48,144},{64,224},{80,240},{96,192},{112... | collective-permute-start | bytes 172040 | tf_op jit(solution)/shard_map/ppermute | solution.py:492
  32.5 7.1 %collective-permute-start.10 = (bf16[32,896]{1,0:T(8,128)(2,1)S(1)}, bf16[32,896]{1,0:T(8,128)(2,1)S(1)}, u32[]{:S(2)}, u32[]{:S(2)}) collective-permute-start(bf16[32,896]{1,0:T(8,128)(2,1)S(1)} %get-tuple-element.50), channel_id=1, source_target_pairs={{0,176},{16,160},{32,144},{48,128},{64,240},{80,224},{96,208},{112... | collective-permute-start | bytes 172040 | tf_op jit(solution)/shard_map/ppermute | solution.py:492
  32.8 7.1 %collective-permute-start.11 = (bf16[32,896]{1,0:T(8,128)(2,1)S(1)}, bf16[32,896]{1,0:T(8,128)(2,1)S(1)}, u32[]{:S(2)}, u32[]{:S(2)}) collective-permute-start(bf16[32,896]{1,0:T(8,128)(2,1)S(1)} %get-tuple-element.51), channel_id=1, source_target_pairs={{0,192},{16,208},{32,224},{48,240},{64,128},{80,144},{96,160},{112... | collective-permute-start | bytes 172040 | tf_op jit(solution)/shard_map/ppermute | solution.py:492
  35.1 6.5 %collective-permute-start.12 = (bf16[32,896]{1,0:T(8,128)(2,1)S(1)}, bf16[32,896]{1,0:T(8,128)(2,1)S(1)}, u32[]{:S(2)}, u32[]{:S(2)}) collective-permute-start(bf16[32,896]{1,0:T(8,128)(2,1)S(1)} %get-tuple-element.52), channel_id=1, source_target_pairs={{0,208},{16,192},{32,240},{48,224},{64,144},{80,128},{96,176},{112... | collective-permute-start | bytes 172040 | tf_op jit(solution)/shard_map/ppermute | solution.py:492
  37.6 6.0 %collective-permute-start.13 = (bf16[32,896]{1,0:T(8,128)(2,1)S(1)}, bf16[32,896]{1,0:T(8,128)(2,1)S(1)}, u32[]{:S(2)}, u32[]{:S(2)}) collective-permute-start(bf16[32,896]{1,0:T(8,128)(2,1)S(1)} %get-tuple-element.53), channel_id=1, source_target_pairs={{0,224},{16,240},{32,192},{48,208},{64,160},{80,176},{96,128},{112... | collective-permute-start | bytes 172040 | tf_op jit(solution)/shard_map/ppermute | solution.py:492
  39.1 5.5 %collective-permute-start.14 = (bf16[32,896]{1,0:T(8,128)(2,1)S(1)}, bf16[32,896]{1,0:T(8,128)(2,1)}, u32[]{:S(2)}, u32[]{:S(2)}) collective-permute-start(bf16[32,896]{1,0:T(8,128)(2,1)S(1)} %get-tuple-element.54), channel_id=1, source_target_pairs={{0,240},{16,224},{32,208},{48,192},{64,176},{80,160},{96,144},{112... | collective-permute-start | bytes 172040 | tf_op jit(solution)/shard_map/ppermute | solution.py:492
  174.4 38.9 %all-to-all-start.4 = ((bf16[16,64,768]{2,1,0:T(8,128)(2,1)}), bf16[16,64,768]{2,1,0:T(8,128)(2,1)S(1)}, u32[]{:S(2)}, u32[]{:S(2)}) async-start(bf16[16,64,768]{2,1,0:T(8,128)(2,1)} %get-tuple-element.72), calls=%async_computation.4 | async-start | bytes 3145728 | tf_op jit(solution)/shard_map/all_to_all | solution.py:483
  180.0 9.3 %collective-permute-start.15 = (bf16[80,256]{1,0:T(8,128)(2,1)S(1)}, bf16[80,256]{1,0:T(8,128)(2,1)S(1)}, u32[]{:S(2)}, u32[]{:S(2)}) collective-permute-start(bf16[80,256]{1,0:T(8,128)(2,1)S(1)} %copy-done.20), channel_id=1, source_target_pairs={{0,0},{1,16},{2,32},{3,48},{4,64},{5,80},{6,96},{7,112},{8,128},{9... | collective-permute-start | bytes 122888 | tf_op jit(solution)/shard_map/ppermute | solution.py:488
  189.3 11.8 %collective-permute-start.18 = (bf16[80,256]{1,0:T(8,128)(2,1)S(1)}, bf16[80,256]{1,0:T(8,128)(2,1)S(1)}, u32[]{:S(2)}, u32[]{:S(2)}) collective-permute-start(bf16[80,256]{1,0:T(8,128)(2,1)S(1)} %collective-permute-done.15), channel_id=1, source_target_pairs={{0,12},{1,13},{2,14},{3,15},{4,8},{5,9},{6,10},{7,11},{8,4},{9,5},... | collective-permute-start | bytes 122888 | tf_op jit(solution)/shard_map/ppermute | solution.py:492
  192.6 8.4 %collective-permute-start.17 = (bf16[80,256]{1,0:T(8,128)(2,1)S(1)}, bf16[80,256]{1,0:T(8,128)(2,1)S(1)}, u32[]{:S(2)}, u32[]{:S(2)}) collective-permute-start(bf16[80,256]{1,0:T(8,128)(2,1)S(1)} %collective-permute-done.15), channel_id=1, source_target_pairs={{0,8},{1,9},{2,10},{3,11},{4,12},{5,13},{6,14},{7,15},{8,0},{9,1},... | collective-permute-start | bytes 122888 | tf_op jit(solution)/shard_map/ppermute | solution.py:492
  193.2 6.6 %collective-permute-start.16 = (bf16[80,256]{1,0:T(8,128)(2,1)S(1)}, bf16[80,256]{1,0:T(8,128)(2,1)S(1)}, u32[]{:S(2)}, u32[]{:S(2)}) collective-permute-start(bf16[80,256]{1,0:T(8,128)(2,1)S(1)} %collective-permute-done.15), channel_id=1, source_target_pairs={{0,4},{1,5},{2,6},{3,7},{4,0},{5,1},{6,2},{7,3},{8,12},{9,13},{10,... | collective-permute-start | bytes 122888 | tf_op jit(solution)/shard_map/ppermute | solution.py:492
  201.1 13.7 %collective-permute-start.21 = (bf16[320,256]{1,0:T(8,128)(2,1)S(1)}, bf16[320,256]{1,0:T(8,128)(2,1)S(1)}, u32[]{:S(2)}, u32[]{:S(2)}) collective-permute-start(bf16[320,256]{1,0:T(8,128)(2,1)S(1)} %constant_dynamic-update-slice_fusion.r0), channel_id=1, source_target_pairs={{0,3},{1,2},{2,1},{3,0},{4,7},{5,6},{6,5},{7,4},{8,11},{9,10},{10,... | collective-permute-start | bytes 491528 | tf_op jit(solution)/shard_map/ppermute | solution.py:492
  203.0 15.4 %collective-permute-start.20 = (bf16[320,256]{1,0:T(8,128)(2,1)S(1)}, bf16[320,256]{1,0:T(8,128)(2,1)S(1)}, u32[]{:S(2)}, u32[]{:S(2)}) collective-permute-start(bf16[320,256]{1,0:T(8,128)(2,1)S(1)} %constant_dynamic-update-slice_fusion.r0), channel_id=1, source_target_pairs={{0,2},{1,3},{2,0},{3,1},{4,6},{5,7},{6,4},{7,5},{8,10},{9,11},{10,... | collective-permute-start | bytes 491528 | tf_op jit(solution)/shard_map/ppermute | solution.py:492
  213.3 6.8 %collective-permute-start.19 = (bf16[320,256]{1,0:T(8,128)(2,1)S(1)}, bf16[320,256]{1,0:T(8,128)(2,1)S(1)}, u32[]{:S(2)}, u32[]{:S(2)}) collective-permute-start(bf16[320,256]{1,0:T(8,128)(2,1)S(1)} %constant_dynamic-update-slice_fusion.r0), channel_id=1, source_target_pairs={{0,1},{1,0},{2,3},{3,2},{4,5},{5,4},{6,7},{7,6},{8,9},{9,8},{10,11... | collective-permute-start | bytes 491528 | tf_op jit(solution)/shard_map/ppermute | solution.py:492
  (21 other events, 611.4 us)

commit v6 on v5

--- a/solution.py
+++ b/solution.py
@@ -104,8 +104,9 @@
     sent = []
     xn = xn_ref[...]
     half = ROWS // 2
+    for copy in tiles:
+        copy.wait()
     for index in range(3):
-        tiles[index].wait()
         rows = slice(256 * index, 256 * index + 256)
         for n in range(3):
             y = mm(xn, wv[index, :, 256 * n : 256 * n + 256])
@@ -260,7 +261,7 @@
     me_ref, mr_ref, f1_ref, f2_ref, wo_hbm, cq_hbm, ck_hbm, cv_hbm, co_hbm, *refs
 ):
     x_hbm, refs = refs[:N], refs[N:]
-    out_hbm, r_ref, ysc, xsc, qs, ks, vs, ms, weights, xb, ao, left, sems, out_sems = refs
+    out_ref, r_ref, ysc, xsc, qs, ks, vs, ms, weights, xb, sems = refs
     copies = []
     for k, w in enumerate((wo_hbm, cq_hbm, ck_hbm, cv_hbm, co_hbm)):
         for part in range(PARTS):
@@ -279,8 +280,12 @@
         copy.start()
 
     def weight(k):
-        for copy in copies[PARTS * k : PARTS * k + PARTS]:
-            copy.wait()
+        if k == 0:
+            for copy in copies[:PARTS] + fetch:
+                copy.wait()
+        if k == 1:
+            for copy in copies[PARTS:]:
+                copy.wait()
         return weights[k]
 
     halves = []
@@ -296,8 +301,6 @@
         )
     mixed = jnp.concatenate(halves, axis=0)
     ysc[...] = mm(mixed, weight(0)).reshape(2, N, 2, 8, E)
-    for copy in fetch:
-        copy.wait()
     xsc[...] = xb[...].astype(f32).reshape(N, 2, 2, 8, XW)
     blocks = []
     masks = []
@@ -339,9 +342,7 @@
         for s2 in range(2):
             at = SEQS * i + 128 * s2
             xsc[:, i, s2, :, :E] = out_wide[at : at + 128].reshape(N, 8, E)
-    ao[...] = xsc[:, :, :, :, :E].reshape(N, I, E).astype(bf16)
-    sent = [pltpu.make_async_copy(ao, out_hbm.at[:, pl.ds(0, I)], out_sems.at[N])]
-    sent[0].start()
+    out_ref[:, :I] = xsc[:, :, :, :, :E].reshape(N, I, E).astype(bf16)
 
     f = jnp.concatenate([f1_ref[...], f2_ref[...]], axis=0)
     factors = (mmt(f, norm(out_wide)) * alive[0:1, :]).astype(bf16)
@@ -354,19 +355,16 @@
     row = lax.broadcasted_iota(jnp.int32, (C, SEQS), 0)
     count = jnp.where(row == 0, counts[0], counts[1]).astype(bf16)
     r_ref[2 * C :, :] = count[: RW - 2 * C, :]
-    left[...] = jnp.concatenate([factors[:C, :], count], axis=1)
+    left = jnp.concatenate([factors[:C, :], count], axis=1)
     for k in range(N):
-        sent.append(pltpu.make_async_copy(left, out_hbm.at[k, pl.ds(I, C)], out_sems.at[k]))
-        sent[-1].start()
-    for copy in sent:
-        copy.wait()
+        out_ref[k, I:] = left
 
 
 def column_step(me, mr, f1, f2, wo, cq, ck, cv, co, xs):
     return pl.pallas_call(
         column_kernel,
         in_specs=[pl.BlockSpec(memory_space=pltpu.SMEM)] + whole(3) + [HBM] * (5 + N),
-        out_specs=[HBM, pl.BlockSpec(memory_space=pltpu.VMEM)],
+        out_specs=whole(2),
         out_shape=[
             jax.ShapeDtypeStruct((N, 2 * I, E), bf16),
             jax.ShapeDtypeStruct((RW, SEQS), bf16),
@@ -380,10 +378,7 @@
             pltpu.VMEM((ROWS, E), bf16),
             pltpu.VMEM((5, E, E), bf16),
             pltpu.VMEM((N, I, XW), bf16),
-            pltpu.VMEM((N, I, E), bf16),
-            pltpu.VMEM((C, E), bf16),
             pltpu.SemaphoreType.DMA((5 * PARTS + N,)),
-            pltpu.SemaphoreType.DMA((N + 1,)),
         ],
         compiler_params=params(59),
         cost_estimate=cost(5 * 2 * ROWS * E * E, 9_000_000, 2 * H * SEQS * SEQS),
@@ -412,11 +407,13 @@
 
 def pair_kernel(
     me_ref, l_ref, r0, r1, r2, r3, wp_ref, out_ref,
-    l0, l1, l2, l3, l4, lp, lhs, osc, wk, r_ref,
+    l0, l1, l2, l3, l4, lp, lhs, osc, wk, r_ref, n_ref,
 ):
     for near, ref in enumerate((r0, r1, r2, r3)):
         for far in range(4):
-            r_ref[jnp.bitwise_xor(me_ref[1], 4 * far + near)] = ref[RW * far : RW * far + RW]
+            at = jnp.bitwise_xor(me_ref[1], 4 * far + near)
+            r_ref[at] = ref[2 * C * far : 2 * C * far + 2 * C]
+            n_ref[at] = ref[8 * C + 4 * far : 8 * C + 4 * far + 4, :128].astype(f32)
     wk[...] = jnp.zeros_like(wk)
     for c in range(C):
         w = wp_ref[C * c : C * c + C, :]
@@ -435,7 +432,7 @@
         lp[rows, :128] = jnp.concatenate([across(l0, c), across(l2, c)], axis=0).astype(bf16)
         lp[rows, 128:] = jnp.concatenate([across(l1, c), across(l3, c)], axis=0).astype(bf16)
     left_count = jnp.concatenate([across(l4, 0), across(l4, 1)], axis=0)
-    right = r_ref[:, : 2 * C, :].reshape(N * 2 * C, SEQS)
+    right = r_ref[...].reshape(N * 2 * C, SEQS)
     for c in range(0, C, 4):
         outer = mmt(lp[C * c : C * c + 4 * C, :], right).astype(bf16)
         for k in range(4):
@@ -444,7 +441,7 @@
                     C * k : C * k + C, 128 * j : 128 * j + 128
                 ]
     acc = mm(lhs[...], wk[...])
-    right_count = r_ref[:, 2 * C :, :128].astype(f32)
+    right_count = n_ref[...]
     for j in range(C):
         part = acc[C * (j // 4) : C * (j // 4) + C, 128 * (j % 4) : 128 * (j % 4) + 128]
         count = right_count[j // 2, j % 2 : j % 2 + 1, :]
@@ -462,7 +459,7 @@
             pl.BlockSpec(memory_space=pltpu.SMEM),
             pl.BlockSpec((N, I, E), lambda n: (0, 1, 0)),
         ]
-        + [pl.BlockSpec((4 * RW, SEQS), lambda n: (0, 0))] * 4
+        + [pl.BlockSpec((8 * C + 16, SEQS), lambda n: (0, 0))] * 4
         + [pl.BlockSpec((C * C, PC), lambda n: (0, 0))],
         out_specs=pl.BlockSpec((C * C, PC), lambda n: (0, 0)),
         out_shape=jax.ShapeDtypeStruct((C * C, PC), bf16),
@@ -472,7 +469,8 @@
             pltpu.VMEM((256, 4096), bf16),
             pltpu.VMEM((1024, PC), f32),
             pltpu.VMEM((4096, 512), bf16),
-            pltpu.VMEM((N, RW, SEQS), bf16),
+            pltpu.VMEM((N, 2 * C, SEQS), bf16),
+            pltpu.VMEM((N, 4, 128), f32),
         ],
         compiler_params=params(24),
         cost_estimate=cost(2 * 1024 * 1024 * 256 + 2 * 256 * 4096 * 512, 6_000_000),
@@ -514,7 +512,8 @@
     both = exchange(both, "depth")
     right = swap(right)
     far = [right] + [mirror(right, 4 * k, "cols") for k in range(1, 4)]
-    far = jnp.concatenate(far, axis=0)
+    counts = [part[2 * C : 2 * C + 4] for part in far]
+    far = jnp.concatenate([part[: 2 * C] for part in far] + counts, axis=0)
     rights = [far] + [mirror(far, k, "cols") for k in range(1, 4)]
     out = back(both)
     pair = pair_step(me, both, rights, wp)

time: 225 us -> 223 us (level)
  transfers between devices with their start and end apart: 24 -> 24, of which waited for: 11 -> 10; matrix products, arithmetic and copies ran while one was open for 0% -> 0% of each run, Pallas kernels for 1% -> 1%
where the time goes in v6:
time: 223 us
  waiting for transfers between devices  70.7 us (32%)
  blocking collectives  65 us (29%)
  starting transfers between devices  55.1 us (25%)
  Pallas kernels  28.5 us (13%)
  local copies, waits for them, and re-layouts  2.54 us (1%)
    all_to_all x3, blocking collectives, exchange(): return lax.all_to_all(x, axis, split_axis=0, concat_axis=0, tiled=True)  65 us
    all_to_all x2, waiting for transfers between devices, exchange(): return lax.all_to_all(x, axis, split_axis=0, concat_axis=0, tiled=True)  48.5 us
    ppermute x21, starting transfers between devices, mirror(): return lax.ppermute(x, axis, [(d, d ^ k) for d in range(N)])  36.2 us
    all_to_all x2, starting transfers between devices, exchange(): return lax.all_to_all(x, axis, split_axis=0, concat_axis=0, tiled=True)  16.7 us
    ppermute x21, waiting for transfers between devices, mirror(): return lax.ppermute(x, axis, [(d, d ^ k) for d in range(N)])  15.2 us
    pallas_call x1, Pallas kernels, column_step(): pl.pallas_call(column_kernel, in_specs=[pl.BlockSpec(memory_space=pltpu.S...  12.3 us
    ppermute x1, waiting for transfers between devices, swap(): return lax.ppermute(x, ('depth', 'cols'), pairs)  7.04 us
    pallas_call x1, Pallas kernels, row_proj(): pl.pallas_call(row_proj_kernel, in_specs=[HBM] * 5, out_specs=HBM, out_sh...  6.46 us
  transfers between devices with their start and end apart: 24, of which 10 were waited for; matrix products, arithmetic and copies ran while one was open for 0% of the time, Pallas kernels for 1%

profile of v6, /device:TPU:4, one launch (start us, length us, event | category | flops | bytes accessed | tf_op | source)
XLA Modules:
  0.0 223.0 jit_solution(17276023493294204259)
XLA Ops:
  0.6 6.5 %shard_map.140 = bf16[16,768,128]{2,1,0:T(8,128)(2,1)} custom-call(bf16[512,768]{1,0:T(8,128)(2,1)} %bitcast.12, s32[16,32]{1,0:T(8,128)} %occ_ref.1, bf16[768,768]{1,0:T(8,128)(2,1)} %wq_hbm.1, bf16[768,768]{1,0:T(8,128)(2,1)} %wk_hbm.1, bf16[768,768]{1,0:T(8,128)(2,1)} %wv_hbm.1), custom_call_target="tpu_custom_call" | custom-call | flops 1811939328 | bytes 8000000 | tf_op jit(solution)/shard_map/pallas_call | solution.py:133
  7.1 11.2 %all-to-all-start = ((bf16[16,768,128]{2,1,0:T(8,128)(2,1)}), bf16[16,768,128]{2,1,0:T(8,128)(2,1)S(1)}, u32[]{:S(2)}, u32[]{:S(2)}) async-start(bf16[16,768,128]{2,1,0:T(8,128)(2,1)} %shard_map.140), calls=%async_computation | async-start | bytes 6291456 | tf_op jit(solution)/shard_map/all_to_all | solution.py:481
  24.0 2.6 %collective-permute-start.4 = (bf16[32,896]{1,0:T(8,128)(2,1)S(1)}, bf16[32,896]{1,0:T(8,128)(2,1)S(1)}, u32[]{:S(2)}, u32[]{:S(2)}) collective-permute-start(bf16[32,896]{1,0:T(8,128)(2,1)S(1)} %get-tuple-element.44), channel_id=1, source_target_pairs={{0,80},{16,64},{32,112},{48,96},{64,16},{80,0},{96,48},{112,32},{1... | collective-permute-start | bytes 172040 | tf_op jit(solution)/shard_map/ppermute | solution.py:490
  30.2 2.5 %collective-permute-start.9 = (bf16[32,896]{1,0:T(8,128)(2,1)S(1)}, bf16[32,896]{1,0:T(8,128)(2,1)S(1)}, u32[]{:S(2)}, u32[]{:S(2)}) collective-permute-start(bf16[32,896]{1,0:T(8,128)(2,1)S(1)} %get-tuple-element.49), channel_id=1, source_target_pairs={{0,160},{16,176},{32,128},{48,144},{64,224},{80,240},{96,192},{112... | collective-permute-start | bytes 172040 | tf_op jit(solution)/shard_map/ppermute | solution.py:490
  32.9 2.4 %collective-permute-start.11 = (bf16[32,896]{1,0:T(8,128)(2,1)S(1)}, bf16[32,896]{1,0:T(8,128)(2,1)S(1)}, u32[]{:S(2)}, u32[]{:S(2)}) collective-permute-start(bf16[32,896]{1,0:T(8,128)(2,1)S(1)} %get-tuple-element.51), channel_id=1, source_target_pairs={{0,192},{16,208},{32,224},{48,240},{64,128},{80,144},{96,160},{112... | collective-permute-start | bytes 172040 | tf_op jit(solution)/shard_map/ppermute | solution.py:490
  35.3 2.5 %collective-permute-start.12 = (bf16[32,896]{1,0:T(8,128)(2,1)S(1)}, bf16[32,896]{1,0:T(8,128)(2,1)S(1)}, u32[]{:S(2)}, u32[]{:S(2)}) collective-permute-start(bf16[32,896]{1,0:T(8,128)(2,1)S(1)} %get-tuple-element.52), channel_id=1, source_target_pairs={{0,208},{16,192},{32,240},{48,224},{64,144},{80,128},{96,176},{112... | collective-permute-start | bytes 172040 | tf_op jit(solution)/shard_map/ppermute | solution.py:490
  40.0 1.8 collective-permute-done.12.refs_13_
  41.8 2.0 collective-permute-done.13.refs_14_
  44.8 48.5 %all-to-all-done.qk_ref.v_ref = bf16[16,768,128]{2,1,0:T(8,128)(2,1)S(1)} async-done(((bf16[16,768,128]{2,1,0:T(8,128)(2,1)}), bf16[16,768,128]{2,1,0:T(8,128)(2,1)S(1)}, u32[]{:S(2)}, u32[]{:S(2)}) %all-to-all-start) | async-done | bytes 3145760 | tf_op jit(solution)/shard_map/all_to_all | solution.py:481
  94.1 12.2 %all_to_all.25.in_ref = bf16[16,32,512]{2,1,0:T(8,128)(2,1)S(1)} all-to-all(bf16[16,32,512]{2,1,0:T(8,128)(2,1)S(1)} %bitcast.11), channel_id=1, replica_groups=mesh['depth'=16,'cols'=16] {'depth'}, dimensions={0} | all-to-all | bytes 1048576 | tf_op jit(solution)/shard_map/all_to_all | solution.py:481
  106.6 13.4 %all_to_all.26.p_ref = bf16[16,32,512]{2,1,0:T(8,128)(2,1)S(1)} all-to-all(bf16[16,32,512]{2,1,0:T(8,128)(2,1)S(1)} %shard_map.143), channel_id=1, replica_groups=mesh['depth'=16,'cols'=16] {'depth'}, dimensions={0} | all-to-all | bytes 1048576 | tf_op jit(solution)/shard_map/all_to_all | solution.py:481
  121.1 39.4 %all_to_all.27 = bf16[256,16,128]{2,1,0:T(8,128)(2,1)} all-to-all(bf16[256,16,128]{2,1,0:T(8,128)(2,1)S(1)} %bitcast.10), channel_id=1, replica_groups=mesh['depth'=16,'cols'=16] {'cols','depth'}, dimensions={0} | all-to-all | bytes 2097152 | tf_op jit(solution)/shard_map/all_to_all | solution.py:481
  160.5 12.3 %shard_map.145 = (bf16[16,64,768]{2,1,0:T(8,128)(2,1)}, bf16[80,256]{1,0:T(8,128)(2,1)}) custom-call(s32[2]{0:T(128)} %copy-done.3, bf16[4096,128]{1,0:T(8,128)(2,1)} %bitcast.14, bf16[32,768]{1,0:T(8,128)(2,1)} %bitcast.16, bf16[32,768]{1,0:T(8,128)(2,1)} %bitcast.17, bf16[768,768]{1,0:T(8,128)(2,1)} %wo_hbm.1, bf16[768,768]{1,0:T(8,128)(2,1)} %cq_hbm.1, ...), custom_call_target="tpu_custom_call" | custom-call | flops 3019898880 | bytes 9000000 | tf_op jit(solution)/shard_map/pallas_call | solution.py:364
  172.9 5.5 %all-to-all-start.4 = ((bf16[16,64,768]{2,1,0:T(8,128)(2,1)}), bf16[16,64,768]{2,1,0:T(8,128)(2,1)S(1)}, u32[]{:S(2)}, u32[]{:S(2)}) async-start(bf16[16,64,768]{2,1,0:T(8,128)(2,1)} %get-tuple-element.72), calls=%async_computation.4 | async-start | bytes 3145728 | tf_op jit(solution)/shard_map/all_to_all | solution.py:481
  178.4 2.2 %collective-permute-start.15 = (bf16[80,256]{1,0:T(8,128)(2,1)S(1)}, bf16[80,256]{1,0:T(8,128)(2,1)S(1)}, u32[]{:S(2)}, u32[]{:S(2)}) collective-permute-start(bf16[80,256]{1,0:T(8,128)(2,1)S(1)} %copy-done.20), channel_id=1, source_target_pairs={{0,0},{1,16},{2,32},{3,48},{4,64},{5,80},{6,96},{7,112},{8,128},{9... | collective-permute-start | bytes 122888 | tf_op jit(solution)/shard_map/ppermute | solution.py:486
  180.7 7.0 %collective-permute-done.15 = bf16[80,256]{1,0:T(8,128)(2,1)S(1)} collective-permute-done((bf16[80,256]{1,0:T(8,128)(2,1)S(1)}, bf16[80,256]{1,0:T(8,128)(2,1)S(1)}, u32[]{:S(2)}, u32[]{:S(2)}) %collective-permute-start.15) | collective-permute-done | bytes 40992 | tf_op jit(solution)/shard_map/ppermute | solution.py:486
  187.7 3.4 %collective-permute-start.18 = (bf16[80,256]{1,0:T(8,128)(2,1)S(1)}, bf16[80,256]{1,0:T(8,128)(2,1)S(1)}, u32[]{:S(2)}, u32[]{:S(2)}) collective-permute-start(bf16[80,256]{1,0:T(8,128)(2,1)S(1)} %collective-permute-done.15), channel_id=1, source_target_pairs={{0,12},{1,13},{2,14},{3,15},{4,8},{5,9},{6,10},{7,11},{8,4},{9,5},... | collective-permute-start | bytes 122888 | tf_op jit(solution)/shard_map/ppermute | solution.py:490
  191.6 2.6 %collective-permute-start.16 = (bf16[80,256]{1,0:T(8,128)(2,1)S(1)}, bf16[80,256]{1,0:T(8,128)(2,1)S(1)}, u32[]{:S(2)}, u32[]{:S(2)}) collective-permute-start(bf16[80,256]{1,0:T(8,128)(2,1)S(1)} %collective-permute-done.15), channel_id=1, source_target_pairs={{0,4},{1,5},{2,6},{3,7},{4,0},{5,1},{6,2},{7,3},{8,12},{9,13},{10,... | collective-permute-start | bytes 122888 | tf_op jit(solution)/shard_map/ppermute | solution.py:490
  194.2 5.3 %collective-permute-done.17 = bf16[80,256]{1,0:T(8,128)(2,1)S(1)} collective-permute-done((bf16[80,256]{1,0:T(8,128)(2,1)S(1)}, bf16[80,256]{1,0:T(8,128)(2,1)S(1)}, u32[]{:S(2)}, u32[]{:S(2)}) %collective-permute-start.17) | collective-permute-done | bytes 40992 | tf_op jit(solution)/shard_map/ppermute | solution.py:490
  199.6 1.9 collective-permute-start.21
  201.5 10.2 %collective-permute-start.20 = (bf16[272,256]{1,0:T(8,128)(2,1)S(1)}, bf16[272,256]{1,0:T(8,128)(2,1)S(1)}, u32[]{:S(2)}, u32[]{:S(2)}) collective-permute-start(bf16[272,256]{1,0:T(8,128)(2,1)S(1)} %concatenate.3.r0), channel_id=1, source_target_pairs={{0,2},{1,3},{2,0},{3,1},{4,6},{5,7},{6,4},{7,5},{8,10},{9,11},{10,... | collective-permute-start | bytes 417800 | tf_op jit(solution)/shard_map/ppermute | solution.py:490
  213.2 3.1 %collective-permute-done.20.r2 = bf16[272,256]{1,0:T(8,128)(2,1)S(1)} collective-permute-done((bf16[272,256]{1,0:T(8,128)(2,1)S(1)}, bf16[272,256]{1,0:T(8,128)(2,1)S(1)}, u32[]{:S(2)}, u32[]{:S(2)}) %collective-permute-start.20) | collective-permute-done | bytes 139296 | tf_op jit(solution)/shard_map/ppermute | solution.py:490
  216.3 2.0 collective-permute-done.19.r1
  218.3 4.6 %shard_map.147 = bf16[1024,128]{1,0:T(8,128)(2,1)} custom-call(s32[2]{0:T(128)S(1)} %copy-done.4, bf16[16,64,768]{2,1,0:T(8,128)(2,1)S(1)} %all-to-all-done.4.in_ref.l_ref, bf16[272,256]{1,0:T(8,128)(2,1)S(1)} %concatenate.3.r0, bf16[272,256]{1,0:T(8,128)(2,1)S(1)} %collective-permute-done.19.r1, bf16[272,256]{1,0:T(8,128)(2,1)S(1)} %collective-permute-done.20.r2, ...), custom_call_target="tpu_custom_call" | custom-call | flops 1610612736 | bytes 6000000 | tf_op jit(solution)/shard_map/pallas_call | solution.py:455
  (87 shorter events, 16.9 us)
Async XLA Ops:
  7.1 86.1 %all-to-all-start = ((bf16[16,768,128]{2,1,0:T(8,128)(2,1)}), bf16[16,768,128]{2,1,0:T(8,128)(2,1)S(1)}, u32[]{:S(2)}, u32[]{:S(2)}) async-start(bf16[16,768,128]{2,1,0:T(8,128)(2,1)} %shard_map.140), calls=%async_computation | async-start | bytes 6291456 | tf_op jit(solution)/shard_map/all_to_all | solution.py:481
  21.7 5.0 %collective-permute-start = (bf16[32,896]{1,0:T(8,128)(2,1)S(1)}, bf16[32,896]{1,0:T(8,128)(2,1)S(1)}, u32[]{:S(2)}, u32[]{:S(2)}) collective-permute-start(bf16[32,896]{1,0:T(8,128)(2,1)S(1)} %get-tuple-element.40), channel_id=1, source_target_pairs={{0,16},{16,0},{32,48},{48,32},{64,80},{80,64},{96,112},{112,96},{1... | collective-permute-start | bytes 172040 | tf_op jit(solution)/shard_map/ppermute | solution.py:490
  21.7 5.5 %collective-permute-start.1 = (bf16[32,896]{1,0:T(8,128)(2,1)S(1)}, bf16[32,896]{1,0:T(8,128)(2,1)S(1)}, u32[]{:S(2)}, u32[]{:S(2)}) collective-permute-start(bf16[32,896]{1,0:T(8,128)(2,1)S(1)} %get-tuple-element.41), channel_id=1, source_target_pairs={{0,32},{16,48},{32,0},{48,16},{64,96},{80,112},{96,64},{112,80},{1... | collective-permute-start | bytes 172040 | tf_op jit(solution)/shard_map/ppermute | solution.py:490
  22.9 5.7 %collective-permute-start.2 = (bf16[32,896]{1,0:T(8,128)(2,1)S(1)}, bf16[32,896]{1,0:T(8,128)(2,1)S(1)}, u32[]{:S(2)}, u32[]{:S(2)}) collective-permute-start(bf16[32,896]{1,0:T(8,128)(2,1)S(1)} %get-tuple-element.42), channel_id=1, source_target_pairs={{0,48},{16,32},{32,16},{48,0},{64,112},{80,96},{96,80},{112,64},{1... | collective-permute-start | bytes 172040 | tf_op jit(solution)/shard_map/ppermute | solution.py:490
  23.5 6.2 %collective-permute-start.3 = (bf16[32,896]{1,0:T(8,128)(2,1)S(1)}, bf16[32,896]{1,0:T(8,128)(2,1)S(1)}, u32[]{:S(2)}, u32[]{:S(2)}) collective-permute-start(bf16[32,896]{1,0:T(8,128)(2,1)S(1)} %get-tuple-element.43), channel_id=1, source_target_pairs={{0,64},{16,80},{32,96},{48,112},{64,0},{80,16},{96,32},{112,48},{1... | collective-permute-start | bytes 172040 | tf_op jit(solution)/shard_map/ppermute | solution.py:490
  24.0 6.2 %collective-permute-start.4 = (bf16[32,896]{1,0:T(8,128)(2,1)S(1)}, bf16[32,896]{1,0:T(8,128)(2,1)S(1)}, u32[]{:S(2)}, u32[]{:S(2)}) collective-permute-start(bf16[32,896]{1,0:T(8,128)(2,1)S(1)} %get-tuple-element.44), channel_id=1, source_target_pairs={{0,80},{16,64},{32,112},{48,96},{64,16},{80,0},{96,48},{112,32},{1... | collective-permute-start | bytes 172040 | tf_op jit(solution)/shard_map/ppermute | solution.py:490
  26.7 6.0 %collective-permute-start.5 = (bf16[32,896]{1,0:T(8,128)(2,1)S(1)}, bf16[32,896]{1,0:T(8,128)(2,1)S(1)}, u32[]{:S(2)}, u32[]{:S(2)}) collective-permute-start(bf16[32,896]{1,0:T(8,128)(2,1)S(1)} %get-tuple-element.45), channel_id=1, source_target_pairs={{0,96},{16,112},{32,64},{48,80},{64,32},{80,48},{96,0},{112,16},{1... | collective-permute-start | bytes 172040 | tf_op jit(solution)/shard_map/ppermute | solution.py:490
  27.2 5.7 %collective-permute-start.6 = (bf16[32,896]{1,0:T(8,128)(2,1)S(1)}, bf16[32,896]{1,0:T(8,128)(2,1)S(1)}, u32[]{:S(2)}, u32[]{:S(2)}) collective-permute-start(bf16[32,896]{1,0:T(8,128)(2,1)S(1)} %get-tuple-element.46), channel_id=1, source_target_pairs={{0,112},{16,96},{32,80},{48,64},{64,48},{80,32},{96,16},{112,0},{1... | collective-permute-start | bytes 172040 | tf_op jit(solution)/shard_map/ppermute | solution.py:490
  28.5 6.8 %collective-permute-start.7 = (bf16[32,896]{1,0:T(8,128)(2,1)S(1)}, bf16[32,896]{1,0:T(8,128)(2,1)S(1)}, u32[]{:S(2)}, u32[]{:S(2)}) collective-permute-start(bf16[32,896]{1,0:T(8,128)(2,1)S(1)} %get-tuple-element.47), channel_id=1, source_target_pairs={{0,128},{16,144},{32,160},{48,176},{64,192},{80,208},{96,224},{112... | collective-permute-start | bytes 172040 | tf_op jit(solution)/shard_map/ppermute | solution.py:490
  29.7 8.0 %collective-permute-start.8 = (bf16[32,896]{1,0:T(8,128)(2,1)S(1)}, bf16[32,896]{1,0:T(8,128)(2,1)S(1)}, u32[]{:S(2)}, u32[]{:S(2)}) collective-permute-start(bf16[32,896]{1,0:T(8,128)(2,1)S(1)} %get-tuple-element.48), channel_id=1, source_target_pairs={{0,144},{16,128},{32,176},{48,160},{64,208},{80,192},{96,240},{112... | collective-permute-start | bytes 172040 | tf_op jit(solution)/shard_map/ppermute | solution.py:490
  30.2 9.1 %collective-permute-start.9 = (bf16[32,896]{1,0:T(8,128)(2,1)S(1)}, bf16[32,896]{1,0:T(8,128)(2,1)S(1)}, u32[]{:S(2)}, u32[]{:S(2)}) collective-permute-start(bf16[32,896]{1,0:T(8,128)(2,1)S(1)} %get-tuple-element.49), channel_id=1, source_target_pairs={{0,160},{16,176},{32,128},{48,144},{64,224},{80,240},{96,192},{112... | collective-permute-start | bytes 172040 | tf_op jit(solution)/shard_map/ppermute | solution.py:490
  32.7 7.1 %collective-permute-start.10 = (bf16[32,896]{1,0:T(8,128)(2,1)S(1)}, bf16[32,896]{1,0:T(8,128)(2,1)S(1)}, u32[]{:S(2)}, u32[]{:S(2)}) collective-permute-start(bf16[32,896]{1,0:T(8,128)(2,1)S(1)} %get-tuple-element.50), channel_id=1, source_target_pairs={{0,176},{16,160},{32,144},{48,128},{64,240},{80,224},{96,208},{112... | collective-permute-start | bytes 172040 | tf_op jit(solution)/shard_map/ppermute | solution.py:490
  32.9 7.1 %collective-permute-start.11 = (bf16[32,896]{1,0:T(8,128)(2,1)S(1)}, bf16[32,896]{1,0:T(8,128)(2,1)S(1)}, u32[]{:S(2)}, u32[]{:S(2)}) collective-permute-start(bf16[32,896]{1,0:T(8,128)(2,1)S(1)} %get-tuple-element.51), channel_id=1, source_target_pairs={{0,192},{16,208},{32,224},{48,240},{64,128},{80,144},{96,160},{112... | collective-permute-start | bytes 172040 | tf_op jit(solution)/shard_map/ppermute | solution.py:490
  35.3 6.5 %collective-permute-start.12 = (bf16[32,896]{1,0:T(8,128)(2,1)S(1)}, bf16[32,896]{1,0:T(8,128)(2,1)S(1)}, u32[]{:S(2)}, u32[]{:S(2)}) collective-permute-start(bf16[32,896]{1,0:T(8,128)(2,1)S(1)} %get-tuple-element.52), channel_id=1, source_target_pairs={{0,208},{16,192},{32,240},{48,224},{64,144},{80,128},{96,176},{112... | collective-permute-start | bytes 172040 | tf_op jit(solution)/shard_map/ppermute | solution.py:490
  37.8 6.0 %collective-permute-start.13 = (bf16[32,896]{1,0:T(8,128)(2,1)S(1)}, bf16[32,896]{1,0:T(8,128)(2,1)S(1)}, u32[]{:S(2)}, u32[]{:S(2)}) collective-permute-start(bf16[32,896]{1,0:T(8,128)(2,1)S(1)} %get-tuple-element.53), channel_id=1, source_target_pairs={{0,224},{16,240},{32,192},{48,208},{64,160},{80,176},{96,128},{112... | collective-permute-start | bytes 172040 | tf_op jit(solution)/shard_map/ppermute | solution.py:490
  39.3 5.5 %collective-permute-start.14 = (bf16[32,896]{1,0:T(8,128)(2,1)S(1)}, bf16[32,896]{1,0:T(8,128)(2,1)}, u32[]{:S(2)}, u32[]{:S(2)}) collective-permute-start(bf16[32,896]{1,0:T(8,128)(2,1)S(1)} %get-tuple-element.54), channel_id=1, source_target_pairs={{0,240},{16,224},{32,208},{48,192},{64,176},{80,160},{96,144},{112... | collective-permute-start | bytes 172040 | tf_op jit(solution)/shard_map/ppermute | solution.py:490
  172.9 38.9 %all-to-all-start.4 = ((bf16[16,64,768]{2,1,0:T(8,128)(2,1)}), bf16[16,64,768]{2,1,0:T(8,128)(2,1)S(1)}, u32[]{:S(2)}, u32[]{:S(2)}) async-start(bf16[16,64,768]{2,1,0:T(8,128)(2,1)} %get-tuple-element.72), calls=%async_computation.4 | async-start | bytes 3145728 | tf_op jit(solution)/shard_map/all_to_all | solution.py:481
  178.4 9.3 %collective-permute-start.15 = (bf16[80,256]{1,0:T(8,128)(2,1)S(1)}, bf16[80,256]{1,0:T(8,128)(2,1)S(1)}, u32[]{:S(2)}, u32[]{:S(2)}) collective-permute-start(bf16[80,256]{1,0:T(8,128)(2,1)S(1)} %copy-done.20), channel_id=1, source_target_pairs={{0,0},{1,16},{2,32},{3,48},{4,64},{5,80},{6,96},{7,112},{8,128},{9... | collective-permute-start | bytes 122888 | tf_op jit(solution)/shard_map/ppermute | solution.py:486
  187.7 6.5 %collective-permute-start.18 = (bf16[80,256]{1,0:T(8,128)(2,1)S(1)}, bf16[80,256]{1,0:T(8,128)(2,1)S(1)}, u32[]{:S(2)}, u32[]{:S(2)}) collective-permute-start(bf16[80,256]{1,0:T(8,128)(2,1)S(1)} %collective-permute-done.15), channel_id=1, source_target_pairs={{0,12},{1,13},{2,14},{3,15},{4,8},{5,9},{6,10},{7,11},{8,4},{9,5},... | collective-permute-start | bytes 122888 | tf_op jit(solution)/shard_map/ppermute | solution.py:490
  191.1 8.4 %collective-permute-start.17 = (bf16[80,256]{1,0:T(8,128)(2,1)S(1)}, bf16[80,256]{1,0:T(8,128)(2,1)S(1)}, u32[]{:S(2)}, u32[]{:S(2)}) collective-permute-start(bf16[80,256]{1,0:T(8,128)(2,1)S(1)} %collective-permute-done.15), channel_id=1, source_target_pairs={{0,8},{1,9},{2,10},{3,11},{4,12},{5,13},{6,14},{7,15},{8,0},{9,1},... | collective-permute-start | bytes 122888 | tf_op jit(solution)/shard_map/ppermute | solution.py:490
  191.6 7.9 %collective-permute-start.16 = (bf16[80,256]{1,0:T(8,128)(2,1)S(1)}, bf16[80,256]{1,0:T(8,128)(2,1)S(1)}, u32[]{:S(2)}, u32[]{:S(2)}) collective-permute-start(bf16[80,256]{1,0:T(8,128)(2,1)S(1)} %collective-permute-done.15), channel_id=1, source_target_pairs={{0,4},{1,5},{2,6},{3,7},{4,0},{5,1},{6,2},{7,3},{8,12},{9,13},{10,... | collective-permute-start | bytes 122888 | tf_op jit(solution)/shard_map/ppermute | solution.py:490
  199.6 13.6 %collective-permute-start.21 = (bf16[272,256]{1,0:T(8,128)(2,1)S(1)}, bf16[272,256]{1,0:T(8,128)(2,1)S(1)}, u32[]{:S(2)}, u32[]{:S(2)}) collective-permute-start(bf16[272,256]{1,0:T(8,128)(2,1)S(1)} %concatenate.3.r0), channel_id=1, source_target_pairs={{0,3},{1,2},{2,1},{3,0},{4,7},{5,6},{6,5},{7,4},{8,11},{9,10},{10,... | collective-permute-start | bytes 417800 | tf_op jit(solution)/shard_map/ppermute | solution.py:490
  201.5 14.8 %collective-permute-start.20 = (bf16[272,256]{1,0:T(8,128)(2,1)S(1)}, bf16[272,256]{1,0:T(8,128)(2,1)S(1)}, u32[]{:S(2)}, u32[]{:S(2)}) collective-permute-start(bf16[272,256]{1,0:T(8,128)(2,1)S(1)} %concatenate.3.r0), channel_id=1, source_target_pairs={{0,2},{1,3},{2,0},{3,1},{4,6},{5,7},{6,4},{7,5},{8,10},{9,11},{10,... | collective-permute-start | bytes 417800 | tf_op jit(solution)/shard_map/ppermute | solution.py:490
  211.7 6.6 %collective-permute-start.19 = (bf16[272,256]{1,0:T(8,128)(2,1)S(1)}, bf16[272,256]{1,0:T(8,128)(2,1)S(1)}, u32[]{:S(2)}, u32[]{:S(2)}) collective-permute-start(bf16[272,256]{1,0:T(8,128)(2,1)S(1)} %concatenate.3.r0), channel_id=1, source_target_pairs={{0,1},{1,0},{2,3},{3,2},{4,5},{5,4},{6,7},{7,6},{8,9},{9,8},{10,11... | collective-permute-start | bytes 417800 | tf_op jit(solution)/shard_map/ppermute | solution.py:490
  (21 other events, 560.4 us)

commit v7 on v6

--- a/solution.py
+++ b/solution.py
@@ -23,7 +23,7 @@
 PC = 128
 XW = E + 128
 RW = 80
-PARTS = 2
+PARTS = 1
 
 NT = (((1,), (1,)), ((), ()))
 
@@ -91,16 +91,14 @@
         pltpu.make_async_copy(w, wv.at[k], sems.at[5 + k])
         for k, w in enumerate((wq_hbm, wk_hbm, wv_hbm))
     ]
+    for copy in tiles:
+        copy.start()
     first[0].wait()
     live = mask_rows(occ[...], 128)
     for k in range(4):
         first[1 + k].wait()
-        if k == 0:
-            tiles[0].start()
         rows = slice(128 * k, 128 * k + 128)
         xn_ref[rows] = norm(xv[rows].astype(f32))
-    for copy in tiles[1:]:
-        copy.start()
     sent = []
     xn = xn_ref[...]
     half = ROWS // 2
@@ -332,8 +330,8 @@
                 logits = mmt(jnp.where(own, q, jnp.zeros_like(q)), k) * 0.125
                 logits = jnp.where(keep, logits, -1000000000.0)
                 e = jnp.exp(logits - jnp.max(logits, axis=-1, keepdims=True))
-                p = (e * (1.0 / jnp.sum(e, axis=-1, keepdims=True))).astype(bf16)
-                mixes.append(mm(p, v))
+                total = jnp.sum(e, axis=-1, keepdims=True)
+                mixes.append(mm(e.astype(bf16), v) * (1.0 / total))
             ms[rows, lanes] = jnp.where(low, mixes[0], mixes[1]).astype(bf16)
 
     out = (wide + mm(ms[...], weight(4))).astype(bf16)

time: 223 us -> 222 us (level)
  no operation moved by 1% of the time
where the time goes in v7:
time: 222 us; the launch traced here: 221 us
  waiting for transfers between devices  70.7 us (32%)
  blocking collectives  65 us (29%)
  starting transfers between devices  55.4 us (25%)
  Pallas kernels  26.5 us (12%)
  local copies, waits for them, and re-layouts  2.54 us (1%)
    all_to_all x3, blocking collectives, exchange(): return lax.all_to_all(x, axis, split_axis=0, concat_axis=0, tiled=True)  65 us
    all_to_all x2, waiting for transfers between devices, exchange(): return lax.all_to_all(x, axis, split_axis=0, concat_axis=0, tiled=True)  48.5 us
    ppermute x21, starting transfers between devices, mirror(): return lax.ppermute(x, axis, [(d, d ^ k) for d in range(N)])  36.4 us
    all_to_all x2, starting transfers between devices, exchange(): return lax.all_to_all(x, axis, split_axis=0, concat_axis=0, tiled=True)  16.7 us
    ppermute x21, waiting for transfers between devices, mirror(): return lax.ppermute(x, axis, [(d, d ^ k) for d in range(N)])  15.2 us
    pallas_call x1, Pallas kernels, column_step(): pl.pallas_call(column_kernel, in_specs=[pl.BlockSpec(memory_space=pltpu.S...  11.3 us
    ppermute x1, waiting for transfers between devices, swap(): return lax.ppermute(x, ('depth', 'cols'), pairs)  7.04 us
    pallas_call x1, Pallas kernels, row_proj(): pl.pallas_call(row_proj_kernel, in_specs=[HBM] * 5, out_specs=HBM, out_sh...  5.49 us
  transfers between devices with their start and end apart: 24, of which 10 were waited for; matrix products, arithmetic and copies ran while one was open for 0% of the time, Pallas kernels for 1%

profile of v7, /device:TPU:4, one launch (start us, length us, event | category | flops | bytes accessed | tf_op | source)
XLA Modules:
  0.0 221.2 jit_solution(5098687128018730897)
XLA Ops:
  0.6 5.5 %shard_map.140 = bf16[16,768,128]{2,1,0:T(8,128)(2,1)} custom-call(bf16[512,768]{1,0:T(8,128)(2,1)} %bitcast.12, s32[16,32]{1,0:T(8,128)} %occ_ref.1, bf16[768,768]{1,0:T(8,128)(2,1)} %wq_hbm.1, bf16[768,768]{1,0:T(8,128)(2,1)} %wk_hbm.1, bf16[768,768]{1,0:T(8,128)(2,1)} %wv_hbm.1), custom_call_target="tpu_custom_call" | custom-call | flops 1811939328 | bytes 8000000 | tf_op jit(solution)/shard_map/pallas_call | solution.py:131
  6.1 11.2 %all-to-all-start = ((bf16[16,768,128]{2,1,0:T(8,128)(2,1)}), bf16[16,768,128]{2,1,0:T(8,128)(2,1)S(1)}, u32[]{:S(2)}, u32[]{:S(2)}) async-start(bf16[16,768,128]{2,1,0:T(8,128)(2,1)} %shard_map.140), calls=%async_computation | async-start | bytes 6291456 | tf_op jit(solution)/shard_map/all_to_all | solution.py:479
  23.0 2.6 %collective-permute-start.4 = (bf16[32,896]{1,0:T(8,128)(2,1)S(1)}, bf16[32,896]{1,0:T(8,128)(2,1)S(1)}, u32[]{:S(2)}, u32[]{:S(2)}) collective-permute-start(bf16[32,896]{1,0:T(8,128)(2,1)S(1)} %get-tuple-element.44), channel_id=1, source_target_pairs={{0,80},{16,64},{32,112},{48,96},{64,16},{80,0},{96,48},{112,32},{1... | collective-permute-start | bytes 172040 | tf_op jit(solution)/shard_map/ppermute | solution.py:488
  29.2 2.5 %collective-permute-start.9 = (bf16[32,896]{1,0:T(8,128)(2,1)S(1)}, bf16[32,896]{1,0:T(8,128)(2,1)S(1)}, u32[]{:S(2)}, u32[]{:S(2)}) collective-permute-start(bf16[32,896]{1,0:T(8,128)(2,1)S(1)} %get-tuple-element.49), channel_id=1, source_target_pairs={{0,160},{16,176},{32,128},{48,144},{64,224},{80,240},{96,192},{112... | collective-permute-start | bytes 172040 | tf_op jit(solution)/shard_map/ppermute | solution.py:488
  32.0 2.4 %collective-permute-start.11 = (bf16[32,896]{1,0:T(8,128)(2,1)S(1)}, bf16[32,896]{1,0:T(8,128)(2,1)S(1)}, u32[]{:S(2)}, u32[]{:S(2)}) collective-permute-start(bf16[32,896]{1,0:T(8,128)(2,1)S(1)} %get-tuple-element.51), channel_id=1, source_target_pairs={{0,192},{16,208},{32,224},{48,240},{64,128},{80,144},{96,160},{112... | collective-permute-start | bytes 172040 | tf_op jit(solution)/shard_map/ppermute | solution.py:488
  34.3 2.5 %collective-permute-start.12 = (bf16[32,896]{1,0:T(8,128)(2,1)S(1)}, bf16[32,896]{1,0:T(8,128)(2,1)S(1)}, u32[]{:S(2)}, u32[]{:S(2)}) collective-permute-start(bf16[32,896]{1,0:T(8,128)(2,1)S(1)} %get-tuple-element.52), channel_id=1, source_target_pairs={{0,208},{16,192},{32,240},{48,224},{64,144},{80,128},{96,176},{112... | collective-permute-start | bytes 172040 | tf_op jit(solution)/shard_map/ppermute | solution.py:488
  39.1 1.8 collective-permute-done.12.refs_13_
  40.8 2.0 collective-permute-done.13.refs_14_
  43.8 48.5 %all-to-all-done.qk_ref.v_ref = bf16[16,768,128]{2,1,0:T(8,128)(2,1)S(1)} async-done(((bf16[16,768,128]{2,1,0:T(8,128)(2,1)}), bf16[16,768,128]{2,1,0:T(8,128)(2,1)S(1)}, u32[]{:S(2)}, u32[]{:S(2)}) %all-to-all-start) | async-done | bytes 3145760 | tf_op jit(solution)/shard_map/all_to_all | solution.py:479
  93.2 12.2 %all_to_all.25.in_ref = bf16[16,32,512]{2,1,0:T(8,128)(2,1)S(1)} all-to-all(bf16[16,32,512]{2,1,0:T(8,128)(2,1)S(1)} %bitcast.11), channel_id=1, replica_groups=mesh['depth'=16,'cols'=16] {'depth'}, dimensions={0} | all-to-all | bytes 1048576 | tf_op jit(solution)/shard_map/all_to_all | solution.py:479
  105.7 13.4 %all_to_all.26.p_ref = bf16[16,32,512]{2,1,0:T(8,128)(2,1)S(1)} all-to-all(bf16[16,32,512]{2,1,0:T(8,128)(2,1)S(1)} %shard_map.143), channel_id=1, replica_groups=mesh['depth'=16,'cols'=16] {'depth'}, dimensions={0} | all-to-all | bytes 1048576 | tf_op jit(solution)/shard_map/all_to_all | solution.py:479
  120.2 39.4 %all_to_all.27 = bf16[256,16,128]{2,1,0:T(8,128)(2,1)} all-to-all(bf16[256,16,128]{2,1,0:T(8,128)(2,1)S(1)} %bitcast.10), channel_id=1, replica_groups=mesh['depth'=16,'cols'=16] {'cols','depth'}, dimensions={0} | all-to-all | bytes 2097152 | tf_op jit(solution)/shard_map/all_to_all | solution.py:479
  159.5 11.3 %shard_map.145 = (bf16[16,64,768]{2,1,0:T(8,128)(2,1)}, bf16[80,256]{1,0:T(8,128)(2,1)}) custom-call(s32[2]{0:T(128)} %copy-done.3, bf16[4096,128]{1,0:T(8,128)(2,1)} %bitcast.14, bf16[32,768]{1,0:T(8,128)(2,1)} %bitcast.16, bf16[32,768]{1,0:T(8,128)(2,1)} %bitcast.17, bf16[768,768]{1,0:T(8,128)(2,1)} %wo_hbm.1, bf16[768,768]{1,0:T(8,128)(2,1)} %cq_hbm.1, ...), custom_call_target="tpu_custom_call" | custom-call | flops 3019898880 | bytes 9000000 | tf_op jit(solution)/shard_map/pallas_call | solution.py:362
  170.8 5.5 %all-to-all-start.4 = ((bf16[16,64,768]{2,1,0:T(8,128)(2,1)}), bf16[16,64,768]{2,1,0:T(8,128)(2,1)S(1)}, u32[]{:S(2)}, u32[]{:S(2)}) async-start(bf16[16,64,768]{2,1,0:T(8,128)(2,1)} %get-tuple-element.72), calls=%async_computation.4 | async-start | bytes 3145728 | tf_op jit(solution)/shard_map/all_to_all | solution.py:479
  176.4 2.2 %collective-permute-start.15 = (bf16[80,256]{1,0:T(8,128)(2,1)S(1)}, bf16[80,256]{1,0:T(8,128)(2,1)S(1)}, u32[]{:S(2)}, u32[]{:S(2)}) collective-permute-start(bf16[80,256]{1,0:T(8,128)(2,1)S(1)} %copy-done.20), channel_id=1, source_target_pairs={{0,0},{1,16},{2,32},{3,48},{4,64},{5,80},{6,96},{7,112},{8,128},{9... | collective-permute-start | bytes 122888 | tf_op jit(solution)/shard_map/ppermute | solution.py:484
  178.6 7.0 %collective-permute-done.15 = bf16[80,256]{1,0:T(8,128)(2,1)S(1)} collective-permute-done((bf16[80,256]{1,0:T(8,128)(2,1)S(1)}, bf16[80,256]{1,0:T(8,128)(2,1)S(1)}, u32[]{:S(2)}, u32[]{:S(2)}) %collective-permute-start.15) | collective-permute-done | bytes 40992 | tf_op jit(solution)/shard_map/ppermute | solution.py:484
  185.7 3.4 %collective-permute-start.18 = (bf16[80,256]{1,0:T(8,128)(2,1)S(1)}, bf16[80,256]{1,0:T(8,128)(2,1)S(1)}, u32[]{:S(2)}, u32[]{:S(2)}) collective-permute-start(bf16[80,256]{1,0:T(8,128)(2,1)S(1)} %collective-permute-done.15), channel_id=1, source_target_pairs={{0,12},{1,13},{2,14},{3,15},{4,8},{5,9},{6,10},{7,11},{8,4},{9,5},... | collective-permute-start | bytes 122888 | tf_op jit(solution)/shard_map/ppermute | solution.py:488
  189.6 2.6 %collective-permute-start.16 = (bf16[80,256]{1,0:T(8,128)(2,1)S(1)}, bf16[80,256]{1,0:T(8,128)(2,1)S(1)}, u32[]{:S(2)}, u32[]{:S(2)}) collective-permute-start(bf16[80,256]{1,0:T(8,128)(2,1)S(1)} %collective-permute-done.15), channel_id=1, source_target_pairs={{0,4},{1,5},{2,6},{3,7},{4,0},{5,1},{6,2},{7,3},{8,12},{9,13},{10,... | collective-permute-start | bytes 122888 | tf_op jit(solution)/shard_map/ppermute | solution.py:488
  192.2 5.3 %collective-permute-done.17 = bf16[80,256]{1,0:T(8,128)(2,1)S(1)} collective-permute-done((bf16[80,256]{1,0:T(8,128)(2,1)S(1)}, bf16[80,256]{1,0:T(8,128)(2,1)S(1)}, u32[]{:S(2)}, u32[]{:S(2)}) %collective-permute-start.17) | collective-permute-done | bytes 40992 | tf_op jit(solution)/shard_map/ppermute | solution.py:488
  197.6 2.1 collective-permute-start.21
  199.7 10.2 %collective-permute-start.20 = (bf16[272,256]{1,0:T(8,128)(2,1)S(1)}, bf16[272,256]{1,0:T(8,128)(2,1)S(1)}, u32[]{:S(2)}, u32[]{:S(2)}) collective-permute-start(bf16[272,256]{1,0:T(8,128)(2,1)S(1)} %concatenate.3.r0), channel_id=1, source_target_pairs={{0,2},{1,3},{2,0},{3,1},{4,6},{5,7},{6,4},{7,5},{8,10},{9,11},{10,... | collective-permute-start | bytes 417800 | tf_op jit(solution)/shard_map/ppermute | solution.py:488
  211.4 3.1 %collective-permute-done.20.r2 = bf16[272,256]{1,0:T(8,128)(2,1)S(1)} collective-permute-done((bf16[272,256]{1,0:T(8,128)(2,1)S(1)}, bf16[272,256]{1,0:T(8,128)(2,1)S(1)}, u32[]{:S(2)}, u32[]{:S(2)}) %collective-permute-start.20) | collective-permute-done | bytes 139296 | tf_op jit(solution)/shard_map/ppermute | solution.py:488
  214.5 2.0 collective-permute-done.19.r1
  216.5 4.6 %shard_map.147 = bf16[1024,128]{1,0:T(8,128)(2,1)} custom-call(s32[2]{0:T(128)S(1)} %copy-done.4, bf16[16,64,768]{2,1,0:T(8,128)(2,1)S(1)} %all-to-all-done.4.in_ref.l_ref, bf16[272,256]{1,0:T(8,128)(2,1)S(1)} %concatenate.3.r0, bf16[272,256]{1,0:T(8,128)(2,1)S(1)} %collective-permute-done.19.r1, bf16[272,256]{1,0:T(8,128)(2,1)S(1)} %collective-permute-done.20.r2, ...), custom_call_target="tpu_custom_call" | custom-call | flops 1610612736 | bytes 6000000 | tf_op jit(solution)/shard_map/pallas_call | solution.py:453
  (87 shorter events, 16.9 us)
Async XLA Ops:
  6.1 86.1 %all-to-all-start = ((bf16[16,768,128]{2,1,0:T(8,128)(2,1)}), bf16[16,768,128]{2,1,0:T(8,128)(2,1)S(1)}, u32[]{:S(2)}, u32[]{:S(2)}) async-start(bf16[16,768,128]{2,1,0:T(8,128)(2,1)} %shard_map.140), calls=%async_computation | async-start | bytes 6291456 | tf_op jit(solution)/shard_map/all_to_all | solution.py:479
  20.7 5.0 %collective-permute-start = (bf16[32,896]{1,0:T(8,128)(2,1)S(1)}, bf16[32,896]{1,0:T(8,128)(2,1)S(1)}, u32[]{:S(2)}, u32[]{:S(2)}) collective-permute-start(bf16[32,896]{1,0:T(8,128)(2,1)S(1)} %get-tuple-element.40), channel_id=1, source_target_pairs={{0,16},{16,0},{32,48},{48,32},{64,80},{80,64},{96,112},{112,96},{1... | collective-permute-start | bytes 172040 | tf_op jit(solution)/shard_map/ppermute | solution.py:488
  20.7 5.5 %collective-permute-start.1 = (bf16[32,896]{1,0:T(8,128)(2,1)S(1)}, bf16[32,896]{1,0:T(8,128)(2,1)S(1)}, u32[]{:S(2)}, u32[]{:S(2)}) collective-permute-start(bf16[32,896]{1,0:T(8,128)(2,1)S(1)} %get-tuple-element.41), channel_id=1, source_target_pairs={{0,32},{16,48},{32,0},{48,16},{64,96},{80,112},{96,64},{112,80},{1... | collective-permute-start | bytes 172040 | tf_op jit(solution)/shard_map/ppermute | solution.py:488
  21.9 5.7 %collective-permute-start.2 = (bf16[32,896]{1,0:T(8,128)(2,1)S(1)}, bf16[32,896]{1,0:T(8,128)(2,1)S(1)}, u32[]{:S(2)}, u32[]{:S(2)}) collective-permute-start(bf16[32,896]{1,0:T(8,128)(2,1)S(1)} %get-tuple-element.42), channel_id=1, source_target_pairs={{0,48},{16,32},{32,16},{48,0},{64,112},{80,96},{96,80},{112,64},{1... | collective-permute-start | bytes 172040 | tf_op jit(solution)/shard_map/ppermute | solution.py:488
  22.5 6.2 %collective-permute-start.3 = (bf16[32,896]{1,0:T(8,128)(2,1)S(1)}, bf16[32,896]{1,0:T(8,128)(2,1)S(1)}, u32[]{:S(2)}, u32[]{:S(2)}) collective-permute-start(bf16[32,896]{1,0:T(8,128)(2,1)S(1)} %get-tuple-element.43), channel_id=1, source_target_pairs={{0,64},{16,80},{32,96},{48,112},{64,0},{80,16},{96,32},{112,48},{1... | collective-permute-start | bytes 172040 | tf_op jit(solution)/shard_map/ppermute | solution.py:488
  23.0 6.1 %collective-permute-start.4 = (bf16[32,896]{1,0:T(8,128)(2,1)S(1)}, bf16[32,896]{1,0:T(8,128)(2,1)S(1)}, u32[]{:S(2)}, u32[]{:S(2)}) collective-permute-start(bf16[32,896]{1,0:T(8,128)(2,1)S(1)} %get-tuple-element.44), channel_id=1, source_target_pairs={{0,80},{16,64},{32,112},{48,96},{64,16},{80,0},{96,48},{112,32},{1... | collective-permute-start | bytes 172040 | tf_op jit(solution)/shard_map/ppermute | solution.py:488
  25.7 6.0 %collective-permute-start.5 = (bf16[32,896]{1,0:T(8,128)(2,1)S(1)}, bf16[32,896]{1,0:T(8,128)(2,1)S(1)}, u32[]{:S(2)}, u32[]{:S(2)}) collective-permute-start(bf16[32,896]{1,0:T(8,128)(2,1)S(1)} %get-tuple-element.45), channel_id=1, source_target_pairs={{0,96},{16,112},{32,64},{48,80},{64,32},{80,48},{96,0},{112,16},{1... | collective-permute-start | bytes 172040 | tf_op jit(solution)/shard_map/ppermute | solution.py:488
  26.2 5.7 %collective-permute-start.6 = (bf16[32,896]{1,0:T(8,128)(2,1)S(1)}, bf16[32,896]{1,0:T(8,128)(2,1)S(1)}, u32[]{:S(2)}, u32[]{:S(2)}) collective-permute-start(bf16[32,896]{1,0:T(8,128)(2,1)S(1)} %get-tuple-element.46), channel_id=1, source_target_pairs={{0,112},{16,96},{32,80},{48,64},{64,48},{80,32},{96,16},{112,0},{1... | collective-permute-start | bytes 172040 | tf_op jit(solution)/shard_map/ppermute | solution.py:488
  27.6 6.8 %collective-permute-start.7 = (bf16[32,896]{1,0:T(8,128)(2,1)S(1)}, bf16[32,896]{1,0:T(8,128)(2,1)S(1)}, u32[]{:S(2)}, u32[]{:S(2)}) collective-permute-start(bf16[32,896]{1,0:T(8,128)(2,1)S(1)} %get-tuple-element.47), channel_id=1, source_target_pairs={{0,128},{16,144},{32,160},{48,176},{64,192},{80,208},{96,224},{112... | collective-permute-start | bytes 172040 | tf_op jit(solution)/shard_map/ppermute | solution.py:488
  28.8 8.0 %collective-permute-start.8 = (bf16[32,896]{1,0:T(8,128)(2,1)S(1)}, bf16[32,896]{1,0:T(8,128)(2,1)S(1)}, u32[]{:S(2)}, u32[]{:S(2)}) collective-permute-start(bf16[32,896]{1,0:T(8,128)(2,1)S(1)} %get-tuple-element.48), channel_id=1, source_target_pairs={{0,144},{16,128},{32,176},{48,160},{64,208},{80,192},{96,240},{112... | collective-permute-start | bytes 172040 | tf_op jit(solution)/shard_map/ppermute | solution.py:488
  29.2 9.1 %collective-permute-start.9 = (bf16[32,896]{1,0:T(8,128)(2,1)S(1)}, bf16[32,896]{1,0:T(8,128)(2,1)S(1)}, u32[]{:S(2)}, u32[]{:S(2)}) collective-permute-start(bf16[32,896]{1,0:T(8,128)(2,1)S(1)} %get-tuple-element.49), channel_id=1, source_target_pairs={{0,160},{16,176},{32,128},{48,144},{64,224},{80,240},{96,192},{112... | collective-permute-start | bytes 172040 | tf_op jit(solution)/shard_map/ppermute | solution.py:488
  31.7 7.1 %collective-permute-start.10 = (bf16[32,896]{1,0:T(8,128)(2,1)S(1)}, bf16[32,896]{1,0:T(8,128)(2,1)S(1)}, u32[]{:S(2)}, u32[]{:S(2)}) collective-permute-start(bf16[32,896]{1,0:T(8,128)(2,1)S(1)} %get-tuple-element.50), channel_id=1, source_target_pairs={{0,176},{16,160},{32,144},{48,128},{64,240},{80,224},{96,208},{112... | collective-permute-start | bytes 172040 | tf_op jit(solution)/shard_map/ppermute | solution.py:488
  32.0 7.1 %collective-permute-start.11 = (bf16[32,896]{1,0:T(8,128)(2,1)S(1)}, bf16[32,896]{1,0:T(8,128)(2,1)S(1)}, u32[]{:S(2)}, u32[]{:S(2)}) collective-permute-start(bf16[32,896]{1,0:T(8,128)(2,1)S(1)} %get-tuple-element.51), channel_id=1, source_target_pairs={{0,192},{16,208},{32,224},{48,240},{64,128},{80,144},{96,160},{112... | collective-permute-start | bytes 172040 | tf_op jit(solution)/shard_map/ppermute | solution.py:488
  34.3 6.5 %collective-permute-start.12 = (bf16[32,896]{1,0:T(8,128)(2,1)S(1)}, bf16[32,896]{1,0:T(8,128)(2,1)S(1)}, u32[]{:S(2)}, u32[]{:S(2)}) collective-permute-start(bf16[32,896]{1,0:T(8,128)(2,1)S(1)} %get-tuple-element.52), channel_id=1, source_target_pairs={{0,208},{16,192},{32,240},{48,224},{64,144},{80,128},{96,176},{112... | collective-permute-start | bytes 172040 | tf_op jit(solution)/shard_map/ppermute | solution.py:488
  36.8 6.0 %collective-permute-start.13 = (bf16[32,896]{1,0:T(8,128)(2,1)S(1)}, bf16[32,896]{1,0:T(8,128)(2,1)S(1)}, u32[]{:S(2)}, u32[]{:S(2)}) collective-permute-start(bf16[32,896]{1,0:T(8,128)(2,1)S(1)} %get-tuple-element.53), channel_id=1, source_target_pairs={{0,224},{16,240},{32,192},{48,208},{64,160},{80,176},{96,128},{112... | collective-permute-start | bytes 172040 | tf_op jit(solution)/shard_map/ppermute | solution.py:488
  38.3 5.5 %collective-permute-start.14 = (bf16[32,896]{1,0:T(8,128)(2,1)S(1)}, bf16[32,896]{1,0:T(8,128)(2,1)}, u32[]{:S(2)}, u32[]{:S(2)}) collective-permute-start(bf16[32,896]{1,0:T(8,128)(2,1)S(1)} %get-tuple-element.54), channel_id=1, source_target_pairs={{0,240},{16,224},{32,208},{48,192},{64,176},{80,160},{96,144},{112... | collective-permute-start | bytes 172040 | tf_op jit(solution)/shard_map/ppermute | solution.py:488
  170.8 39.1 %all-to-all-start.4 = ((bf16[16,64,768]{2,1,0:T(8,128)(2,1)}), bf16[16,64,768]{2,1,0:T(8,128)(2,1)S(1)}, u32[]{:S(2)}, u32[]{:S(2)}) async-start(bf16[16,64,768]{2,1,0:T(8,128)(2,1)} %get-tuple-element.72), calls=%async_computation.4 | async-start | bytes 3145728 | tf_op jit(solution)/shard_map/all_to_all | solution.py:479
  176.4 9.3 %collective-permute-start.15 = (bf16[80,256]{1,0:T(8,128)(2,1)S(1)}, bf16[80,256]{1,0:T(8,128)(2,1)S(1)}, u32[]{:S(2)}, u32[]{:S(2)}) collective-permute-start(bf16[80,256]{1,0:T(8,128)(2,1)S(1)} %copy-done.20), channel_id=1, source_target_pairs={{0,0},{1,16},{2,32},{3,48},{4,64},{5,80},{6,96},{7,112},{8,128},{9... | collective-permute-start | bytes 122888 | tf_op jit(solution)/shard_map/ppermute | solution.py:484
  185.7 6.5 %collective-permute-start.18 = (bf16[80,256]{1,0:T(8,128)(2,1)S(1)}, bf16[80,256]{1,0:T(8,128)(2,1)S(1)}, u32[]{:S(2)}, u32[]{:S(2)}) collective-permute-start(bf16[80,256]{1,0:T(8,128)(2,1)S(1)} %collective-permute-done.15), channel_id=1, source_target_pairs={{0,12},{1,13},{2,14},{3,15},{4,8},{5,9},{6,10},{7,11},{8,4},{9,5},... | collective-permute-start | bytes 122888 | tf_op jit(solution)/shard_map/ppermute | solution.py:488
  189.0 8.4 %collective-permute-start.17 = (bf16[80,256]{1,0:T(8,128)(2,1)S(1)}, bf16[80,256]{1,0:T(8,128)(2,1)S(1)}, u32[]{:S(2)}, u32[]{:S(2)}) collective-permute-start(bf16[80,256]{1,0:T(8,128)(2,1)S(1)} %collective-permute-done.15), channel_id=1, source_target_pairs={{0,8},{1,9},{2,10},{3,11},{4,12},{5,13},{6,14},{7,15},{8,0},{9,1},... | collective-permute-start | bytes 122888 | tf_op jit(solution)/shard_map/ppermute | solution.py:488
  189.6 7.9 %collective-permute-start.16 = (bf16[80,256]{1,0:T(8,128)(2,1)S(1)}, bf16[80,256]{1,0:T(8,128)(2,1)S(1)}, u32[]{:S(2)}, u32[]{:S(2)}) collective-permute-start(bf16[80,256]{1,0:T(8,128)(2,1)S(1)} %collective-permute-done.15), channel_id=1, source_target_pairs={{0,4},{1,5},{2,6},{3,7},{4,0},{5,1},{6,2},{7,3},{8,12},{9,13},{10,... | collective-permute-start | bytes 122888 | tf_op jit(solution)/shard_map/ppermute | solution.py:488
  197.6 13.9 %collective-permute-start.21 = (bf16[272,256]{1,0:T(8,128)(2,1)S(1)}, bf16[272,256]{1,0:T(8,128)(2,1)S(1)}, u32[]{:S(2)}, u32[]{:S(2)}) collective-permute-start(bf16[272,256]{1,0:T(8,128)(2,1)S(1)} %concatenate.3.r0), channel_id=1, source_target_pairs={{0,3},{1,2},{2,1},{3,0},{4,7},{5,6},{6,5},{7,4},{8,11},{9,10},{10,... | collective-permute-start | bytes 417800 | tf_op jit(solution)/shard_map/ppermute | solution.py:488
  199.7 14.8 %collective-permute-start.20 = (bf16[272,256]{1,0:T(8,128)(2,1)S(1)}, bf16[272,256]{1,0:T(8,128)(2,1)S(1)}, u32[]{:S(2)}, u32[]{:S(2)}) collective-permute-start(bf16[272,256]{1,0:T(8,128)(2,1)S(1)} %concatenate.3.r0), channel_id=1, source_target_pairs={{0,2},{1,3},{2,0},{3,1},{4,6},{5,7},{6,4},{7,5},{8,10},{9,11},{10,... | collective-permute-start | bytes 417800 | tf_op jit(solution)/shard_map/ppermute | solution.py:488
  209.9 6.6 %collective-permute-start.19 = (bf16[272,256]{1,0:T(8,128)(2,1)S(1)}, bf16[272,256]{1,0:T(8,128)(2,1)S(1)}, u32[]{:S(2)}, u32[]{:S(2)}) collective-permute-start(bf16[272,256]{1,0:T(8,128)(2,1)S(1)} %concatenate.3.r0), channel_id=1, source_target_pairs={{0,1},{1,0},{2,3},{3,2},{4,5},{5,4},{6,7},{7,6},{8,9},{9,8},{10,11... | collective-permute-start | bytes 417800 | tf_op jit(solution)/shard_map/ppermute | solution.py:488
  (21 other events, 560.8 us)

commit v8 on v7

--- a/solution.py
+++ b/solution.py
@@ -408,10 +408,11 @@
     l0, l1, l2, l3, l4, lp, lhs, osc, wk, r_ref, n_ref,
 ):
     for near, ref in enumerate((r0, r1, r2, r3)):
+        tail = ref[8 * C : 8 * C + 16, :128].astype(f32)
         for far in range(4):
             at = jnp.bitwise_xor(me_ref[1], 4 * far + near)
             r_ref[at] = ref[2 * C * far : 2 * C * far + 2 * C]
-            n_ref[at] = ref[8 * C + 4 * far : 8 * C + 4 * far + 4, :128].astype(f32)
+            n_ref[at] = tail[4 * far : 4 * far + 4]
     wk[...] = jnp.zeros_like(wk)
     for c in range(C):
         w = wp_ref[C * c : C * c + C, :]

time: 222 us -> 222 us (level)
  no operation moved by 1% of the time
where the time goes in v8:
time: 222 us; the launch traced here: 221 us
  waiting for transfers between devices  70.7 us (32%)
  blocking collectives  65 us (29%)
  starting transfers between devices  55.4 us (25%)
  Pallas kernels  26.5 us (12%)
  local copies, waits for them, and re-layouts  2.54 us (1%)
    all_to_all x3, blocking collectives, exchange(): return lax.all_to_all(x, axis, split_axis=0, concat_axis=0, tiled=True)  65 us
    all_to_all x2, waiting for transfers between devices, exchange(): return lax.all_to_all(x, axis, split_axis=0, concat_axis=0, tiled=True)  48.5 us
    ppermute x21, starting transfers between devices, mirror(): return lax.ppermute(x, axis, [(d, d ^ k) for d in range(N)])  36.4 us
    all_to_all x2, starting transfers between devices, exchange(): return lax.all_to_all(x, axis, split_axis=0, concat_axis=0, tiled=True)  16.7 us
    ppermute x21, waiting for transfers between devices, mirror(): return lax.ppermute(x, axis, [(d, d ^ k) for d in range(N)])  15.2 us
    pallas_call x1, Pallas kernels, column_step(): pl.pallas_call(column_kernel, in_specs=[pl.BlockSpec(memory_space=pltpu.S...  11.3 us
    ppermute x1, waiting for transfers between devices, swap(): return lax.ppermute(x, ('depth', 'cols'), pairs)  7.04 us
    pallas_call x1, Pallas kernels, row_proj(): pl.pallas_call(row_proj_kernel, in_specs=[HBM] * 5, out_specs=HBM, out_sh...  5.49 us
  transfers between devices with their start and end apart: 24, of which 10 were waited for; matrix products, arithmetic and copies ran while one was open for 0% of the time, Pallas kernels for 1%

profile of v8, /device:TPU:4, one launch (start us, length us, event | category | flops | bytes accessed | tf_op | source)
XLA Modules:
  0.0 221.2 jit_solution(5306395273000244640)
XLA Ops:
  0.6 5.5 %shard_map.140 = bf16[16,768,128]{2,1,0:T(8,128)(2,1)} custom-call(bf16[512,768]{1,0:T(8,128)(2,1)} %bitcast.12, s32[16,32]{1,0:T(8,128)} %occ_ref.1, bf16[768,768]{1,0:T(8,128)(2,1)} %wq_hbm.1, bf16[768,768]{1,0:T(8,128)(2,1)} %wk_hbm.1, bf16[768,768]{1,0:T(8,128)(2,1)} %wv_hbm.1), custom_call_target="tpu_custom_call" | custom-call | flops 1811939328 | bytes 8000000 | tf_op jit(solution)/shard_map/pallas_call | solution.py:131
  6.1 11.2 %all-to-all-start = ((bf16[16,768,128]{2,1,0:T(8,128)(2,1)}), bf16[16,768,128]{2,1,0:T(8,128)(2,1)S(1)}, u32[]{:S(2)}, u32[]{:S(2)}) async-start(bf16[16,768,128]{2,1,0:T(8,128)(2,1)} %shard_map.140), calls=%async_computation | async-start | bytes 6291456 | tf_op jit(solution)/shard_map/all_to_all | solution.py:480
  23.0 2.6 %collective-permute-start.4 = (bf16[32,896]{1,0:T(8,128)(2,1)S(1)}, bf16[32,896]{1,0:T(8,128)(2,1)S(1)}, u32[]{:S(2)}, u32[]{:S(2)}) collective-permute-start(bf16[32,896]{1,0:T(8,128)(2,1)S(1)} %get-tuple-element.44), channel_id=1, source_target_pairs={{0,80},{16,64},{32,112},{48,96},{64,16},{80,0},{96,48},{112,32},{1... | collective-permute-start | bytes 172040 | tf_op jit(solution)/shard_map/ppermute | solution.py:489
  29.2 2.5 %collective-permute-start.9 = (bf16[32,896]{1,0:T(8,128)(2,1)S(1)}, bf16[32,896]{1,0:T(8,128)(2,1)S(1)}, u32[]{:S(2)}, u32[]{:S(2)}) collective-permute-start(bf16[32,896]{1,0:T(8,128)(2,1)S(1)} %get-tuple-element.49), channel_id=1, source_target_pairs={{0,160},{16,176},{32,128},{48,144},{64,224},{80,240},{96,192},{112... | collective-permute-start | bytes 172040 | tf_op jit(solution)/shard_map/ppermute | solution.py:489
  32.0 2.4 %collective-permute-start.11 = (bf16[32,896]{1,0:T(8,128)(2,1)S(1)}, bf16[32,896]{1,0:T(8,128)(2,1)S(1)}, u32[]{:S(2)}, u32[]{:S(2)}) collective-permute-start(bf16[32,896]{1,0:T(8,128)(2,1)S(1)} %get-tuple-element.51), channel_id=1, source_target_pairs={{0,192},{16,208},{32,224},{48,240},{64,128},{80,144},{96,160},{112... | collective-permute-start | bytes 172040 | tf_op jit(solution)/shard_map/ppermute | solution.py:489
  34.3 2.5 %collective-permute-start.12 = (bf16[32,896]{1,0:T(8,128)(2,1)S(1)}, bf16[32,896]{1,0:T(8,128)(2,1)S(1)}, u32[]{:S(2)}, u32[]{:S(2)}) collective-permute-start(bf16[32,896]{1,0:T(8,128)(2,1)S(1)} %get-tuple-element.52), channel_id=1, source_target_pairs={{0,208},{16,192},{32,240},{48,224},{64,144},{80,128},{96,176},{112... | collective-permute-start | bytes 172040 | tf_op jit(solution)/shard_map/ppermute | solution.py:489
  39.1 1.8 collective-permute-done.12.refs_13_
  40.8 2.0 collective-permute-done.13.refs_14_
  43.8 48.5 %all-to-all-done.qk_ref.v_ref = bf16[16,768,128]{2,1,0:T(8,128)(2,1)S(1)} async-done(((bf16[16,768,128]{2,1,0:T(8,128)(2,1)}), bf16[16,768,128]{2,1,0:T(8,128)(2,1)S(1)}, u32[]{:S(2)}, u32[]{:S(2)}) %all-to-all-start) | async-done | bytes 3145760 | tf_op jit(solution)/shard_map/all_to_all | solution.py:480
  93.2 12.2 %all_to_all.25.in_ref = bf16[16,32,512]{2,1,0:T(8,128)(2,1)S(1)} all-to-all(bf16[16,32,512]{2,1,0:T(8,128)(2,1)S(1)} %bitcast.11), channel_id=1, replica_groups=mesh['depth'=16,'cols'=16] {'depth'}, dimensions={0} | all-to-all | bytes 1048576 | tf_op jit(solution)/shard_map/all_to_all | solution.py:480
  105.7 13.4 %all_to_all.26.p_ref = bf16[16,32,512]{2,1,0:T(8,128)(2,1)S(1)} all-to-all(bf16[16,32,512]{2,1,0:T(8,128)(2,1)S(1)} %shard_map.143), channel_id=1, replica_groups=mesh['depth'=16,'cols'=16] {'depth'}, dimensions={0} | all-to-all | bytes 1048576 | tf_op jit(solution)/shard_map/all_to_all | solution.py:480
  120.2 39.4 %all_to_all.27 = bf16[256,16,128]{2,1,0:T(8,128)(2,1)} all-to-all(bf16[256,16,128]{2,1,0:T(8,128)(2,1)S(1)} %bitcast.10), channel_id=1, replica_groups=mesh['depth'=16,'cols'=16] {'cols','depth'}, dimensions={0} | all-to-all | bytes 2097152 | tf_op jit(solution)/shard_map/all_to_all | solution.py:480
  159.5 11.3 %shard_map.145 = (bf16[16,64,768]{2,1,0:T(8,128)(2,1)}, bf16[80,256]{1,0:T(8,128)(2,1)}) custom-call(s32[2]{0:T(128)} %copy-done.3, bf16[4096,128]{1,0:T(8,128)(2,1)} %bitcast.14, bf16[32,768]{1,0:T(8,128)(2,1)} %bitcast.16, bf16[32,768]{1,0:T(8,128)(2,1)} %bitcast.17, bf16[768,768]{1,0:T(8,128)(2,1)} %wo_hbm.1, bf16[768,768]{1,0:T(8,128)(2,1)} %cq_hbm.1, ...), custom_call_target="tpu_custom_call" | custom-call | flops 3019898880 | bytes 9000000 | tf_op jit(solution)/shard_map/pallas_call | solution.py:362
  170.8 5.5 %all-to-all-start.4 = ((bf16[16,64,768]{2,1,0:T(8,128)(2,1)}), bf16[16,64,768]{2,1,0:T(8,128)(2,1)S(1)}, u32[]{:S(2)}, u32[]{:S(2)}) async-start(bf16[16,64,768]{2,1,0:T(8,128)(2,1)} %get-tuple-element.72), calls=%async_computation.4 | async-start | bytes 3145728 | tf_op jit(solution)/shard_map/all_to_all | solution.py:480
  176.4 2.2 %collective-permute-start.15 = (bf16[80,256]{1,0:T(8,128)(2,1)S(1)}, bf16[80,256]{1,0:T(8,128)(2,1)S(1)}, u32[]{:S(2)}, u32[]{:S(2)}) collective-permute-start(bf16[80,256]{1,0:T(8,128)(2,1)S(1)} %copy-done.20), channel_id=1, source_target_pairs={{0,0},{1,16},{2,32},{3,48},{4,64},{5,80},{6,96},{7,112},{8,128},{9... | collective-permute-start | bytes 122888 | tf_op jit(solution)/shard_map/ppermute | solution.py:485
  178.6 7.0 %collective-permute-done.15 = bf16[80,256]{1,0:T(8,128)(2,1)S(1)} collective-permute-done((bf16[80,256]{1,0:T(8,128)(2,1)S(1)}, bf16[80,256]{1,0:T(8,128)(2,1)S(1)}, u32[]{:S(2)}, u32[]{:S(2)}) %collective-permute-start.15) | collective-permute-done | bytes 40992 | tf_op jit(solution)/shard_map/ppermute | solution.py:485
  185.7 3.4 %collective-permute-start.18 = (bf16[80,256]{1,0:T(8,128)(2,1)S(1)}, bf16[80,256]{1,0:T(8,128)(2,1)S(1)}, u32[]{:S(2)}, u32[]{:S(2)}) collective-permute-start(bf16[80,256]{1,0:T(8,128)(2,1)S(1)} %collective-permute-done.15), channel_id=1, source_target_pairs={{0,12},{1,13},{2,14},{3,15},{4,8},{5,9},{6,10},{7,11},{8,4},{9,5},... | collective-permute-start | bytes 122888 | tf_op jit(solution)/shard_map/ppermute | solution.py:489
  189.6 2.6 %collective-permute-start.16 = (bf16[80,256]{1,0:T(8,128)(2,1)S(1)}, bf16[80,256]{1,0:T(8,128)(2,1)S(1)}, u32[]{:S(2)}, u32[]{:S(2)}) collective-permute-start(bf16[80,256]{1,0:T(8,128)(2,1)S(1)} %collective-permute-done.15), channel_id=1, source_target_pairs={{0,4},{1,5},{2,6},{3,7},{4,0},{5,1},{6,2},{7,3},{8,12},{9,13},{10,... | collective-permute-start | bytes 122888 | tf_op jit(solution)/shard_map/ppermute | solution.py:489
  192.2 5.3 %collective-permute-done.17 = bf16[80,256]{1,0:T(8,128)(2,1)S(1)} collective-permute-done((bf16[80,256]{1,0:T(8,128)(2,1)S(1)}, bf16[80,256]{1,0:T(8,128)(2,1)S(1)}, u32[]{:S(2)}, u32[]{:S(2)}) %collective-permute-start.17) | collective-permute-done | bytes 40992 | tf_op jit(solution)/shard_map/ppermute | solution.py:489
  197.6 2.1 collective-permute-start.21
  199.7 10.2 %collective-permute-start.20 = (bf16[272,256]{1,0:T(8,128)(2,1)S(1)}, bf16[272,256]{1,0:T(8,128)(2,1)S(1)}, u32[]{:S(2)}, u32[]{:S(2)}) collective-permute-start(bf16[272,256]{1,0:T(8,128)(2,1)S(1)} %concatenate.3.r0), channel_id=1, source_target_pairs={{0,2},{1,3},{2,0},{3,1},{4,6},{5,7},{6,4},{7,5},{8,10},{9,11},{10,... | collective-permute-start | bytes 417800 | tf_op jit(solution)/shard_map/ppermute | solution.py:489
  211.4 3.1 %collective-permute-done.20.r2 = bf16[272,256]{1,0:T(8,128)(2,1)S(1)} collective-permute-done((bf16[272,256]{1,0:T(8,128)(2,1)S(1)}, bf16[272,256]{1,0:T(8,128)(2,1)S(1)}, u32[]{:S(2)}, u32[]{:S(2)}) %collective-permute-start.20) | collective-permute-done | bytes 139296 | tf_op jit(solution)/shard_map/ppermute | solution.py:489
  214.5 2.0 collective-permute-done.19.r1
  216.5 4.6 %shard_map.147 = bf16[1024,128]{1,0:T(8,128)(2,1)} custom-call(s32[2]{0:T(128)S(1)} %copy-done.4, bf16[16,64,768]{2,1,0:T(8,128)(2,1)S(1)} %all-to-all-done.4.in_ref.l_ref, bf16[272,256]{1,0:T(8,128)(2,1)S(1)} %concatenate.3.r0, bf16[272,256]{1,0:T(8,128)(2,1)S(1)} %collective-permute-done.19.r1, bf16[272,256]{1,0:T(8,128)(2,1)S(1)} %collective-permute-done.20.r2, ...), custom_call_target="tpu_custom_call" | custom-call | flops 1610612736 | bytes 6000000 | tf_op jit(solution)/shard_map/pallas_call | solution.py:454
  (87 shorter events, 16.9 us)
Async XLA Ops:
  6.1 86.1 %all-to-all-start = ((bf16[16,768,128]{2,1,0:T(8,128)(2,1)}), bf16[16,768,128]{2,1,0:T(8,128)(2,1)S(1)}, u32[]{:S(2)}, u32[]{:S(2)}) async-start(bf16[16,768,128]{2,1,0:T(8,128)(2,1)} %shard_map.140), calls=%async_computation | async-start | bytes 6291456 | tf_op jit(solution)/shard_map/all_to_all | solution.py:480
  20.7 5.0 %collective-permute-start = (bf16[32,896]{1,0:T(8,128)(2,1)S(1)}, bf16[32,896]{1,0:T(8,128)(2,1)S(1)}, u32[]{:S(2)}, u32[]{:S(2)}) collective-permute-start(bf16[32,896]{1,0:T(8,128)(2,1)S(1)} %get-tuple-element.40), channel_id=1, source_target_pairs={{0,16},{16,0},{32,48},{48,32},{64,80},{80,64},{96,112},{112,96},{1... | collective-permute-start | bytes 172040 | tf_op jit(solution)/shard_map/ppermute | solution.py:489
  20.7 5.5 %collective-permute-start.1 = (bf16[32,896]{1,0:T(8,128)(2,1)S(1)}, bf16[32,896]{1,0:T(8,128)(2,1)S(1)}, u32[]{:S(2)}, u32[]{:S(2)}) collective-permute-start(bf16[32,896]{1,0:T(8,128)(2,1)S(1)} %get-tuple-element.41), channel_id=1, source_target_pairs={{0,32},{16,48},{32,0},{48,16},{64,96},{80,112},{96,64},{112,80},{1... | collective-permute-start | bytes 172040 | tf_op jit(solution)/shard_map/ppermute | solution.py:489
  21.9 5.7 %collective-permute-start.2 = (bf16[32,896]{1,0:T(8,128)(2,1)S(1)}, bf16[32,896]{1,0:T(8,128)(2,1)S(1)}, u32[]{:S(2)}, u32[]{:S(2)}) collective-permute-start(bf16[32,896]{1,0:T(8,128)(2,1)S(1)} %get-tuple-element.42), channel_id=1, source_target_pairs={{0,48},{16,32},{32,16},{48,0},{64,112},{80,96},{96,80},{112,64},{1... | collective-permute-start | bytes 172040 | tf_op jit(solution)/shard_map/ppermute | solution.py:489
  22.5 6.2 %collective-permute-start.3 = (bf16[32,896]{1,0:T(8,128)(2,1)S(1)}, bf16[32,896]{1,0:T(8,128)(2,1)S(1)}, u32[]{:S(2)}, u32[]{:S(2)}) collective-permute-start(bf16[32,896]{1,0:T(8,128)(2,1)S(1)} %get-tuple-element.43), channel_id=1, source_target_pairs={{0,64},{16,80},{32,96},{48,112},{64,0},{80,16},{96,32},{112,48},{1... | collective-permute-start | bytes 172040 | tf_op jit(solution)/shard_map/ppermute | solution.py:489
  23.0 6.1 %collective-permute-start.4 = (bf16[32,896]{1,0:T(8,128)(2,1)S(1)}, bf16[32,896]{1,0:T(8,128)(2,1)S(1)}, u32[]{:S(2)}, u32[]{:S(2)}) collective-permute-start(bf16[32,896]{1,0:T(8,128)(2,1)S(1)} %get-tuple-element.44), channel_id=1, source_target_pairs={{0,80},{16,64},{32,112},{48,96},{64,16},{80,0},{96,48},{112,32},{1... | collective-permute-start | bytes 172040 | tf_op jit(solution)/shard_map/ppermute | solution.py:489
  25.7 6.0 %collective-permute-start.5 = (bf16[32,896]{1,0:T(8,128)(2,1)S(1)}, bf16[32,896]{1,0:T(8,128)(2,1)S(1)}, u32[]{:S(2)}, u32[]{:S(2)}) collective-permute-start(bf16[32,896]{1,0:T(8,128)(2,1)S(1)} %get-tuple-element.45), channel_id=1, source_target_pairs={{0,96},{16,112},{32,64},{48,80},{64,32},{80,48},{96,0},{112,16},{1... | collective-permute-start | bytes 172040 | tf_op jit(solution)/shard_map/ppermute | solution.py:489
  26.2 5.7 %collective-permute-start.6 = (bf16[32,896]{1,0:T(8,128)(2,1)S(1)}, bf16[32,896]{1,0:T(8,128)(2,1)S(1)}, u32[]{:S(2)}, u32[]{:S(2)}) collective-permute-start(bf16[32,896]{1,0:T(8,128)(2,1)S(1)} %get-tuple-element.46), channel_id=1, source_target_pairs={{0,112},{16,96},{32,80},{48,64},{64,48},{80,32},{96,16},{112,0},{1... | collective-permute-start | bytes 172040 | tf_op jit(solution)/shard_map/ppermute | solution.py:489
  27.6 6.8 %collective-permute-start.7 = (bf16[32,896]{1,0:T(8,128)(2,1)S(1)}, bf16[32,896]{1,0:T(8,128)(2,1)S(1)}, u32[]{:S(2)}, u32[]{:S(2)}) collective-permute-start(bf16[32,896]{1,0:T(8,128)(2,1)S(1)} %get-tuple-element.47), channel_id=1, source_target_pairs={{0,128},{16,144},{32,160},{48,176},{64,192},{80,208},{96,224},{112... | collective-permute-start | bytes 172040 | tf_op jit(solution)/shard_map/ppermute | solution.py:489
  28.8 8.0 %collective-permute-start.8 = (bf16[32,896]{1,0:T(8,128)(2,1)S(1)}, bf16[32,896]{1,0:T(8,128)(2,1)S(1)}, u32[]{:S(2)}, u32[]{:S(2)}) collective-permute-start(bf16[32,896]{1,0:T(8,128)(2,1)S(1)} %get-tuple-element.48), channel_id=1, source_target_pairs={{0,144},{16,128},{32,176},{48,160},{64,208},{80,192},{96,240},{112... | collective-permute-start | bytes 172040 | tf_op jit(solution)/shard_map/ppermute | solution.py:489
  29.2 9.1 %collective-permute-start.9 = (bf16[32,896]{1,0:T(8,128)(2,1)S(1)}, bf16[32,896]{1,0:T(8,128)(2,1)S(1)}, u32[]{:S(2)}, u32[]{:S(2)}) collective-permute-start(bf16[32,896]{1,0:T(8,128)(2,1)S(1)} %get-tuple-element.49), channel_id=1, source_target_pairs={{0,160},{16,176},{32,128},{48,144},{64,224},{80,240},{96,192},{112... | collective-permute-start | bytes 172040 | tf_op jit(solution)/shard_map/ppermute | solution.py:489
  31.7 7.1 %collective-permute-start.10 = (bf16[32,896]{1,0:T(8,128)(2,1)S(1)}, bf16[32,896]{1,0:T(8,128)(2,1)S(1)}, u32[]{:S(2)}, u32[]{:S(2)}) collective-permute-start(bf16[32,896]{1,0:T(8,128)(2,1)S(1)} %get-tuple-element.50), channel_id=1, source_target_pairs={{0,176},{16,160},{32,144},{48,128},{64,240},{80,224},{96,208},{112... | collective-permute-start | bytes 172040 | tf_op jit(solution)/shard_map/ppermute | solution.py:489
  32.0 7.1 %collective-permute-start.11 = (bf16[32,896]{1,0:T(8,128)(2,1)S(1)}, bf16[32,896]{1,0:T(8,128)(2,1)S(1)}, u32[]{:S(2)}, u32[]{:S(2)}) collective-permute-start(bf16[32,896]{1,0:T(8,128)(2,1)S(1)} %get-tuple-element.51), channel_id=1, source_target_pairs={{0,192},{16,208},{32,224},{48,240},{64,128},{80,144},{96,160},{112... | collective-permute-start | bytes 172040 | tf_op jit(solution)/shard_map/ppermute | solution.py:489
  34.3 6.5 %collective-permute-start.12 = (bf16[32,896]{1,0:T(8,128)(2,1)S(1)}, bf16[32,896]{1,0:T(8,128)(2,1)S(1)}, u32[]{:S(2)}, u32[]{:S(2)}) collective-permute-start(bf16[32,896]{1,0:T(8,128)(2,1)S(1)} %get-tuple-element.52), channel_id=1, source_target_pairs={{0,208},{16,192},{32,240},{48,224},{64,144},{80,128},{96,176},{112... | collective-permute-start | bytes 172040 | tf_op jit(solution)/shard_map/ppermute | solution.py:489
  36.8 6.0 %collective-permute-start.13 = (bf16[32,896]{1,0:T(8,128)(2,1)S(1)}, bf16[32,896]{1,0:T(8,128)(2,1)S(1)}, u32[]{:S(2)}, u32[]{:S(2)}) collective-permute-start(bf16[32,896]{1,0:T(8,128)(2,1)S(1)} %get-tuple-element.53), channel_id=1, source_target_pairs={{0,224},{16,240},{32,192},{48,208},{64,160},{80,176},{96,128},{112... | collective-permute-start | bytes 172040 | tf_op jit(solution)/shard_map/ppermute | solution.py:489
  38.3 5.5 %collective-permute-start.14 = (bf16[32,896]{1,0:T(8,128)(2,1)S(1)}, bf16[32,896]{1,0:T(8,128)(2,1)}, u32[]{:S(2)}, u32[]{:S(2)}) collective-permute-start(bf16[32,896]{1,0:T(8,128)(2,1)S(1)} %get-tuple-element.54), channel_id=1, source_target_pairs={{0,240},{16,224},{32,208},{48,192},{64,176},{80,160},{96,144},{112... | collective-permute-start | bytes 172040 | tf_op jit(solution)/shard_map/ppermute | solution.py:489
  170.8 39.1 %all-to-all-start.4 = ((bf16[16,64,768]{2,1,0:T(8,128)(2,1)}), bf16[16,64,768]{2,1,0:T(8,128)(2,1)S(1)}, u32[]{:S(2)}, u32[]{:S(2)}) async-start(bf16[16,64,768]{2,1,0:T(8,128)(2,1)} %get-tuple-element.72), calls=%async_computation.4 | async-start | bytes 3145728 | tf_op jit(solution)/shard_map/all_to_all | solution.py:480
  176.4 9.3 %collective-permute-start.15 = (bf16[80,256]{1,0:T(8,128)(2,1)S(1)}, bf16[80,256]{1,0:T(8,128)(2,1)S(1)}, u32[]{:S(2)}, u32[]{:S(2)}) collective-permute-start(bf16[80,256]{1,0:T(8,128)(2,1)S(1)} %copy-done.20), channel_id=1, source_target_pairs={{0,0},{1,16},{2,32},{3,48},{4,64},{5,80},{6,96},{7,112},{8,128},{9... | collective-permute-start | bytes 122888 | tf_op jit(solution)/shard_map/ppermute | solution.py:485
  185.7 6.5 %collective-permute-start.18 = (bf16[80,256]{1,0:T(8,128)(2,1)S(1)}, bf16[80,256]{1,0:T(8,128)(2,1)S(1)}, u32[]{:S(2)}, u32[]{:S(2)}) collective-permute-start(bf16[80,256]{1,0:T(8,128)(2,1)S(1)} %collective-permute-done.15), channel_id=1, source_target_pairs={{0,12},{1,13},{2,14},{3,15},{4,8},{5,9},{6,10},{7,11},{8,4},{9,5},... | collective-permute-start | bytes 122888 | tf_op jit(solution)/shard_map/ppermute | solution.py:489
  189.0 8.4 %collective-permute-start.17 = (bf16[80,256]{1,0:T(8,128)(2,1)S(1)}, bf16[80,256]{1,0:T(8,128)(2,1)S(1)}, u32[]{:S(2)}, u32[]{:S(2)}) collective-permute-start(bf16[80,256]{1,0:T(8,128)(2,1)S(1)} %collective-permute-done.15), channel_id=1, source_target_pairs={{0,8},{1,9},{2,10},{3,11},{4,12},{5,13},{6,14},{7,15},{8,0},{9,1},... | collective-permute-start | bytes 122888 | tf_op jit(solution)/shard_map/ppermute | solution.py:489
  189.6 7.9 %collective-permute-start.16 = (bf16[80,256]{1,0:T(8,128)(2,1)S(1)}, bf16[80,256]{1,0:T(8,128)(2,1)S(1)}, u32[]{:S(2)}, u32[]{:S(2)}) collective-permute-start(bf16[80,256]{1,0:T(8,128)(2,1)S(1)} %collective-permute-done.15), channel_id=1, source_target_pairs={{0,4},{1,5},{2,6},{3,7},{4,0},{5,1},{6,2},{7,3},{8,12},{9,13},{10,... | collective-permute-start | bytes 122888 | tf_op jit(solution)/shard_map/ppermute | solution.py:489
  197.6 13.9 %collective-permute-start.21 = (bf16[272,256]{1,0:T(8,128)(2,1)S(1)}, bf16[272,256]{1,0:T(8,128)(2,1)S(1)}, u32[]{:S(2)}, u32[]{:S(2)}) collective-permute-start(bf16[272,256]{1,0:T(8,128)(2,1)S(1)} %concatenate.3.r0), channel_id=1, source_target_pairs={{0,3},{1,2},{2,1},{3,0},{4,7},{5,6},{6,5},{7,4},{8,11},{9,10},{10,... | collective-permute-start | bytes 417800 | tf_op jit(solution)/shard_map/ppermute | solution.py:489
  199.7 14.8 %collective-permute-start.20 = (bf16[272,256]{1,0:T(8,128)(2,1)S(1)}, bf16[272,256]{1,0:T(8,128)(2,1)S(1)}, u32[]{:S(2)}, u32[]{:S(2)}) collective-permute-start(bf16[272,256]{1,0:T(8,128)(2,1)S(1)} %concatenate.3.r0), channel_id=1, source_target_pairs={{0,2},{1,3},{2,0},{3,1},{4,6},{5,7},{6,4},{7,5},{8,10},{9,11},{10,... | collective-permute-start | bytes 417800 | tf_op jit(solution)/shard_map/ppermute | solution.py:489
  209.9 6.6 %collective-permute-start.19 = (bf16[272,256]{1,0:T(8,128)(2,1)S(1)}, bf16[272,256]{1,0:T(8,128)(2,1)S(1)}, u32[]{:S(2)}, u32[]{:S(2)}) collective-permute-start(bf16[272,256]{1,0:T(8,128)(2,1)S(1)} %concatenate.3.r0), channel_id=1, source_target_pairs={{0,1},{1,0},{2,3},{3,2},{4,5},{5,4},{6,7},{7,6},{8,9},{9,8},{10,11... | collective-permute-start | bytes 417800 | tf_op jit(solution)/shard_map/ppermute | solution.py:489
  (21 other events, 560.8 us)
